TPU v7x, 128 devices: a whole 4x4x4 slice. The times are simulated.
128 devices in a mesh: dp: 16 (over z_hi, y, core), ctx: 8 (over z_lo, x).
Axes of the slice: x: 4, y: 4, z: 4 (z_hi: 2, z_lo: 2; z = z_hi * 2 + z_lo), core: 2. Of those that a mesh axis runs over, the one named last changes fastest.
Arguments:
- token_ids: int32 [16, 1024], P('dp', 'ctx'), may hold values from 0 to 511
- bucket_of_slot: int32 [32], replicated, may hold values from 0 to 31, each once
- embed_tiles: bfloat16 [32, 512, 128], P('dp'), may hold values from -6 to 6
- norm_gain: float32 [4096], replicated, may hold values from 0.1 to 1.9
- in_tiles: bfloat16 [32, 128, 3, 4096], P('dp', None, None, 'ctx'), may hold values from -0.09375 to 0.09375
- short_taps: float32 [3, 3, 4096], P(None, None, 'ctx'), may hold values from -3 to 3
- decay_rate: float32 [16, 256], P(None, 'ctx'), may hold values from 0.002 to 0.05
- residue: float32 [16, 256], P(None, 'ctx'), may hold values from -0.3 to 0.3
- skip_gain: float32 [4096], P('ctx'), may hold values from -4 to 4
- out_tiles: bfloat16 [32, 128, 4096], P('dp', None, 'ctx'), may hold values from -0.09375 to 0.09375
Outputs:
- hidden_out: bfloat16 [16, 1024, 4096], P('dp', 'ctx')
Inputs may be any that keep to these rules, and one draw needn't show every extreme that they name: `bucket_of_slot`: each bucket stands in exactly one slot; slot s is kept by dp index s // 2.
All inputs are finite; a program needn't handle non-finite values.
Results may differ from a plain program's by a relative error of at most 0.02.
Values may be sent and summed in bfloat16 or wider, within the bound.
No kernel may reach another device: no remote copies, remote signals or barrier semaphores. Data moves between devices by JAX's collectives and lax.ppermute only.
A program may use at most 192 MiB of HBM per device.

v0:
```python
import jax
import jax.numpy as jnp
from jax import lax
from jax.sharding import PartitionSpec as P

GSIZE = 16


def bucket_order(bucket_of_slot):
    slot_count = bucket_of_slot.shape[0]
    slot_index = jnp.arange(slot_count, dtype=jnp.int32)
    hits = (bucket_of_slot[:, None] == slot_index[None, :]).astype(jnp.int32)
    return jnp.sum(slot_index[:, None] * hits, axis=0)


def long_filter(product, decay_rate, residue):
    seq_len, chan_count = product.shape
    group_count = chan_count // GSIZE
    block_len = min(256, seq_len)
    block_count = seq_len // block_len
    offsets = jnp.arange(block_len, dtype=jnp.float32)
    highest = lax.Precision.HIGHEST
    block_taps = jnp.einsum(
        "mg,mgt->tg",
        residue,
        jnp.exp(-decay_rate[:, :, None] * offsets[None, None, :]),
        precision=highest,
    )
    row_index = jnp.arange(block_len, dtype=jnp.int32)
    lag_index = row_index[:, None] - row_index[None, :]
    causal = (lag_index >= 0).astype(jnp.float32)
    toeplitz = block_taps[jnp.maximum(lag_index, 0)] * causal[:, :, None]
    toeplitz = toeplitz.astype(jnp.bfloat16)
    blocked = product.reshape(block_count, block_len, group_count, GSIZE)
    inner = jnp.einsum("tsg,nsgj->ntgj", toeplitz, blocked, preferred_element_type=jnp.float32)
    end_decay = jnp.exp(
        -decay_rate[:, None, :] * (block_len - 1.0 - offsets)[None, :, None]
    ).astype(jnp.bfloat16)
    local_end = jnp.einsum("msg,nsgj->nmgj", end_decay, blocked, preferred_element_type=jnp.float32)
    block_pos = jnp.arange(block_count, dtype=jnp.float32)
    distance = block_pos[:, None] - block_pos[None, :] - 1.0
    earlier = (distance >= 0).astype(jnp.float32)
    carry_decay = (
        jnp.exp(-decay_rate[:, :, None, None] * block_len * jnp.maximum(distance, 0.0)[None, None])
        * earlier[None, None]
    )
    starts = jnp.einsum("mgni,imgj->nmgj", carry_decay, local_end, precision=highest)
    leading = residue[:, None, :] * jnp.exp(
        -decay_rate[:, None, :] * (offsets + 1.0)[None, :, None]
    )
    outer = jnp.einsum("mtg,nmgj->ntgj", leading, starts, precision=highest)
    return (inner + outer).reshape(seq_len, chan_count)


def body(
    token_ids,
    bucket_of_slot,
    embed_tiles,
    norm_gain,
    in_tiles,
    short_taps,
    decay_rate,
    residue,
    skip_gain,
    out_tiles,
):
    slot_of_bucket = bucket_order(bucket_of_slot)
    slot_count = bucket_of_slot.shape[0]
    local_ids = token_ids[0]
    tok_count = local_ids.shape[0]
    vocab_size = embed_tiles.shape[1]
    bucket_width = embed_tiles.shape[2]
    model_width = slot_count * bucket_width
    vocab_index = jnp.arange(vocab_size, dtype=jnp.int32)
    width_index = jnp.arange(bucket_width, dtype=jnp.int32)
    one_hot = (local_ids[:, None] == vocab_index[None, :]).astype(jnp.bfloat16)
    piece = lax.all_gather(embed_tiles, "dp", axis=0, tiled=True)
    looked = jnp.einsum("tv,svw->stw", one_hot, piece, preferred_element_type=jnp.float32).astype(
        jnp.bfloat16
    )

    def one_slot(slot, current):
        bucket = bucket_of_slot[slot]
        columns = lax.dynamic_index_in_dim(looked, slot, 0, keepdims=False)
        return lax.dynamic_update_slice_in_dim(current, columns, bucket * bucket_width, 1)

    embedded = lax.fori_loop(
        0, piece.shape[0], one_slot, jnp.zeros((tok_count, model_width), jnp.bfloat16)
    )
    embed_f32 = embedded.astype(jnp.float32)
    scale = lax.rsqrt(jnp.mean(embed_f32 * embed_f32, axis=-1, keepdims=True) + 1e-06)
    normed = (embed_f32 * scale * norm_gain).astype(jnp.bfloat16)
    all_rows = lax.all_gather(normed, "ctx", axis=0, tiled=True)
    seq_len = all_rows.shape[0]
    chan_count = in_tiles.shape[3]
    piece = lax.all_gather(in_tiles, "dp", axis=0, tiled=True)
    count = piece.shape[0]
    column_index = (bucket_of_slot[:, None] * bucket_width + width_index[None, :]).reshape(-1)
    columns = jnp.take(all_rows, column_index, axis=1)
    weight_rows = piece.reshape(count * bucket_width, 3 * chan_count)
    projected = jnp.dot(columns, weight_rows, preferred_element_type=jnp.float32)
    projected = projected.reshape(seq_len, 3, chan_count)
    padded = jnp.pad(projected, ((2, 0), (0, 0), (0, 0)))
    featured = (
        short_taps[0] * projected
        + short_taps[1] * padded[1 : seq_len + 1]
        + short_taps[2] * padded[0:seq_len]
    )
    query_part = featured[:, 0]
    product = (featured[:, 1] * featured[:, 2]).astype(jnp.bfloat16)
    mixed = long_filter(product, decay_rate, residue) + skip_gain * product.astype(jnp.float32)
    gated = (query_part * mixed).astype(jnp.bfloat16)
    gathered = lax.all_gather(out_tiles, "dp", axis=0, tiled=True)
    w_out = jnp.take(gathered, slot_of_bucket, axis=0).reshape(model_width, chan_count)
    returned = lax.psum_scatter(
        lax.dot_general(
            gated, w_out, (((1,), (1,)), ((), ())), preferred_element_type=jnp.float32
        ).astype(jnp.bfloat16),
        "ctx",
        scatter_dimension=0,
        tiled=True,
    ).astype(jnp.float32)
    return (embed_f32 + returned).astype(jnp.bfloat16)[None]


def solution(mesh):
    in_specs = (
        P("dp", "ctx"),
        P(),
        P("dp", None, None),
        P(),
        P("dp", None, None, "ctx"),
        P(None, None, "ctx"),
        P(None, "ctx"),
        P(None, "ctx"),
        P("ctx"),
        P("dp", None, "ctx"),
    )
    out_specs = P("dp", "ctx", None)
    return jax.shard_map(body, mesh=mesh, in_specs=in_specs, out_specs=out_specs, check_vma=False)
```

profile of v0, /device:TPU:1, one launch (start us, length us, event | category | flops | bytes accessed | tf_op | source)
XLA Modules:
  0.0 599.1 jit_solution(5968249426643129062)
XLA Ops:
  6.5 0.7 all-gather.5.cloned.1.call-update
  7.3 0.7 all-gather.11.cloned.1.call-update
  8.1 61.5 %all-gather.5.cloned.1.call-done = bf16[32,512,128]{2,1,0:T(8,128)(2,1)} async-done(((bf16[2,512,128]{2,1,0:T(8,128)(2,1)}), bf16[32,512,128]{2,1,0:T(8,128)(2,1)}) %all-gather.5.cloned.1.call-update) | async-done | bytes 4194320 | tf_op jit(solution)/shard_map/all_gather | solution.py:77
  69.6 3.0 fusion.17
  72.7 44.9 %while.13 = (s32[]{:T(128)}, bf16[128,4096]{1,0:T(8,128)(2,1)S(1)}, bf16[32,128,128]{2,1,0:T(8,128)(2,1)S(1)}, s32[32]{0:T(128)S(1)}, s32[]{:T(128)}, /*index=5*/s32[1]{0:T(128)}, s32[]{:T(128)}, s32[]{:T(128)}) while((s32[]{:T(128)}, bf16[128,4096]{1,0:T(8,128)(2,1)S(1)}, bf16[32,128,128]{2,1,0:T(8,128)(2,1)S(1)}, s32[32]{0:T(128)S(1)}, ...), condition=%wide.region_1.2_spmd, body=%wide.region_0.0_spmd.sunk | while | flops 6 | bytes 65687 | solution.py:87
  72.7 0.7 dynamic_slice.19
  74.1 0.7 dynamic_slice.19
  75.5 0.7 dynamic_slice.19
  76.9 0.7 dynamic_slice.19
  78.3 0.7 dynamic_slice.19
  79.7 0.7 dynamic_slice.19
  81.1 0.7 dynamic_slice.19
  82.5 0.7 dynamic_slice.19
  83.9 0.7 dynamic_slice.19
  85.3 0.7 dynamic_slice.19
  86.7 0.7 dynamic_slice.19
  88.1 0.7 dynamic_slice.19
  89.5 0.7 dynamic_slice.19
  90.9 0.7 dynamic_slice.19
  92.3 0.7 dynamic_slice.19
  93.7 0.7 dynamic_slice.19
  95.1 0.7 dynamic_slice.19
  96.5 0.7 dynamic_slice.19
  97.9 0.7 dynamic_slice.19
  99.3 0.7 dynamic_slice.19
  100.7 0.7 dynamic_slice.19
  102.1 0.7 dynamic_slice.19
  103.5 0.7 dynamic_slice.19
  104.9 0.7 dynamic_slice.19
  106.3 0.7 dynamic_slice.19
  107.7 0.7 dynamic_slice.19
  109.1 0.7 dynamic_slice.19
  110.5 0.7 dynamic_slice.19
  111.9 0.7 dynamic_slice.19
  113.3 0.7 dynamic_slice.19
  114.7 0.7 dynamic_slice.19
  116.1 0.7 dynamic_slice.19
  117.9 1.3 fusion.11
  119.8 0.6 broadcast_multiply_fusion
  120.4 0.7 copy.47
  121.1 0.7 copy.50
  122.3 217.1 %gather_fusion.1 = f32[65536,32]{1,0:T(8,128)} fusion(f32[256,32]{1,0:T(8,128)S(1)} %bitcast.88, s32[65536]{0:T(1024)S(1)} %broadcast_clamp_fusion), kind=kCustom, calls=%fused_computation.1 | custom fusion | bytes 17039360 | tf_op jit(solution)/shard_map/gather | solution.py:32
  339.4 22.2 %copy.45 = f32[256,256,32]{1,0,2:T(8,128)} copy(f32[256,256,32]{2,1,0:T(8,128)} %bitcast.89) | data formatting | bytes 16777216 | tf_op jit(solution)/shard_map/gather | solution.py:32
  362.1 5.0 gather_fusion.2
  367.1 4.7 broadcast_select_fusion
  371.7 12.0 %copy.41 = bf16[1024,4096]{0,1:T(8,128)(2,1)} copy(bf16[1024,4096]{1,0:T(8,128)(2,1)} %all-gather.7.cloned.1.call-done) | data formatting | bytes 16777216 | tf_op jit(solution)/shard_map/all_gather | solution.py:93
  383.7 25.4 %gather_fusion = bf16[4096,1024]{1,0:T(8,128)(2,1)} fusion(bf16[1024,4096]{0,1:T(8,128)(2,1)} %copy.41, s32[4096]{0:T(1024)S(1)} %broadcast_clamp_fusion.1), kind=kCustom, calls=%fused_computation | custom fusion | bytes 16793600 | tf_op jit(solution)/shard_map/jit(_take)/gather | solution.py:99
  409.1 17.2 %copy.42 = bf16[32,128,3,512]{1,0,3,2:T(8,128)(2,1)} copy(bf16[32,128,3,512]{3,1,2,0:T(8,128)(2,1)} %all-gather.9.cloned.1.call-done) | data formatting | bytes 25165824 | tf_op jit(solution)/shard_map/all_gather | solution.py:96
  426.4 13.3 %copy.75 = bf16[192,8,32,128]{3,1,2,0:T(8,128)(2,1)} copy(bf16[192,8,32,128]{3,2,1,0:T(8,128)(2,1)} %bitcast.90) | data formatting | bytes 25165824
  439.7 21.3 %fusion = f32[1024,3,512]{2,0,1:T(8,128)S(1)} fusion(bf16[3,512,4096]{2,1,0:T(8,128)(2,1)} %bitcast.91, bf16[4096,1024]{1,0:T(8,128)(2,1)} %gather_fusion, pred[4096]{0:T(1024)(128)(4,1)S(1)} %compare_and_fusion), kind=kOutput, calls=%fused_computation.5 | convolution fusion | flops 12889096192 | bytes 27267072 | tf_op jit(solution)/shard_map/dot_general | solution.py:101
  460.9 1.9 multiply_add_fusion
  462.8 2.7 copy-done
  466.5 1.0 convert_element_type.68
  467.5 1.5 convolution_bitcast_fusion.1
  469.0 2.3 copy.49
  471.3 3.8 convolution_bitcast_fusion
  475.1 2.4 fusion.21
  477.5 4.8 add_bitcast_fusion
  482.3 1.8 copy.52
  484.1 2.1 reshape.198
  486.2 2.2 copy.53
  488.4 10.6 %convolution_convert_fusion = bf16[1024,4096]{1,0:T(8,128)(2,1)} fusion(bf16[4096,512]{1,0:T(8,128)(2,1)} %bitcast.92, f32[1024,1,512]{2,0,1:T(8,128)S(1)} %copy.53, bf16[1024,1,512]{2,0,1:T(8,128)(2,1)S(1)} %fusion.13, f32[1024,3,512]{2,0,1:T(8,128)} %copy-done, f32[512]{0:T(512)S(1)} %copy-done.10), kind=kOutput, calls=%fused_computation.10 | convolution fusion | flops 4301783040 | bytes 17827840 | tf_op jit(solution)/shard_map/dot_general | solution.py:116
  499.0 91.1 %reduce-scatter.2.cloned.1.call-done = bf16[128,4096]{1,0:T(8,128)(2,1)} async-done(((bf16[1024,4096]{1,0:T(8,128)(2,1)}), bf16[128,4096]{1,0:T(8,128)(2,1)}) %reduce-scatter.2.cloned.1.call-update) | async-done | bytes 1048592 | tf_op jit(solution)/shard_map/reduce_scatter | solution.py:115
  590.1 2.4 fusion.20
  (91 shorter events, 3.6 us)
Async XLA Ops:
  6.5 66.1 %copy-start.11 = (s32[32]{0:T(128)S(1)}, s32[32]{0:T(128)}, u32[]{:S(2)}) copy-start(s32[32]{0:T(128)} %param.13) | copy-start | bytes 388
  6.5 111.3 %copy-start.7 = (f32[4096]{0:T(1024)S(1)}, f32[4096]{0:T(1024)}, u32[]{:S(2)}) copy-start(f32[4096]{0:T(1024)} %param.15) | copy-start | bytes 49156
  6.5 63.0 %all-gather.5.cloned.1.call-start = ((), (), s32[]{:S(2)}) async-start(), calls=%async_computation.1 | async-start | bytes 4456448 | tf_op jit(solution)/shard_map/all_gather | solution.py:77
  7.3 354.8 %all-gather.11.cloned.1.call-start = ((), (), s32[]{:S(2)}) async-start(), calls=%async_computation.4 | async-start | bytes 4456448 | tf_op jit(solution)/shard_map/all_gather | solution.py:113
  8.0 363.7 %all-gather.7.cloned.1.call-start = ((), (), s32[]{:S(2)}) async-start(), calls=%async_computation.2 | async-start | bytes 9437184 | tf_op jit(solution)/shard_map/all_gather | solution.py:93
  72.5 47.3 %copy-start.8 = (f32[16,32]{1,0:T(8,128)S(1)}, f32[16,32]{1,0:T(8,128)}, u32[]{:S(2)}) copy-start(f32[16,32]{1,0:T(8,128)} %param.18) | copy-start | bytes 6148
  72.6 48.5 %copy-start.9 = (f32[16,32]{1,0:T(8,128)S(1)}, f32[16,32]{1,0:T(8,128)}, u32[]{:S(2)}) copy-start(f32[16,32]{1,0:T(8,128)} %param.19) | copy-start | bytes 6148
  117.5 4.2 copy-start.1
  119.2 289.9 %all-gather.9.cloned.1.call-start = ((), (), s32[]{:S(2)}) async-start(), calls=%async_computation.3 | async-start | bytes 13369344 | tf_op jit(solution)/shard_map/all_gather | solution.py:96
  119.8 470.4 %reduce-scatter.2.cloned.1.call-start = ((), (), s32[]{:S(2)}) async-start(), calls=%async_computation.5 | async-start | bytes 9437184 | tf_op jit(solution)/shard_map/reduce_scatter | solution.py:115
  339.4 22.6 %copy-start.6 = (f32[3,3,512]{2,1,0:T(4,128)S(1)}, f32[3,3,512]{2,1,0:T(4,128)}, u32[]{:S(2)}) copy-start(f32[3,3,512]{2,1,0:T(4,128)} %param.17) | copy-start | bytes 55300
  462.8 2.7 copy-start
  465.5 1.9 copy-start.3
  465.9 5.4 copy-start.5
  466.4 8.6 %copy-start.4 = (f32[16,32]{0,1:T(8,128)S(1)}, f32[16,32]{0,1:T(8,128)}, u32[]{:S(2)}) copy-start(f32[16,32]{0,1:T(8,128)} %copy.50) | copy-start | bytes 6148
  484.1 4.3 copy-start.10
  499.0 91.1 %copy-start.2 = (bf16[128,4096]{1,0:T(8,128)(2,1)S(1)}, bf16[128,4096]{1,0:T(8,128)(2,1)}, u32[]{:S(2)}) copy-start(bf16[128,4096]{1,0:T(8,128)(2,1)} %copy-done.1) | copy-start | bytes 3145732
Sparse Core Ops, SparseCore 0:
  9.8 59.7 all-gather.4
  72.0 54.7 all-gather.10
  128.5 90.1 all-gather.6
  220.9 90.1 all-gather.8
  499.1 90.9 reduce-scatter.1
where the time goes:
time: 601 us; the launch traced here: 599 us
  local copies, waits for them, and re-layouts  349 us (58%)
  waiting for transfers between devices  155 us (26%)
  matrix products  47.3 us (8%)
  loops' own time  22.9 us (4%)
  between operations  13.5 us (2%)
  other arithmetic  12.1 us (2%)
    gather x2, local copies, waits for them, and re-layouts, long_filter(): toeplitz = block_taps[jnp.maximum(lag_index, 0)] * causal[:, :, None]  239 us
    reduce_scatter x1, waiting for transfers between devices, body(): lax.psum_scatter(lax.dot_general(gated, w_out, (((1,), (1,)), ((), ())),...  91.1 us
    all_gather x1, waiting for transfers between devices, body(): piece = lax.all_gather(embed_tiles, 'dp', axis=0, tiled=True)  61.5 us
    gather x1, local copies, waits for them, and re-layouts, body(): columns = jnp.take(all_rows, column_index, axis=1)  25.4 us
    another operation x1, loops' own time, body(): lax.fori_loop(0, piece.shape[0], one_slot, jnp.zeros((tok_count, model_wi...  22.9 us
    dot_general x1, matrix products, body(): jnp.dot(columns, weight_rows, preferred_element_type=jnp.float32)  21.3 us
    dynamic_slice x32, local copies, waits for them, and re-layouts, one_slot(): bucket = bucket_of_slot[slot]  21.2 us
    all_gather x1, local copies, waits for them, and re-layouts, body(): piece = lax.all_gather(in_tiles, 'dp', axis=0, tiled=True)  17.2 us
  transfers between devices with their start and end apart: 5, of which 2 were waited for; matrix products, arithmetic and copies ran while one was open for 53% of the time, Pallas kernels for 0%

commit v1 on v0

v1 whole, which is shorter than its diff:
```python
import jax
import jax.numpy as jnp
from jax import lax
from jax.experimental import pallas as pl
from jax.experimental.pallas import tpu as pltpu
from jax.sharding import Mesh
from jax.sharding import PartitionSpec as P

F32 = jnp.float32
BF16 = jnp.bfloat16
D = 4096
SEQ = 1024
EPS = 1e-06
OFFSETS = (0, 3, 1, 2)
ZAX = ("zh", "zl")
DP = ("zh", "y", "co")
CTX = ("zl", "x")


def shift(value, axis, step):
    return lax.ppermute(value, axis, [(i, (i + step) % 4) for i in range(4)])


def flip(value, axes, bits, size):
    return lax.ppermute(value, axes, [(i, i ^ bits) for i in range(size)])


def ring(value, axis):
    half = value.shape[0] // 2
    below = shift(value, axis, 1)
    above = shift(value, axis, -1)
    first = shift(below[:half], axis, 1)
    second = shift(above[half:], axis, -1)
    return value, below, above, first, second


def gather_cube(part, order):
    for axis in order[:2]:
        part = jnp.concatenate(ring(part, axis))
    return ring(part, order[2])


def mixer_kernel(recv, taps, skip, decay, residue, out, toep, prod, query):
    table = recv[0, 0:96, :].astype(F32)
    extra = recv[0, 96:112, :].astype(F32)
    square = extra[8:9] + extra[9:10]
    for i in range(1, 8):
        table = table + recv[i, 0:96, :].astype(F32)
        extra = recv[i, 96:112, :].astype(F32)
        square = square + extra[8:9] + extra[9:10]
    table = (table * lax.rsqrt(square / D + EPS)).astype(BF16)

    for g in range(2):
        time = lax.broadcasted_iota(jnp.int32, (16, SEQ), 1).astype(F32)
        terms = jnp.exp(-decay[:, g : g + 1] * time) * residue[:, g : g + 1]
        filt = jnp.sum(terms, axis=0, keepdims=True).astype(BF16).astype(F32)
        filt = jnp.concatenate([filt, jnp.zeros((1, 128), F32)], axis=1)
        lagged = pltpu.roll(
            jnp.broadcast_to(filt, (128, SEQ + 128)), 0, 1, stride=1, stride_axis=0
        ).astype(BF16)
        for k in range(4):
            toep[g, k, 0:128, :] = lagged[:, 256 * k : 256 * k + 256]
            if k == 0:
                toep[g, k, 128:256, 0:128] = jnp.zeros((128, 128), BF16)
                toep[g, k, 128:256, 128:256] = lagged[:, 0:128]
            else:
                toep[g, k, 128:256, :] = lagged[:, 256 * k - 128 : 256 * k + 128]

    vocab = lax.broadcasted_iota(jnp.int32, (512, 512), 0).astype(F32)
    lane = lax.broadcasted_iota(jnp.int32, (96, SEQ), 1)

    def one_pair(i, carry):
        extra = recv[i, 96:112, :].astype(F32)
        for j in range(2):
            parts = []
            for a in range(2):
                r = 2 * j + a
                ids = extra[r : r + 1] * 256.0 + extra[4 + r : 5 + r]
                hot = jnp.where(vocab == ids, 1.0, 0.0).astype(BF16)
                parts.append(jnp.dot(table, hot, preferred_element_type=F32))
            z0 = jnp.concatenate(parts, axis=1)
            z1 = jnp.where(lane >= 1, pltpu.roll(z0, 1, 1), 0.0)
            z2 = jnp.where(lane >= 2, pltpu.roll(z0, 2, 1), 0.0)
            f = taps[0] * z0 + taps[1] * z1 + taps[2] * z2
            u = (f[32:64] * f[64:96]).astype(BF16)
            rows = pl.ds(pl.multiple_of((2 * i + j) * 16, 16), 16)
            for g in range(2):
                for b in range(4):
                    cols = slice(256 * b, 256 * b + 256)
                    prod[g, b, rows, :] = u[16 * g : 16 * g + 16, cols]
                    query[g, b, rows, :] = f[16 * g : 16 * g + 16, cols]
        return carry

    lax.fori_loop(0, 8, one_pair, 0)

    for g in range(2):
        for b in range(4):
            mixed = skip[g] * prod[g, b].astype(F32)
            for a in range(b + 1):
                mixed = mixed + jnp.dot(prod[g, a], toep[g, b - a], preferred_element_type=F32)
            gated = (query[g, b] * mixed).astype(BF16)
            for n in range(16):
                for h in range(2):
                    out[
                        2 * b + h,
                        n // 2,
                        16 * g : 16 * g + 16,
                        128 * (n % 2) : 128 * (n % 2) + 128,
                    ] = gated[16 * n : 16 * n + 16, 128 * h : 128 * h + 128]


def mixer(recv, taps, skip, decay, residue):
    vmem = pl.BlockSpec(memory_space=pltpu.VMEM)
    return pl.pallas_call(
        mixer_kernel,
        out_shape=jax.ShapeDtypeStruct((8, 8, 32, 256), BF16),
        in_specs=[vmem] * 5,
        out_specs=vmem,
        scratch_shapes=[
            pltpu.VMEM((2, 4, 256, 256), BF16),
            pltpu.VMEM((2, 4, 256, 256), BF16),
            pltpu.VMEM((2, 4, 256, 256), F32),
        ],
        compiler_params=pltpu.CompilerParams(vmem_limit_bytes=32 << 20),
        cost_estimate=pl.CostEstimate(
            flops=2 * 16 * 96 * 512 * 1024, bytes_accessed=4 << 20, transcendentals=0
        ),
        name="mixer",
    )(recv, taps, skip, decay, residue)


def project_kernel(where, bucket, gated, ids, *refs):
    pieces = [refs[5 * p : 5 * p + 5] for p in range(3)]
    own, other, total, embed = refs[15:]
    x, y, z, co = where[0], where[1], where[2], where[3]
    total[...] = jnp.zeros_like(total)

    def block(p, rel):
        near, mid, far = rel
        at = mid * 4 + near
        if far < 3:
            return pieces[p][far], 4 * at
        return (pieces[p][3], 4 * at) if at < 8 else (pieces[p][4], 4 * (at - 8))

    for yr in range(4):
        for zr in range(4):
            y_of = lax.rem(y + OFFSETS[yr], 4)
            z_of = lax.rem(z + OFFSETS[zr], 4)
            owner = (z_of // 2) * 4 + y_of
            left, right = [], []
            for xr in range(4):
                chunk = lax.rem(z_of, 2) * 4 + lax.rem(x + OFFSETS[xr], 4)
                rel = ((xr, yr, zr), (yr, zr, xr), (zr, xr, yr))
                rows = []
                for p in range(3):
                    ref, at = block(p, rel[p])
                    if p < 2:
                        rows.append(ref[at : at + 4].reshape(192, 256))
                    else:
                        rows.append(ref[at : at + 4, 0:32].reshape(128, 256))
                        for s in range(4):
                            for h in range(2):
                                at_row = pl.multiple_of(chunk * 32 + 16 * h, 16)
                                embed[owner, pl.ds(at_row, 16), 128 * s : 128 * s + 128] = ref[
                                    at + s, 32:48, 128 * h : 128 * h + 128
                                ]
                left.append(jnp.concatenate(rows, axis=0))
                right.append(gated[chunk])
            total[owner] += jnp.dot(
                jnp.concatenate(left, axis=1),
                jnp.concatenate(right, axis=0),
                preferred_element_type=F32,
            )

    lane = lax.broadcasted_iota(jnp.int32, (256, 256), 1)
    vocab = lane + (lane // 32) * 32 + co * 32
    hot = jnp.where(ids[...] == vocab, 1.0, 0.0).astype(BF16)
    for owner in range(8):
        looked = jnp.dot(hot, embed[owner], preferred_element_type=F32)
        for s in range(4):
            rows = jnp.concatenate(
                [
                    total[owner, 48 * s : 48 * s + 48],
                    total[owner, 192 + 48 * s : 240 + 48 * s],
                    total[owner, 384 + 32 * s : 416 + 32 * s],
                ],
                axis=0,
            )
            both = rows.T + looked[:, 128 * s : 128 * s + 128]
            core = co if s < 2 else 1 - co
            slot = 4 * owner + 2 * core + s % 2
            cols = pl.ds(pl.multiple_of(bucket[slot] * 128, 128), 128)
            own[:, cols] = jnp.where(co == 0, both[0:128], both[128:256])
            other[:, cols] = jnp.where(co == 0, both[128:256], both[0:128]).astype(BF16)


def project(where, bucket, gated, ids, pieces):
    vmem = pl.BlockSpec(memory_space=pltpu.VMEM)
    smem = pl.BlockSpec(memory_space=pltpu.SMEM)
    return pl.pallas_call(
        project_kernel,
        out_shape=(
            jax.ShapeDtypeStruct((128, D), F32),
            jax.ShapeDtypeStruct((128, D), BF16),
        ),
        in_specs=[smem, smem] + [vmem] * (2 + len(pieces)),
        out_specs=(vmem, vmem),
        scratch_shapes=[
            pltpu.VMEM((8, 512, 256), F32),
            pltpu.VMEM((8, 256, 512), BF16),
        ],
        compiler_params=pltpu.CompilerParams(vmem_limit_bytes=48 << 20),
        cost_estimate=pl.CostEstimate(
            flops=2 * 256 * 4096 * 2048, bytes_accessed=24 << 20, transcendentals=0
        ),
        name="project",
    )(where, bucket, gated, ids, *pieces)


def body(
    token_ids,
    bucket_of_slot,
    embed_tiles,
    norm_gain,
    in_tiles,
    short_taps,
    decay_rate,
    residue,
    skip_gain,
    out_tiles,
):
    zh, y, co, zl, x = (lax.axis_index(a) for a in ("zh", "y", "co", "zl", "x"))
    zy = zh * 4 + y
    c = zl * 4 + x
    d = zy * 2 + co

    def tile_for(core):
        rows = lax.dynamic_slice_in_dim(out_tiles, core * 256, 256, axis=2)
        words = lax.dynamic_slice_in_dim(embed_tiles, (c * 2 + core) * 32, 32, axis=1)
        words = words.reshape(2, 2, 16, 128).transpose(0, 2, 1, 3).reshape(2, 16, 256)
        return jnp.concatenate([rows, words], axis=1)

    tiles = jnp.concatenate([tile_for(co), flip(tile_for(1 - co), "co", 1, 2)])
    pieces = []
    for p, order in enumerate((("x", "y", ZAX), ("y", ZAX, "x"), (ZAX, "x", "y"))):
        pieces += gather_cube(tiles[:, 48 * p : 48 * p + 48], order)

    core_index = lax.broadcasted_iota(jnp.int32, (2, 8, 128), 0)
    ctx_index = lax.broadcasted_iota(jnp.int32, (2, 8, 128), 1)
    ids = jnp.where((core_index == co) & (ctx_index == c), token_ids[None], 0)
    ids = ids + shift(ids, "x", 1) + shift(ids, "x", -1) + shift(ids, "x", 2)
    ids = ids + sum(flip(ids, ("co", "zl"), b, 4) for b in (1, 2, 3))
    here = lax.dynamic_index_in_dim(ids, c, 1, keepdims=False).reshape(256, 1)
    ids = ids.reshape(4, 512)
    ids_rows = jnp.concatenate([ids // 256, ids % 256]).astype(BF16)

    buckets = lax.dynamic_slice_in_dim(bucket_of_slot, 2 * d, 2)
    gain = jnp.take(norm_gain.reshape(32, 128), buckets, axis=0)
    embed_f32 = embed_tiles.astype(F32)
    scaled = (embed_f32 * gain[:, None, :]).astype(BF16)
    square = jnp.sum(embed_f32 * embed_f32, axis=(0, 2))
    high = lax.reduce_precision(square, 8, 7)
    square_rows = jnp.stack([high, square - high]).astype(BF16)

    def partial_for(core):
        weights = lax.dynamic_slice_in_dim(in_tiles, core * 256, 256, axis=3)
        weights = weights.reshape(2, 128, 3, 8, 32).transpose(0, 1, 3, 2, 4).reshape(2, 128, 768)
        return lax.dot_general(
            weights, scaled, (((0, 1), (0, 2)), ((), ())), preferred_element_type=F32
        )

    given = jnp.concatenate(
        [partial_for(1 - co).astype(BF16), square_rows, jnp.zeros((14, 512), BF16)]
    )
    taken = flip(given, "co", 1, 2).astype(F32)
    table = (partial_for(co) + taken[:768]).astype(BF16).reshape(8, 96, 512)
    square = square + taken[768] + taken[769]
    high = lax.reduce_precision(square, 8, 7)
    square_rows = jnp.stack([high, square - high]).astype(BF16)
    extra = jnp.concatenate([ids_rows, square_rows, jnp.zeros((6, 512), BF16)])
    packed = jnp.concatenate([table, jnp.broadcast_to(extra[None], (8, 16, 512))], axis=1)
    packed = lax.all_to_all(packed, ("zh", "y"), split_axis=0, concat_axis=0, tiled=True)

    first = co * 256 + zy * 32
    taps = lax.dynamic_slice_in_dim(short_taps, first, 32, axis=2).reshape(3, 96, 1)
    skip = lax.dynamic_slice_in_dim(skip_gain, first, 32).reshape(2, 1, 16)
    skip = jnp.broadcast_to(skip, (2, 16, 16)).reshape(2, 256, 1)
    decay = lax.dynamic_slice_in_dim(decay_rate, co * 16 + zy * 2, 2, axis=1)
    weight = lax.dynamic_slice_in_dim(residue, co * 16 + zy * 2, 2, axis=1)
    gated = mixer(packed, taps, skip, decay, weight)
    gated = lax.all_to_all(
        gated.reshape(64, 32, 256), ("zl", "x", "zh", "y"), split_axis=0, concat_axis=0, tiled=True
    ).reshape(8, 256, 256)

    where = jnp.stack([x, y, zh * 2 + zl, co]).astype(jnp.int32)
    own, other = project(where, bucket_of_slot, gated, here, pieces)
    other = flip(other, "co", 1, 2)
    return (own + other.astype(F32)).astype(BF16)[None]


def solution(mesh):
    mesh = Mesh(mesh.devices.reshape(2, 4, 2, 2, 4), ("zh", "y", "co", "zl", "x"))
    in_specs = (
        P(DP, CTX),
        P(),
        P(DP, None, None),
        P(),
        P(DP, None, None, CTX),
        P(None, None, CTX),
        P(None, CTX),
        P(None, CTX),
        P(CTX),
        P(DP, None, CTX),
    )
    out_specs = P(DP, CTX, None)
    return jax.shard_map(body, mesh=mesh, in_specs=in_specs, out_specs=out_specs, check_vma=False)
```

time: 601 us -> 241 us (0.40)
  local copies, waits for them, and re-layouts: 349 us -> 38.4 us
  starting transfers between devices: 0.16 us -> 80 us
  waiting for transfers between devices: 155 us -> 89.7 us
  matrix products: 47.3 us -> 0.81 us
  Pallas kernels: 0 us -> 22.9 us
  loops' own time: 22.9 us -> 0 us
  between operations: 13.5 us -> 0.47 us
    gather x4 -> x1, local copies, waits for them, and re-layouts: 270 us -> 0.56 us  [body(): gain = jnp.take(norm_gain.reshape(32, 128), buckets, axis=0)]
    reduce_scatter x1 -> x0, waiting for transfers between devices: 91.1 us -> none  [body(): lax.psum_scatter(lax.dot_general(gated, w_out, (((1,), (1,)), ((), ())),...]
    ppermute x0 -> x45, starting transfers between devices: none -> 69.4 us  [the longest x39 53.6 us: shift(): return lax.ppermute(value, axis, [(i, (i + step) % 4) for i in range(4)])]
    all_gather x4 -> x0, waiting for transfers between devices: 61.5 us -> none  [the longest x1 61.5 us: body(): piece = lax.all_gather(embed_tiles, 'dp', axis=0, tiled=True)]
    ppermute x0 -> x45, waiting for transfers between devices: none -> 56 us  [the longest x39 53.7 us: shift(): return lax.ppermute(value, axis, [(i, (i + step) % 4) for i in range(4)])]
    dot_general x7 -> x2, matrix products: 47.3 us -> 0.81 us  [partial_for(): lax.dot_general(weights, scaled, (((0, 1), (0, 2)), ((), ())), preferred_...]
    all_to_all x0 -> x2, waiting for transfers between devices: none -> 33.6 us  [the longest x1 33.6 us: body(): lax.all_to_all(packed, ('zh', 'y'), split_axis=0, concat_axis=0, tiled=True)]
    all_gather x2 -> x0, local copies, waits for them, and re-layouts: 29.2 us -> none  [the longest x1 17.2 us: body(): piece = lax.all_gather(in_tiles, 'dp', axis=0, tiled=True)]
  transfers between devices with their start and end apart: 5 -> 47, of which waited for: 2 -> 8; matrix products, arithmetic and copies ran while one was open for 53% -> 18% of each run, Pallas kernels for 0% -> 4%
where the time goes in v1:
time: 241 us; the launch traced here: 240 us
  waiting for transfers between devices  89.7 us (37%)
  starting transfers between devices  80 us (33%)
  local copies, waits for them, and re-layouts  38.4 us (16%)
  Pallas kernels  22.9 us (10%)
  other arithmetic  8.07 us (3%)
    ppermute x39, waiting for transfers between devices, shift(): return lax.ppermute(value, axis, [(i, (i + step) % 4) for i in range(4)])  53.7 us
    ppermute x39, starting transfers between devices, shift(): return lax.ppermute(value, axis, [(i, (i + step) % 4) for i in range(4)])  53.6 us
    all_to_all x1, waiting for transfers between devices, body(): lax.all_to_all(packed, ('zh', 'y'), split_axis=0, concat_axis=0, tiled=True)  33.6 us
    ppermute x6, starting transfers between devices, flip(): return lax.ppermute(value, axes, [(i, i ^ bits) for i in range(size)])  15.9 us
    pallas_call x1, Pallas kernels, project(): pl.pallas_call(project_kernel, out_shape=(jax.ShapeDtypeStruct((128, D),...  13.8 us
    unnamed x45, local copies, waits for them, and re-layouts  13.7 us
    pallas_call x1, Pallas kernels, mixer(): pl.pallas_call(mixer_kernel, out_shape=jax.ShapeDtypeStruct((8, 8, 32, 25...  9.11 us
    slice x9, local copies, waits for them, and re-layouts, ring(): first = shift(below[:half], axis, 1)  7.63 us
  transfers between devices with their start and end apart: 47, of which 8 were waited for; matrix products, arithmetic and copies ran while one was open for 18% of the time, Pallas kernels for 4%

profile of v1, /device:TPU:1, one launch (start us, length us, event | category | flops | bytes accessed | tf_op | source)
XLA Modules:
  0.0 240.3 jit_solution(3639921432483119645)
XLA Ops:
  0.0 0.8 and_select_fusion
  0.8 3.4 %collective-permute-start.2 = (s32[2,8,128]{2,0,1:T(2,128)S(1)}, s32[2,8,128]{2,0,1:T(2,128)S(1)}, u32[]{:S(2)}, u32[]{:S(2)}) collective-permute-start(s32[2,8,128]{2,0,1:T(2,128)S(1)} %and_select_fusion), channel_id=1, source_target_pairs={{0,3},{1,0},{2,1},{3,2},{4,7},{5,4},{6,5},{7,6},{8,11},{9,8},{10,9... | collective-permute-start | bytes 24584 | tf_op jit(solution)/shard_map/ppermute | solution.py:21
  5.3 0.7 constant_dynamic-slice_fusion.2
  6.1 1.0 constant_dynamic-slice_fusion.3
  7.1 1.6 collective-permute-start.7
  8.7 1.1 fusion.3
  9.8 0.7 compare_and_fusion
  12.3 1.1 maximum_maximum_fusion
  13.7 0.8 copy.12
  14.6 1.6 collective-permute-start.6
  16.7 0.8 constant_dynamic-update-slice_fusion.32
  17.5 3.6 %collective-permute-start.33 = (bf16[4,48,256]{2,1,0:T(8,128)(2,1)S(1)}, bf16[4,48,256]{2,1,0:T(8,128)(2,1)S(1)}, u32[]{:S(2)}, u32[]{:S(2)}) collective-permute-start(bf16[4,48,256]{2,1,0:T(8,128)(2,1)S(1)} %get-tuple-element.21), channel_id=1, source_target_pairs={{0,68},{4,0},{64,4},{68,64},{1,69},{5,1},{65,5},{69,65},{2,70},{6,... | collective-permute-start | bytes 294920 | tf_op jit(solution)/shard_map/ppermute | solution.py:21
  21.1 2.7 %collective-permute-start.21 = (bf16[4,48,256]{2,1,0:T(8,128)(2,1)S(1)}, bf16[4,48,256]{2,1,0:T(8,128)(2,1)S(1)}, u32[]{:S(2)}, u32[]{:S(2)}) collective-permute-start(bf16[4,48,256]{2,1,0:T(8,128)(2,1)S(1)} %get-tuple-element.22), channel_id=1, source_target_pairs={{0,48},{16,0},{32,16},{48,32},{1,49},{17,1},{33,17},{49,33},{2,50}... | collective-permute-start | bytes 294920 | tf_op jit(solution)/shard_map/ppermute | solution.py:21
  23.9 2.1 collective-permute-start.9
  26.1 2.7 %collective-permute-start.35 = (bf16[2,48,256]{2,1,0:T(8,128)(2,1)S(1)}, bf16[2,48,256]{2,1,0:T(8,128)(2,1)S(1)}, u32[]{:S(2)}, u32[]{:S(2)}) collective-permute-start(bf16[2,48,256]{2,1,0:T(8,128)(2,1)S(1)} %slice.117), channel_id=1, source_target_pairs={{0,68},{4,0},{64,4},{68,64},{1,69},{5,1},{65,5},{69,65},{2,70},{6,... | collective-permute-start | bytes 147464 | tf_op jit(solution)/shard_map/ppermute | solution.py:21
  29.0 2.7 %collective-permute-start.23 = (bf16[2,48,256]{2,1,0:T(8,128)(2,1)S(1)}, bf16[2,48,256]{2,1,0:T(8,128)(2,1)S(1)}, u32[]{:S(2)}, u32[]{:S(2)}) collective-permute-start(bf16[2,48,256]{2,1,0:T(8,128)(2,1)S(1)} %slice.110), channel_id=1, source_target_pairs={{0,48},{16,0},{32,16},{48,32},{1,49},{17,1},{33,17},{49,33},{2,50}... | collective-permute-start | bytes 147464 | tf_op jit(solution)/shard_map/ppermute | solution.py:21
  33.1 0.7 constant_dynamic-update-slice_fusion.17
  34.5 2.6 %collective-permute-start.11 = (bf16[2,48,256]{2,1,0:T(8,128)(2,1)S(1)}, bf16[2,48,256]{2,1,0:T(8,128)(2,1)S(1)}, u32[]{:S(2)}, u32[]{:S(2)}) collective-permute-start(bf16[2,48,256]{2,1,0:T(8,128)(2,1)S(1)} %slice.103), channel_id=1, source_target_pairs={{0,3},{1,0},{2,1},{3,2},{4,7},{5,4},{6,5},{7,6},{8,11},{9,8},{10,9... | collective-permute-start | bytes 147464 | tf_op jit(solution)/shard_map/ppermute | solution.py:21
  39.7 2.7 %collective-permute-start.37 = (bf16[16,48,256]{2,1,0:T(8,128)(2,1)S(1)}, bf16[16,48,256]{2,1,0:T(8,128)(2,1)S(1)}, u32[]{:S(2)}, u32[]{:S(2)}) collective-permute-start(bf16[16,48,256]{2,1,0:T(8,128)(2,1)S(1)} %get-tuple-element.40), channel_id=1, source_target_pairs={{0,3},{1,0},{2,1},{3,2},{4,7},{5,4},{6,5},{7,6},{8,11},{9,8},{10,9... | collective-permute-start | bytes 1179656 | tf_op jit(solution)/shard_map/ppermute | solution.py:21
  43.9 2.7 %collective-permute-start.13 = (bf16[16,48,256]{2,1,0:T(8,128)(2,1)}, bf16[16,48,256]{2,1,0:T(8,128)(2,1)S(1)}, u32[]{:S(2)}, u32[]{:S(2)}) collective-permute-start(bf16[16,48,256]{2,1,0:T(8,128)(2,1)} %get-tuple-element.48), channel_id=1, source_target_pairs={{0,48},{16,0},{32,16},{48,32},{1,49},{17,1},{33,17},{49,33},{2,50}... | collective-permute-start | bytes 1179656 | tf_op jit(solution)/shard_map/ppermute | solution.py:21
  47.8 2.6 %collective-permute-start.25 = (bf16[16,48,256]{2,1,0:T(8,128)(2,1)}, bf16[16,48,256]{2,1,0:T(8,128)(2,1)S(1)}, u32[]{:S(2)}, u32[]{:S(2)}) collective-permute-start(bf16[16,48,256]{2,1,0:T(8,128)(2,1)} %get-tuple-element.44), channel_id=1, source_target_pairs={{0,68},{4,0},{64,4},{68,64},{1,69},{5,1},{65,5},{69,65},{2,70},{6,... | collective-permute-start | bytes 1179656 | tf_op jit(solution)/shard_map/ppermute | solution.py:21
  50.5 2.7 %collective-permute-start.39 = (bf16[8,48,256]{2,1,0:T(8,128)(2,1)S(1)}, bf16[8,48,256]{2,1,0:T(8,128)(2,1)S(1)}, u32[]{:S(2)}, u32[]{:S(2)}) collective-permute-start(bf16[8,48,256]{2,1,0:T(8,128)(2,1)S(1)} %slice.119), channel_id=1, source_target_pairs={{0,3},{1,0},{2,1},{3,2},{4,7},{5,4},{6,5},{7,6},{8,11},{9,8},{10,9... | collective-permute-start | bytes 589832 | tf_op jit(solution)/shard_map/ppermute | solution.py:21
  53.3 0.8 constant_dynamic-update-slice_fusion.36
  54.1 0.8 constant_dynamic-update-slice_fusion.35
  54.9 4.5 %collective-permute-done.38 = bf16[8,48,256]{2,1,0:T(8,128)(2,1)S(1)} collective-permute-done((bf16[8,48,256]{2,1,0:T(8,128)(2,1)S(1)}, bf16[8,48,256]{2,1,0:T(8,128)(2,1)S(1)}, u32[]{:S(2)}, u32[]{:S(2)}) %collective-permute-start.38) | collective-permute-done | bytes 196640 | tf_op jit(solution)/shard_map/ppermute | solution.py:21
  59.4 0.7 constant_dynamic-update-slice_fusion.34
  60.1 6.7 %collective-permute-start = (bf16[784,512]{1,0:T(8,128)(2,1)S(1)}, bf16[784,512]{1,0:T(8,128)(2,1)S(1)}, u32[]{:S(2)}, u32[]{:S(2)}) collective-permute-start(bf16[784,512]{1,0:T(8,128)(2,1)S(1)} %copy-done.6), channel_id=1, source_target_pairs={{0,8},{8,0},{1,9},{9,1},{2,10},{10,2},{3,11},{11,3},{4,12},{12,4},... | collective-permute-start | bytes 2408456 | tf_op jit(solution)/shard_map/ppermute | solution.py:25
  67.5 3.0 %collective-permute-start.41 = (bf16[64,48,256]{2,1,0:T(8,128)(2,1)}, bf16[64,48,256]{2,1,0:T(8,128)(2,1)S(1)}, u32[]{:S(2)}, u32[]{:S(2)}) collective-permute-start(bf16[64,48,256]{2,1,0:T(8,128)(2,1)} %constant_dynamic-update-slice_fusion.33.refs_10_), channel_id=1, source_target_pairs={{0,48},{16,0},{32,16},{48,32},{1,49},{17,1},{33,17},{49,33},{2,50}... | collective-permute-start | bytes 4718600 | tf_op jit(solution)/shard_map/ppermute | solution.py:21
  70.4 0.7 slice.105
  71.8 3.0 %collective-permute-start.27 = (bf16[8,48,256]{2,1,0:T(8,128)(2,1)}, bf16[8,48,256]{2,1,0:T(8,128)(2,1)}, u32[]{:S(2)}, u32[]{:S(2)}) collective-permute-start(bf16[8,48,256]{2,1,0:T(8,128)(2,1)} %slice.112), channel_id=1, source_target_pairs={{0,68},{4,0},{64,4},{68,64},{1,69},{5,1},{65,5},{69,65},{2,70},{6,... | collective-permute-start | bytes 589832 | tf_op jit(solution)/shard_map/ppermute | solution.py:21
  75.5 0.7 slice.104
  76.2 0.8 constant_dynamic-update-slice_fusion.22
  77.1 0.8 constant_dynamic-update-slice_fusion.21
  78.1 1.5 collective-permute-start.40
  79.7 3.2 %collective-permute-done.26 = bf16[8,48,256]{2,1,0:T(8,128)(2,1)} collective-permute-done((bf16[8,48,256]{2,1,0:T(8,128)(2,1)}, bf16[8,48,256]{2,1,0:T(8,128)(2,1)}, u32[]{:S(2)}, u32[]{:S(2)}) %collective-permute-start.26) | collective-permute-done | bytes 196640 | tf_op jit(solution)/shard_map/ppermute | solution.py:21
  82.9 1.1 collective-permute-start.14
  84.0 1.6 constant_dynamic-update-slice_fusion.20
  85.6 1.6 constant_dynamic-update-slice_fusion.19.refs_5_
  87.3 30.0 %collective-permute-done.14 = bf16[8,48,256]{2,1,0:T(8,128)(2,1)S(1)} collective-permute-done((bf16[8,48,256]{2,1,0:T(8,128)(2,1)}, bf16[8,48,256]{2,1,0:T(8,128)(2,1)S(1)}, u32[]{:S(2)}, u32[]{:S(2)}) %collective-permute-start.14) | collective-permute-done | bytes 196640 | tf_op jit(solution)/shard_map/ppermute | solution.py:21
  117.2 0.7 constant_dynamic-update-slice_fusion.6
  118.0 1.6 constant_dynamic-update-slice_fusion.5.refs_0_
  119.6 4.3 %collective-permute-start.17 = (bf16[64,48,256]{2,1,0:T(8,128)(2,1)}, bf16[64,48,256]{2,1,0:T(8,128)(2,1)}, u32[]{:S(2)}, u32[]{:S(2)}) collective-permute-start(bf16[64,48,256]{2,1,0:T(8,128)(2,1)} %constant_dynamic-update-slice_fusion.5.refs_0_), channel_id=1, source_target_pairs={{0,68},{4,0},{64,4},{68,64},{1,69},{5,1},{65,5},{69,65},{2,70},{6,... | collective-permute-start | bytes 4718600 | tf_op jit(solution)/shard_map/ppermute | solution.py:21
  124.3 1.0 pad_maximum_fusion
  125.3 3.7 %all-to-all-start = ((bf16[8,112,512]{2,1,0:T(8,128)(2,1)}), bf16[8,112,512]{2,1,0:T(8,128)(2,1)S(1)}, u32[]{:S(2)}, u32[]{:S(2)}) async-start(bf16[8,112,512]{2,1,0:T(8,128)(2,1)} %pad_maximum_fusion), calls=%async_computation | async-start | bytes 1835008 | tf_op jit(solution)/shard_map/all_to_all | solution.py:282
  129.0 1.0 slice.121
  130.0 2.6 %collective-permute-start.43 = (bf16[32,48,256]{2,1,0:T(8,128)(2,1)}, bf16[32,48,256]{2,1,0:T(8,128)(2,1)S(1)}, u32[]{:S(2)}, u32[]{:S(2)}) collective-permute-start(bf16[32,48,256]{2,1,0:T(8,128)(2,1)} %slice.121), channel_id=1, source_target_pairs={{0,48},{16,0},{32,16},{48,32},{1,49},{17,1},{33,17},{49,33},{2,50}... | collective-permute-start | bytes 2359304 | tf_op jit(solution)/shard_map/ppermute | solution.py:21
  132.5 0.8 dynamic_slice.41
  133.9 33.6 %all-to-all-done.recv = bf16[8,112,512]{2,1,0:T(8,128)(2,1)S(1)} async-done(((bf16[8,112,512]{2,1,0:T(8,128)(2,1)}), bf16[8,112,512]{2,1,0:T(8,128)(2,1)S(1)}, u32[]{:S(2)}, u32[]{:S(2)}) %all-to-all-start) | async-done | bytes 917536 | tf_op jit(solution)/shard_map/all_to_all | solution.py:282
  167.5 9.1 %mixer.1 = bf16[8,8,32,256]{3,2,1,0:T(8,128)(2,1)} custom-call(bf16[8,112,512]{2,1,0:T(8,128)(2,1)S(1)} %all-to-all-done.recv, f32[3,96,1]{2,1,0:T(8,128)S(1)} %reshape.114.taps, f32[2,256,1]{2,1,0:T(8,128)S(1)} %reshape.115.skip, f32[16,2]{1,0:T(8,128)S(1)} %get-tuple-element.57.decay, f32[16,2]{1,0:T(8,128)S(1)} %get-tuple-element.56.residue), custom_call_target="tpu_custom_call" | custom-call | flops 1610612736 | bytes 4194304 | tf_op jit(solution)/shard_map/mixer/pallas_call | solution.py:114
  176.7 6.9 %all-to-all-start.1 = ((bf16[64,32,256]{2,1,0:T(8,128)(2,1)}), bf16[64,32,256]{2,1,0:T(8,128)(2,1)}, u32[]{:S(2)}, u32[]{:S(2)}) async-start(bf16[64,32,256]{2,1,0:T(8,128)(2,1)} %bitcast.16), calls=%async_computation.1 | async-start | bytes 2097152 | tf_op jit(solution)/shard_map/all_to_all | solution.py:291
  183.6 2.1 slice.120
  185.6 0.9 collective-permute-start.42
  186.6 2.1 slice.114
  188.7 2.4 %collective-permute-start.31 = (bf16[32,48,256]{2,1,0:T(8,128)(2,1)}, bf16[32,48,256]{2,1,0:T(8,128)(2,1)S(1)}, u32[]{:S(2)}, u32[]{:S(2)}) collective-permute-start(bf16[32,48,256]{2,1,0:T(8,128)(2,1)} %slice.114), channel_id=1, source_target_pairs={{0,3},{1,0},{2,1},{3,2},{4,7},{5,4},{6,5},{7,6},{8,11},{9,8},{10,9... | collective-permute-start | bytes 2359304 | tf_op jit(solution)/shard_map/ppermute | solution.py:21
  191.1 2.1 slice.113
  193.2 2.1 slice.107
  195.2 2.6 %collective-permute-start.19 = (bf16[32,48,256]{2,1,0:T(8,128)(2,1)}, bf16[32,48,256]{2,1,0:T(8,128)(2,1)}, u32[]{:S(2)}, u32[]{:S(2)}) collective-permute-start(bf16[32,48,256]{2,1,0:T(8,128)(2,1)} %slice.107), channel_id=1, source_target_pairs={{0,68},{4,0},{64,4},{68,64},{1,69},{5,1},{65,5},{69,65},{2,70},{6,... | collective-permute-start | bytes 2359304 | tf_op jit(solution)/shard_map/ppermute | solution.py:21
  197.9 2.1 slice.106
  200.2 14.5 %collective-permute-done.42.refs_13_ = bf16[32,48,256]{2,1,0:T(8,128)(2,1)S(1)} collective-permute-done((bf16[32,48,256]{2,1,0:T(8,128)(2,1)}, bf16[32,48,256]{2,1,0:T(8,128)(2,1)S(1)}, u32[]{:S(2)}, u32[]{:S(2)}) %collective-permute-start.42) | collective-permute-done | bytes 786464 | tf_op jit(solution)/shard_map/ppermute | solution.py:21
  214.8 1.3 collective-permute-done.18.refs_3_
  216.0 13.8 %project.1 = (f32[128,4096]{1,0:T(8,128)}, bf16[128,4096]{1,0:T(8,128)(2,1)S(1)}) custom-call(s32[4]{0:T(128)S(1)} %pad_add_fusion.where, s32[32]{0:T(128)S(1)} %copy-done.1, bf16[8,256,256]{2,1,0:T(8,128)(2,1)} %bitcast.17.gated, s32[256,1]{1,0:T(8,128)S(1)} %copy.20.ids, bf16[64,48,256]{2,1,0:T(8,128)(2,1)} %constant_dynamic-update-slice_fusion.5.refs_0_, ...), custom_call_target="tpu_custom_call" | custom-call | flops 4294967296 | bytes 25165824 | tf_op jit(solution)/shard_map/project/pallas_call | solution.py:200
  229.8 5.5 %collective-permute-start.44 = (bf16[128,4096]{1,0:T(8,128)(2,1)S(1)}, bf16[128,4096]{1,0:T(8,128)(2,1)S(1)}, u32[]{:S(2)}, u32[]{:S(2)}) collective-permute-start(bf16[128,4096]{1,0:T(8,128)(2,1)S(1)} %get-tuple-element.8), channel_id=1, source_target_pairs={{0,8},{8,0},{1,9},{9,1},{2,10},{10,2},{3,11},{11,3},{4,12},{12,4},... | collective-permute-start | bytes 3145736 | tf_op jit(solution)/shard_map/ppermute | solution.py:25
  235.2 2.3 collective-permute-done.44
  237.5 2.8 %fusion.1 = bf16[1,128,4096]{2,1,0:T(8,128)(2,1)} fusion(f32[128,4096]{1,0:T(8,128)} %get-tuple-element.7, bf16[128,4096]{1,0:T(8,128)(2,1)S(1)} %collective-permute-done.44), kind=kLoop, calls=%fused_computation.5 | loop fusion | flops 1572864 | bytes 4194304 | tf_op jit(solution)/shard_map/broadcast_in_dim | solution.py:298
  (147 shorter events, 15.2 us)
Async XLA Ops:
  0.0 133.4 %copy-start = (f32[3,3,512]{2,1,0:T(4,128)S(1)}, f32[3,3,512]{2,1,0:T(4,128)}, u32[]{:S(2)}) copy-start(f32[3,3,512]{2,1,0:T(4,128)} %param.15) | copy-start | bytes 55300
  0.0 10.5 %copy-start.7 = (bf16[2,128,3,512]{3,1,2,0:T(8,128)(2,1)S(1)}, bf16[2,128,3,512]{3,1,2,0:T(8,128)(2,1)}, u32[]{:S(2)}) copy-start(bf16[2,128,3,512]{3,1,2,0:T(8,128)(2,1)} %param.14) | copy-start | bytes 2359300
  0.8 13.7 %collective-permute-start.2 = (s32[2,8,128]{2,0,1:T(2,128)S(1)}, s32[2,8,128]{2,0,1:T(2,128)S(1)}, u32[]{:S(2)}, u32[]{:S(2)}) collective-permute-start(s32[2,8,128]{2,0,1:T(2,128)S(1)} %and_select_fusion), channel_id=1, source_target_pairs={{0,3},{1,0},{2,1},{3,2},{4,7},{5,4},{6,5},{7,6},{8,11},{9,8},{10,9... | collective-permute-start | bytes 24584 | tf_op jit(solution)/shard_map/ppermute | solution.py:21
  4.2 10.3 %collective-permute-start.3 = (s32[2,8,128]{2,0,1:T(2,128)S(1)}, s32[2,8,128]{2,0,1:T(2,128)S(1)}, u32[]{:S(2)}, u32[]{:S(2)}) collective-permute-start(s32[2,8,128]{2,0,1:T(2,128)S(1)} %and_select_fusion), channel_id=1, source_target_pairs={{0,2},{1,3},{2,0},{3,1},{4,6},{5,7},{6,4},{7,5},{8,10},{9,11},{10,... | collective-permute-start | bytes 24584 | tf_op jit(solution)/shard_map/ppermute | solution.py:21
  4.7 9.8 %collective-permute-start.1 = (s32[2,8,128]{2,0,1:T(2,128)S(1)}, s32[2,8,128]{2,0,1:T(2,128)S(1)}, u32[]{:S(2)}, u32[]{:S(2)}) collective-permute-start(s32[2,8,128]{2,0,1:T(2,128)S(1)} %and_select_fusion), channel_id=1, source_target_pairs={{0,1},{1,2},{2,3},{3,0},{4,5},{5,6},{6,7},{7,4},{8,9},{9,10},{10,1... | collective-permute-start | bytes 24584 | tf_op jit(solution)/shard_map/ppermute | solution.py:21
  7.1 9.6 %collective-permute-start.7 = (bf16[2,144,256]{2,1,0:T(8,128)(2,1)S(1)}, bf16[2,144,256]{2,1,0:T(8,128)(2,1)S(1)}, u32[]{:S(2)}, u32[]{:S(2)}) collective-permute-start(bf16[2,144,256]{2,1,0:T(8,128)(2,1)S(1)} %pad_maximum_fusion.2), channel_id=1, source_target_pairs={{0,8},{8,0},{1,9},{9,1},{2,10},{10,2},{3,11},{11,3},{4,12},{12,4},... | collective-permute-start | bytes 442376 | tf_op jit(solution)/shard_map/ppermute | solution.py:25
  10.6 0.7 copy-start.10
  10.6 1.3 copy-start.3
  12.3 2.2 copy-start.11
  14.6 6.5 %collective-permute-start.6 = (s32[2,8,128]{2,0,1:T(2,128)S(1)}, s32[2,8,128]{2,0,1:T(2,128)S(1)}, u32[]{:S(2)}, u32[]{:S(2)}) collective-permute-start(s32[2,8,128]{2,0,1:T(2,128)S(1)} %add_add_fusion.1), channel_id=1, source_target_pairs={{0,12},{4,8},{8,4},{12,0},{1,13},{5,9},{9,5},{13,1},{2,14},{6,10},... | collective-permute-start | bytes 24584 | tf_op jit(solution)/shard_map/ppermute | solution.py:25
  16.2 7.6 %collective-permute-start.5 = (s32[2,8,128]{2,0,1:T(2,128)S(1)}, s32[2,8,128]{2,0,1:T(2,128)S(1)}, u32[]{:S(2)}, u32[]{:S(2)}) collective-permute-start(s32[2,8,128]{2,0,1:T(2,128)S(1)} %add_add_fusion.1), channel_id=1, source_target_pairs={{0,8},{4,12},{8,0},{12,4},{1,9},{5,13},{9,1},{13,5},{2,10},{6,14},... | collective-permute-start | bytes 24584 | tf_op jit(solution)/shard_map/ppermute | solution.py:25
  16.7 7.2 %collective-permute-start.4 = (s32[2,8,128]{2,0,1:T(2,128)S(1)}, s32[2,8,128]{2,0,1:T(2,128)S(1)}, u32[]{:S(2)}, u32[]{:S(2)}) collective-permute-start(s32[2,8,128]{2,0,1:T(2,128)S(1)} %add_add_fusion.1), channel_id=1, source_target_pairs={{0,4},{4,0},{8,12},{12,8},{1,5},{5,1},{9,13},{13,9},{2,6},{6,2},{1... | collective-permute-start | bytes 24584 | tf_op jit(solution)/shard_map/ppermute | solution.py:25
  17.5 8.5 %collective-permute-start.33 = (bf16[4,48,256]{2,1,0:T(8,128)(2,1)S(1)}, bf16[4,48,256]{2,1,0:T(8,128)(2,1)S(1)}, u32[]{:S(2)}, u32[]{:S(2)}) collective-permute-start(bf16[4,48,256]{2,1,0:T(8,128)(2,1)S(1)} %get-tuple-element.21), channel_id=1, source_target_pairs={{0,68},{4,0},{64,4},{68,64},{1,69},{5,1},{65,5},{69,65},{2,70},{6,... | collective-permute-start | bytes 294920 | tf_op jit(solution)/shard_map/ppermute | solution.py:21
  21.1 5.0 %collective-permute-start.32 = (bf16[4,48,256]{2,1,0:T(8,128)(2,1)S(1)}, bf16[4,48,256]{2,1,0:T(8,128)(2,1)S(1)}, u32[]{:S(2)}, u32[]{:S(2)}) collective-permute-start(bf16[4,48,256]{2,1,0:T(8,128)(2,1)S(1)} %get-tuple-element.21), channel_id=1, source_target_pairs={{0,4},{4,64},{64,68},{68,0},{1,5},{5,65},{65,69},{69,1},{2,6},{6,6... | collective-permute-start | bytes 294920 | tf_op jit(solution)/shard_map/ppermute | solution.py:21
  21.1 7.8 %collective-permute-start.21 = (bf16[4,48,256]{2,1,0:T(8,128)(2,1)S(1)}, bf16[4,48,256]{2,1,0:T(8,128)(2,1)S(1)}, u32[]{:S(2)}, u32[]{:S(2)}) collective-permute-start(bf16[4,48,256]{2,1,0:T(8,128)(2,1)S(1)} %get-tuple-element.22), channel_id=1, source_target_pairs={{0,48},{16,0},{32,16},{48,32},{1,49},{17,1},{33,17},{49,33},{2,50}... | collective-permute-start | bytes 294920 | tf_op jit(solution)/shard_map/ppermute | solution.py:21
  23.9 5.1 %collective-permute-start.20 = (bf16[4,48,256]{2,1,0:T(8,128)(2,1)S(1)}, bf16[4,48,256]{2,1,0:T(8,128)(2,1)S(1)}, u32[]{:S(2)}, u32[]{:S(2)}) collective-permute-start(bf16[4,48,256]{2,1,0:T(8,128)(2,1)S(1)} %get-tuple-element.22), channel_id=1, source_target_pairs={{0,16},{16,32},{32,48},{48,0},{1,17},{17,33},{33,49},{49,1},{2,18}... | collective-permute-start | bytes 294920 | tf_op jit(solution)/shard_map/ppermute | solution.py:21
  23.9 7.8 %collective-permute-start.9 = (bf16[4,48,256]{2,1,0:T(8,128)(2,1)S(1)}, bf16[4,48,256]{2,1,0:T(8,128)(2,1)S(1)}, u32[]{:S(2)}, u32[]{:S(2)}) collective-permute-start(bf16[4,48,256]{2,1,0:T(8,128)(2,1)S(1)} %get-tuple-element.23), channel_id=1, source_target_pairs={{0,3},{1,0},{2,1},{3,2},{4,7},{5,4},{6,5},{7,6},{8,11},{9,8},{10,9... | collective-permute-start | bytes 294920 | tf_op jit(solution)/shard_map/ppermute | solution.py:21
  26.0 8.4 %collective-permute-start.8 = (bf16[4,48,256]{2,1,0:T(8,128)(2,1)S(1)}, bf16[4,48,256]{2,1,0:T(8,128)(2,1)S(1)}, u32[]{:S(2)}, u32[]{:S(2)}) collective-permute-start(bf16[4,48,256]{2,1,0:T(8,128)(2,1)S(1)} %get-tuple-element.23), channel_id=1, source_target_pairs={{0,1},{1,2},{2,3},{3,0},{4,5},{5,6},{6,7},{7,4},{8,9},{9,10},{10,1... | collective-permute-start | bytes 294920 | tf_op jit(solution)/shard_map/ppermute | solution.py:21
  26.1 13.0 %collective-permute-start.35 = (bf16[2,48,256]{2,1,0:T(8,128)(2,1)S(1)}, bf16[2,48,256]{2,1,0:T(8,128)(2,1)S(1)}, u32[]{:S(2)}, u32[]{:S(2)}) collective-permute-start(bf16[2,48,256]{2,1,0:T(8,128)(2,1)S(1)} %slice.117), channel_id=1, source_target_pairs={{0,68},{4,0},{64,4},{68,64},{1,69},{5,1},{65,5},{69,65},{2,70},{6,... | collective-permute-start | bytes 147464 | tf_op jit(solution)/shard_map/ppermute | solution.py:21
  28.9 9.5 %collective-permute-start.34 = (bf16[2,48,256]{2,1,0:T(8,128)(2,1)S(1)}, bf16[2,48,256]{2,1,0:T(8,128)(2,1)S(1)}, u32[]{:S(2)}, u32[]{:S(2)}) collective-permute-start(bf16[2,48,256]{2,1,0:T(8,128)(2,1)S(1)} %slice.116), channel_id=1, source_target_pairs={{0,4},{4,64},{64,68},{68,0},{1,5},{5,65},{65,69},{69,1},{2,6},{6,6... | collective-permute-start | bytes 147464 | tf_op jit(solution)/shard_map/ppermute | solution.py:21
  29.0 18.2 %collective-permute-start.23 = (bf16[2,48,256]{2,1,0:T(8,128)(2,1)S(1)}, bf16[2,48,256]{2,1,0:T(8,128)(2,1)S(1)}, u32[]{:S(2)}, u32[]{:S(2)}) collective-permute-start(bf16[2,48,256]{2,1,0:T(8,128)(2,1)S(1)} %slice.110), channel_id=1, source_target_pairs={{0,48},{16,0},{32,16},{48,32},{1,49},{17,1},{33,17},{49,33},{2,50}... | collective-permute-start | bytes 147464 | tf_op jit(solution)/shard_map/ppermute | solution.py:21
  31.7 14.9 %collective-permute-start.22 = (bf16[2,48,256]{2,1,0:T(8,128)(2,1)S(1)}, bf16[2,48,256]{2,1,0:T(8,128)(2,1)S(1)}, u32[]{:S(2)}, u32[]{:S(2)}) collective-permute-start(bf16[2,48,256]{2,1,0:T(8,128)(2,1)S(1)} %slice.109), channel_id=1, source_target_pairs={{0,16},{16,32},{32,48},{48,0},{1,17},{17,33},{33,49},{49,1},{2,18}... | collective-permute-start | bytes 147464 | tf_op jit(solution)/shard_map/ppermute | solution.py:21
  34.5 8.8 %collective-permute-start.11 = (bf16[2,48,256]{2,1,0:T(8,128)(2,1)S(1)}, bf16[2,48,256]{2,1,0:T(8,128)(2,1)S(1)}, u32[]{:S(2)}, u32[]{:S(2)}) collective-permute-start(bf16[2,48,256]{2,1,0:T(8,128)(2,1)S(1)} %slice.103), channel_id=1, source_target_pairs={{0,3},{1,0},{2,1},{3,2},{4,7},{5,4},{6,5},{7,6},{8,11},{9,8},{10,9... | collective-permute-start | bytes 147464 | tf_op jit(solution)/shard_map/ppermute | solution.py:21
  38.4 4.2 %collective-permute-start.10 = (bf16[2,48,256]{2,1,0:T(8,128)(2,1)S(1)}, bf16[2,48,256]{2,1,0:T(8,128)(2,1)S(1)}, u32[]{:S(2)}, u32[]{:S(2)}) collective-permute-start(bf16[2,48,256]{2,1,0:T(8,128)(2,1)S(1)} %slice.102), channel_id=1, source_target_pairs={{0,1},{1,2},{2,3},{3,0},{4,5},{5,6},{6,7},{7,4},{8,9},{9,10},{10,1... | collective-permute-start | bytes 147464 | tf_op jit(solution)/shard_map/ppermute | solution.py:21
  39.7 10.8 %collective-permute-start.37 = (bf16[16,48,256]{2,1,0:T(8,128)(2,1)S(1)}, bf16[16,48,256]{2,1,0:T(8,128)(2,1)S(1)}, u32[]{:S(2)}, u32[]{:S(2)}) collective-permute-start(bf16[16,48,256]{2,1,0:T(8,128)(2,1)S(1)} %get-tuple-element.40), channel_id=1, source_target_pairs={{0,3},{1,0},{2,1},{3,2},{4,7},{5,4},{6,5},{7,6},{8,11},{9,8},{10,9... | collective-permute-start | bytes 1179656 | tf_op jit(solution)/shard_map/ppermute | solution.py:21
  42.6 10.6 %collective-permute-start.36 = (bf16[16,48,256]{2,1,0:T(8,128)(2,1)S(1)}, bf16[16,48,256]{2,1,0:T(8,128)(2,1)S(1)}, u32[]{:S(2)}, u32[]{:S(2)}) collective-permute-start(bf16[16,48,256]{2,1,0:T(8,128)(2,1)S(1)} %get-tuple-element.40), channel_id=1, source_target_pairs={{0,1},{1,2},{2,3},{3,0},{4,5},{5,6},{6,7},{7,4},{8,9},{9,10},{10,1... | collective-permute-start | bytes 1179656 | tf_op jit(solution)/shard_map/ppermute | solution.py:21
  43.3 16.8 %copy-start.6 = (bf16[784,512]{1,0:T(8,128)(2,1)S(1)}, bf16[784,512]{1,0:T(8,128)(2,1)}, u32[]{:S(2)}) copy-start(bf16[784,512]{1,0:T(8,128)(2,1)} %maximum_maximum_fusion) | copy-start | bytes 2408452
  43.9 23.6 %collective-permute-start.13 = (bf16[16,48,256]{2,1,0:T(8,128)(2,1)}, bf16[16,48,256]{2,1,0:T(8,128)(2,1)S(1)}, u32[]{:S(2)}, u32[]{:S(2)}) collective-permute-start(bf16[16,48,256]{2,1,0:T(8,128)(2,1)} %get-tuple-element.48), channel_id=1, source_target_pairs={{0,48},{16,0},{32,16},{48,32},{1,49},{17,1},{33,17},{49,33},{2,50}... | collective-permute-start | bytes 1179656 | tf_op jit(solution)/shard_map/ppermute | solution.py:21
  46.5 28.9 %collective-permute-start.12 = (bf16[16,48,256]{2,1,0:T(8,128)(2,1)}, bf16[16,48,256]{2,1,0:T(8,128)(2,1)S(1)}, u32[]{:S(2)}, u32[]{:S(2)}) collective-permute-start(bf16[16,48,256]{2,1,0:T(8,128)(2,1)} %get-tuple-element.48), channel_id=1, source_target_pairs={{0,16},{16,32},{32,48},{48,0},{1,17},{17,33},{33,49},{49,1},{2,18}... | collective-permute-start | bytes 1179656 | tf_op jit(solution)/shard_map/ppermute | solution.py:21
  47.8 23.3 %collective-permute-start.25 = (bf16[16,48,256]{2,1,0:T(8,128)(2,1)}, bf16[16,48,256]{2,1,0:T(8,128)(2,1)S(1)}, u32[]{:S(2)}, u32[]{:S(2)}) collective-permute-start(bf16[16,48,256]{2,1,0:T(8,128)(2,1)} %get-tuple-element.44), channel_id=1, source_target_pairs={{0,68},{4,0},{64,4},{68,64},{1,69},{5,1},{65,5},{69,65},{2,70},{6,... | collective-permute-start | bytes 1179656 | tf_op jit(solution)/shard_map/ppermute | solution.py:21
  50.5 9.6 %collective-permute-start.39 = (bf16[8,48,256]{2,1,0:T(8,128)(2,1)S(1)}, bf16[8,48,256]{2,1,0:T(8,128)(2,1)S(1)}, u32[]{:S(2)}, u32[]{:S(2)}) collective-permute-start(bf16[8,48,256]{2,1,0:T(8,128)(2,1)S(1)} %slice.119), channel_id=1, source_target_pairs={{0,3},{1,0},{2,1},{3,2},{4,7},{5,4},{6,5},{7,6},{8,11},{9,8},{10,9... | collective-permute-start | bytes 589832 | tf_op jit(solution)/shard_map/ppermute | solution.py:21
  53.3 6.1 %collective-permute-start.38 = (bf16[8,48,256]{2,1,0:T(8,128)(2,1)S(1)}, bf16[8,48,256]{2,1,0:T(8,128)(2,1)S(1)}, u32[]{:S(2)}, u32[]{:S(2)}) collective-permute-start(bf16[8,48,256]{2,1,0:T(8,128)(2,1)S(1)} %slice.118), channel_id=1, source_target_pairs={{0,1},{1,2},{2,3},{3,0},{4,5},{5,6},{6,7},{7,4},{8,9},{9,10},{10,1... | collective-permute-start | bytes 589832 | tf_op jit(solution)/shard_map/ppermute | solution.py:21
  59.4 12.5 %collective-permute-start.24 = (bf16[16,48,256]{2,1,0:T(8,128)(2,1)}, bf16[16,48,256]{2,1,0:T(8,128)(2,1)S(1)}, u32[]{:S(2)}, u32[]{:S(2)}) collective-permute-start(bf16[16,48,256]{2,1,0:T(8,128)(2,1)} %get-tuple-element.44), channel_id=1, source_target_pairs={{0,4},{4,64},{64,68},{68,0},{1,5},{5,65},{65,69},{69,1},{2,6},{6,6... | collective-permute-start | bytes 1179656 | tf_op jit(solution)/shard_map/ppermute | solution.py:21
  60.1 17.8 %collective-permute-start = (bf16[784,512]{1,0:T(8,128)(2,1)S(1)}, bf16[784,512]{1,0:T(8,128)(2,1)S(1)}, u32[]{:S(2)}, u32[]{:S(2)}) collective-permute-start(bf16[784,512]{1,0:T(8,128)(2,1)S(1)} %copy-done.6), channel_id=1, source_target_pairs={{0,8},{8,0},{1,9},{9,1},{2,10},{10,2},{3,11},{11,3},{4,12},{12,4},... | collective-permute-start | bytes 2408456 | tf_op jit(solution)/shard_map/ppermute | solution.py:25
  67.5 56.4 %collective-permute-start.41 = (bf16[64,48,256]{2,1,0:T(8,128)(2,1)}, bf16[64,48,256]{2,1,0:T(8,128)(2,1)S(1)}, u32[]{:S(2)}, u32[]{:S(2)}) collective-permute-start(bf16[64,48,256]{2,1,0:T(8,128)(2,1)} %constant_dynamic-update-slice_fusion.33.refs_10_), channel_id=1, source_target_pairs={{0,48},{16,0},{32,16},{48,32},{1,49},{17,1},{33,17},{49,33},{2,50}... | collective-permute-start | bytes 4718600 | tf_op jit(solution)/shard_map/ppermute | solution.py:21
  71.1 46.8 %collective-permute-start.15 = (bf16[8,48,256]{2,1,0:T(8,128)(2,1)}, bf16[8,48,256]{2,1,0:T(8,128)(2,1)}, u32[]{:S(2)}, u32[]{:S(2)}) collective-permute-start(bf16[8,48,256]{2,1,0:T(8,128)(2,1)} %slice.105), channel_id=1, source_target_pairs={{0,48},{16,0},{32,16},{48,32},{1,49},{17,1},{33,17},{49,33},{2,50}... | collective-permute-start | bytes 589832 | tf_op jit(solution)/shard_map/ppermute | solution.py:21
  71.8 13.8 %collective-permute-start.27 = (bf16[8,48,256]{2,1,0:T(8,128)(2,1)}, bf16[8,48,256]{2,1,0:T(8,128)(2,1)}, u32[]{:S(2)}, u32[]{:S(2)}) collective-permute-start(bf16[8,48,256]{2,1,0:T(8,128)(2,1)} %slice.112), channel_id=1, source_target_pairs={{0,68},{4,0},{64,4},{68,64},{1,69},{5,1},{65,5},{69,65},{2,70},{6,... | collective-permute-start | bytes 589832 | tf_op jit(solution)/shard_map/ppermute | solution.py:21
  75.5 7.4 %collective-permute-start.26 = (bf16[8,48,256]{2,1,0:T(8,128)(2,1)}, bf16[8,48,256]{2,1,0:T(8,128)(2,1)}, u32[]{:S(2)}, u32[]{:S(2)}) collective-permute-start(bf16[8,48,256]{2,1,0:T(8,128)(2,1)} %slice.111), channel_id=1, source_target_pairs={{0,4},{4,64},{64,68},{68,0},{1,5},{5,65},{65,69},{69,1},{2,6},{6,6... | collective-permute-start | bytes 589832 | tf_op jit(solution)/shard_map/ppermute | solution.py:21
  76.2 1.6 copy-start.4
  78.1 51.9 %collective-permute-start.40 = (bf16[64,48,256]{2,1,0:T(8,128)(2,1)}, bf16[64,48,256]{2,1,0:T(8,128)(2,1)}, u32[]{:S(2)}, u32[]{:S(2)}) collective-permute-start(bf16[64,48,256]{2,1,0:T(8,128)(2,1)} %constant_dynamic-update-slice_fusion.33.refs_10_), channel_id=1, source_target_pairs={{0,16},{16,32},{32,48},{48,0},{1,17},{17,33},{33,49},{49,1},{2,18}... | collective-permute-start | bytes 4718600 | tf_op jit(solution)/shard_map/ppermute | solution.py:21
  79.7 44.2 %copy-start.5 = (bf16[2,128,8,3,32]{1,4,3,2,0:T(8,128)(2,1)S(1)}, bf16[2,128,8,3,32]{1,4,3,2,0:T(8,128)(2,1)}, u32[]{:S(2)}) copy-start(bf16[2,128,8,3,32]{1,4,3,2,0:T(8,128)(2,1)} %copy.12) | copy-start | bytes 1179652
  82.9 34.4 %collective-permute-start.14 = (bf16[8,48,256]{2,1,0:T(8,128)(2,1)}, bf16[8,48,256]{2,1,0:T(8,128)(2,1)S(1)}, u32[]{:S(2)}, u32[]{:S(2)}) collective-permute-start(bf16[8,48,256]{2,1,0:T(8,128)(2,1)} %slice.104), channel_id=1, source_target_pairs={{0,16},{16,32},{32,48},{48,0},{1,17},{17,33},{33,49},{49,1},{2,18}... | collective-permute-start | bytes 589832 | tf_op jit(solution)/shard_map/ppermute | solution.py:21
  87.3 98.4 %collective-permute-start.29 = (bf16[64,48,256]{2,1,0:T(8,128)(2,1)}, bf16[64,48,256]{2,1,0:T(8,128)(2,1)}, u32[]{:S(2)}, u32[]{:S(2)}) collective-permute-start(bf16[64,48,256]{2,1,0:T(8,128)(2,1)} %constant_dynamic-update-slice_fusion.19.refs_5_), channel_id=1, source_target_pairs={{0,3},{1,0},{2,1},{3,2},{4,7},{5,4},{6,5},{7,6},{8,11},{9,8},{10,9... | collective-permute-start | bytes 4718600 | tf_op jit(solution)/shard_map/ppermute | solution.py:21
  117.2 71.4 %collective-permute-start.28 = (bf16[64,48,256]{2,1,0:T(8,128)(2,1)}, bf16[64,48,256]{2,1,0:T(8,128)(2,1)}, u32[]{:S(2)}, u32[]{:S(2)}) collective-permute-start(bf16[64,48,256]{2,1,0:T(8,128)(2,1)} %constant_dynamic-update-slice_fusion.19.refs_5_), channel_id=1, source_target_pairs={{0,1},{1,2},{2,3},{3,0},{4,5},{5,6},{6,7},{7,4},{8,9},{9,10},{10,1... | collective-permute-start | bytes 4718600 | tf_op jit(solution)/shard_map/ppermute | solution.py:21
  119.6 73.6 %collective-permute-start.17 = (bf16[64,48,256]{2,1,0:T(8,128)(2,1)}, bf16[64,48,256]{2,1,0:T(8,128)(2,1)}, u32[]{:S(2)}, u32[]{:S(2)}) collective-permute-start(bf16[64,48,256]{2,1,0:T(8,128)(2,1)} %constant_dynamic-update-slice_fusion.5.refs_0_), channel_id=1, source_target_pairs={{0,68},{4,0},{64,4},{68,64},{1,69},{5,1},{65,5},{69,65},{2,70},{6,... | collective-permute-start | bytes 4718600 | tf_op jit(solution)/shard_map/ppermute | solution.py:21
  123.8 5.1 %copy-start.2 = (bf16[64,48,256]{2,1,0:T(8,128)(2,1)}, bf16[64,48,256]{2,1,0:T(8,128)(2,1)S(1)}, u32[]{:S(2)}) copy-start(bf16[64,48,256]{2,1,0:T(8,128)(2,1)S(1)} %collective-permute-done.41.refs_12_) | copy-start | bytes 4718596
  123.8 71.4 %collective-permute-start.16 = (bf16[64,48,256]{2,1,0:T(8,128)(2,1)}, bf16[64,48,256]{2,1,0:T(8,128)(2,1)}, u32[]{:S(2)}, u32[]{:S(2)}) collective-permute-start(bf16[64,48,256]{2,1,0:T(8,128)(2,1)} %constant_dynamic-update-slice_fusion.5.refs_0_), channel_id=1, source_target_pairs={{0,4},{4,64},{64,68},{68,0},{1,5},{5,65},{65,69},{69,1},{2,6},{6,6... | collective-permute-start | bytes 4718600 | tf_op jit(solution)/shard_map/ppermute | solution.py:21
  125.3 8.5 %copy-start.8 = (f32[16,32]{1,0:T(8,128)S(1)}, f32[16,32]{1,0:T(8,128)}, u32[]{:S(2)}) copy-start(f32[16,32]{1,0:T(8,128)} %param.17) | copy-start | bytes 6148
  125.3 8.5 %copy-start.9 = (f32[16,32]{1,0:T(8,128)S(1)}, f32[16,32]{1,0:T(8,128)}, u32[]{:S(2)}) copy-start(f32[16,32]{1,0:T(8,128)} %param.16) | copy-start | bytes 6148
  125.3 42.2 %all-to-all-start = ((bf16[8,112,512]{2,1,0:T(8,128)(2,1)}), bf16[8,112,512]{2,1,0:T(8,128)(2,1)S(1)}, u32[]{:S(2)}, u32[]{:S(2)}) async-start(bf16[8,112,512]{2,1,0:T(8,128)(2,1)} %pad_maximum_fusion), calls=%async_computation | async-start | bytes 1835008 | tf_op jit(solution)/shard_map/all_to_all | solution.py:282
  130.0 70.0 %collective-permute-start.43 = (bf16[32,48,256]{2,1,0:T(8,128)(2,1)}, bf16[32,48,256]{2,1,0:T(8,128)(2,1)S(1)}, u32[]{:S(2)}, u32[]{:S(2)}) collective-permute-start(bf16[32,48,256]{2,1,0:T(8,128)(2,1)} %slice.121), channel_id=1, source_target_pairs={{0,48},{16,0},{32,16},{48,32},{1,49},{17,1},{33,17},{49,33},{2,50}... | collective-permute-start | bytes 2359304 | tf_op jit(solution)/shard_map/ppermute | solution.py:21
  176.7 23.6 %all-to-all-start.1 = ((bf16[64,32,256]{2,1,0:T(8,128)(2,1)}), bf16[64,32,256]{2,1,0:T(8,128)(2,1)}, u32[]{:S(2)}, u32[]{:S(2)}) async-start(bf16[64,32,256]{2,1,0:T(8,128)(2,1)} %bitcast.16), calls=%async_computation.1 | async-start | bytes 2097152 | tf_op jit(solution)/shard_map/all_to_all | solution.py:291
  185.6 29.1 %collective-permute-start.42 = (bf16[32,48,256]{2,1,0:T(8,128)(2,1)}, bf16[32,48,256]{2,1,0:T(8,128)(2,1)S(1)}, u32[]{:S(2)}, u32[]{:S(2)}) collective-permute-start(bf16[32,48,256]{2,1,0:T(8,128)(2,1)} %slice.120), channel_id=1, source_target_pairs={{0,16},{16,32},{32,48},{48,0},{1,17},{17,33},{33,49},{49,1},{2,18}... | collective-permute-start | bytes 2359304 | tf_op jit(solution)/shard_map/ppermute | solution.py:21
  188.7 26.1 %collective-permute-start.31 = (bf16[32,48,256]{2,1,0:T(8,128)(2,1)}, bf16[32,48,256]{2,1,0:T(8,128)(2,1)S(1)}, u32[]{:S(2)}, u32[]{:S(2)}) collective-permute-start(bf16[32,48,256]{2,1,0:T(8,128)(2,1)} %slice.114), channel_id=1, source_target_pairs={{0,3},{1,0},{2,1},{3,2},{4,7},{5,4},{6,5},{7,6},{8,11},{9,8},{10,9... | collective-permute-start | bytes 2359304 | tf_op jit(solution)/shard_map/ppermute | solution.py:21
  193.2 22.8 %copy-start.1 = (s32[32]{0:T(128)S(1)}, s32[32]{0:T(128)}, u32[]{:S(2)}) copy-start(s32[32]{0:T(128)} %bucket.1) | copy-start | bytes 388
  193.2 21.6 %collective-permute-start.30 = (bf16[32,48,256]{2,1,0:T(8,128)(2,1)}, bf16[32,48,256]{2,1,0:T(8,128)(2,1)S(1)}, u32[]{:S(2)}, u32[]{:S(2)}) collective-permute-start(bf16[32,48,256]{2,1,0:T(8,128)(2,1)} %slice.113), channel_id=1, source_target_pairs={{0,1},{1,2},{2,3},{3,0},{4,5},{5,6},{6,7},{7,4},{8,9},{9,10},{10,1... | collective-permute-start | bytes 2359304 | tf_op jit(solution)/shard_map/ppermute | solution.py:21
  195.2 19.5 %collective-permute-start.19 = (bf16[32,48,256]{2,1,0:T(8,128)(2,1)}, bf16[32,48,256]{2,1,0:T(8,128)(2,1)}, u32[]{:S(2)}, u32[]{:S(2)}) collective-permute-start(bf16[32,48,256]{2,1,0:T(8,128)(2,1)} %slice.107), channel_id=1, source_target_pairs={{0,68},{4,0},{64,4},{68,64},{1,69},{5,1},{65,5},{69,65},{2,70},{6,... | collective-permute-start | bytes 2359304 | tf_op jit(solution)/shard_map/ppermute | solution.py:21
  200.0 16.0 %collective-permute-start.18 = (bf16[32,48,256]{2,1,0:T(8,128)(2,1)}, bf16[32,48,256]{2,1,0:T(8,128)(2,1)}, u32[]{:S(2)}, u32[]{:S(2)}) collective-permute-start(bf16[32,48,256]{2,1,0:T(8,128)(2,1)} %slice.106), channel_id=1, source_target_pairs={{0,4},{4,64},{64,68},{68,0},{1,5},{5,65},{65,69},{69,1},{2,6},{6,6... | collective-permute-start | bytes 2359304 | tf_op jit(solution)/shard_map/ppermute | solution.py:21
  229.8 7.7 %collective-permute-start.44 = (bf16[128,4096]{1,0:T(8,128)(2,1)S(1)}, bf16[128,4096]{1,0:T(8,128)(2,1)S(1)}, u32[]{:S(2)}, u32[]{:S(2)}) collective-permute-start(bf16[128,4096]{1,0:T(8,128)(2,1)S(1)} %get-tuple-element.8), channel_id=1, source_target_pairs={{0,8},{8,0},{1,9},{9,1},{2,10},{10,2},{3,11},{11,3},{4,12},{12,4},... | collective-permute-start | bytes 3145736 | tf_op jit(solution)/shard_map/ppermute | solution.py:25

commit v2 on v1

--- a/solution.py
+++ b/solution.py
@@ -11,8 +11,6 @@
 D = 4096
 SEQ = 1024
 EPS = 1e-06
-OFFSETS = (0, 3, 1, 2)
-ZAX = ("zh", "zl")
 DP = ("zh", "y", "co")
 CTX = ("zl", "x")
 
@@ -23,21 +21,6 @@
 
 def flip(value, axes, bits, size):
     return lax.ppermute(value, axes, [(i, i ^ bits) for i in range(size)])
-
-
-def ring(value, axis):
-    half = value.shape[0] // 2
-    below = shift(value, axis, 1)
-    above = shift(value, axis, -1)
-    first = shift(below[:half], axis, 1)
-    second = shift(above[half:], axis, -1)
-    return value, below, above, first, second
-
-
-def gather_cube(part, order):
-    for axis in order[:2]:
-        part = jnp.concatenate(ring(part, axis))
-    return ring(part, order[2])
 
 
 def mixer_kernel(recv, taps, skip, decay, residue, out, toep, prod, query):
@@ -129,92 +112,60 @@
     )(recv, taps, skip, decay, residue)
 
 
-def project_kernel(where, bucket, gated, ids, *refs):
-    pieces = [refs[5 * p : 5 * p + 5] for p in range(3)]
-    own, other, total, embed = refs[15:]
-    x, y, z, co = where[0], where[1], where[2], where[3]
-    total[...] = jnp.zeros_like(total)
-
-    def block(p, rel):
-        near, mid, far = rel
-        at = mid * 4 + near
-        if far < 3:
-            return pieces[p][far], 4 * at
-        return (pieces[p][3], 4 * at) if at < 8 else (pieces[p][4], 4 * (at - 8))
-
-    for yr in range(4):
-        for zr in range(4):
-            y_of = lax.rem(y + OFFSETS[yr], 4)
-            z_of = lax.rem(z + OFFSETS[zr], 4)
-            owner = (z_of // 2) * 4 + y_of
-            left, right = [], []
-            for xr in range(4):
-                chunk = lax.rem(z_of, 2) * 4 + lax.rem(x + OFFSETS[xr], 4)
-                rel = ((xr, yr, zr), (yr, zr, xr), (zr, xr, yr))
-                rows = []
-                for p in range(3):
-                    ref, at = block(p, rel[p])
-                    if p < 2:
-                        rows.append(ref[at : at + 4].reshape(192, 256))
-                    else:
-                        rows.append(ref[at : at + 4, 0:32].reshape(128, 256))
-                        for s in range(4):
-                            for h in range(2):
-                                at_row = pl.multiple_of(chunk * 32 + 16 * h, 16)
-                                embed[owner, pl.ds(at_row, 16), 128 * s : 128 * s + 128] = ref[
-                                    at + s, 32:48, 128 * h : 128 * h + 128
-                                ]
-                left.append(jnp.concatenate(rows, axis=0))
-                right.append(gated[chunk])
-            total[owner] += jnp.dot(
-                jnp.concatenate(left, axis=1),
-                jnp.concatenate(right, axis=0),
-                preferred_element_type=F32,
-            )
-
+def project_kernel(core, bucket, gated, ids, tiles, own, other):
+    owner = pl.program_id(0)
+    co = core[0]
+    left = jnp.concatenate(
+        [tiles[0, k // 4, 0, k % 4, :, 0:128].reshape(512, 256) for k in range(8)], axis=1
+    )
+    total = jnp.dot(left, gated[...], preferred_element_type=F32)
     lane = lax.broadcasted_iota(jnp.int32, (256, 256), 1)
     vocab = lane + (lane // 32) * 32 + co * 32
     hot = jnp.where(ids[...] == vocab, 1.0, 0.0).astype(BF16)
-    for owner in range(8):
-        looked = jnp.dot(hot, embed[owner], preferred_element_type=F32)
-        for s in range(4):
-            rows = jnp.concatenate(
-                [
-                    total[owner, 48 * s : 48 * s + 48],
-                    total[owner, 192 + 48 * s : 240 + 48 * s],
-                    total[owner, 384 + 32 * s : 416 + 32 * s],
-                ],
-                axis=0,
-            )
-            both = rows.T + looked[:, 128 * s : 128 * s + 128]
-            core = co if s < 2 else 1 - co
-            slot = 4 * owner + 2 * core + s % 2
-            cols = pl.ds(pl.multiple_of(bucket[slot] * 128, 128), 128)
-            own[:, cols] = jnp.where(co == 0, both[0:128], both[128:256])
-            other[:, cols] = jnp.where(co == 0, both[128:256], both[0:128]).astype(BF16)
-
-
-def project(where, bucket, gated, ids, pieces):
-    vmem = pl.BlockSpec(memory_space=pltpu.VMEM)
+    for s in range(4):
+        words = jnp.concatenate(
+            [
+                tiles[0, k // 4, 0, k % 4, s, 128:144, 128 * h : 128 * h + 128]
+                for k in range(8)
+                for h in range(2)
+            ],
+            axis=0,
+        )
+        looked = jnp.dot(hot, words, preferred_element_type=F32)
+        both = total[128 * s : 128 * s + 128].T + looked
+        slot = 4 * owner + 2 * (co if s < 2 else 1 - co) + s % 2
+        cols = pl.ds(pl.multiple_of(bucket[slot] * 128, 128), 128)
+        own[:, cols] = jnp.where(co == 0, both[0:128], both[128:256])
+        other[:, cols] = jnp.where(co == 0, both[128:256], both[0:128]).astype(BF16)
+
+
+def project(core, bucket, gated, ids, tiles):
     smem = pl.BlockSpec(memory_space=pltpu.SMEM)
+
+    def whole(shape):
+        return pl.BlockSpec(shape, lambda i: (0,) * len(shape))
+
     return pl.pallas_call(
         project_kernel,
+        grid=(8,),
         out_shape=(
             jax.ShapeDtypeStruct((128, D), F32),
             jax.ShapeDtypeStruct((128, D), BF16),
         ),
-        in_specs=[smem, smem] + [vmem] * (2 + len(pieces)),
-        out_specs=(vmem, vmem),
-        scratch_shapes=[
-            pltpu.VMEM((8, 512, 256), F32),
-            pltpu.VMEM((8, 256, 512), BF16),
+        in_specs=[
+            smem,
+            smem,
+            whole((2048, 256)),
+            whole((256, 1)),
+            pl.BlockSpec((1, 2, 1, 4, 4, 144, 256), lambda i: (i // 4, 0, i % 4, 0, 0, 0, 0)),
         ],
-        compiler_params=pltpu.CompilerParams(vmem_limit_bytes=48 << 20),
+        out_specs=(whole((128, D)), whole((128, D))),
+        compiler_params=pltpu.CompilerParams(vmem_limit_bytes=32 << 20),
         cost_estimate=pl.CostEstimate(
             flops=2 * 256 * 4096 * 2048, bytes_accessed=24 << 20, transcendentals=0
         ),
         name="project",
-    )(where, bucket, gated, ids, *pieces)
+    )(core, bucket, gated, ids, tiles)
 
 
 def body(
@@ -241,9 +192,8 @@
         return jnp.concatenate([rows, words], axis=1)
 
     tiles = jnp.concatenate([tile_for(co), flip(tile_for(1 - co), "co", 1, 2)])
-    pieces = []
-    for p, order in enumerate((("x", "y", ZAX), ("y", ZAX, "x"), (ZAX, "x", "y"))):
-        pieces += gather_cube(tiles[:, 48 * p : 48 * p + 48], order)
+    tiles = lax.all_gather(tiles, ("zh", "zl", "y", "x"), axis=0, tiled=True)
+    tiles = tiles.reshape(2, 2, 4, 4, 4, 144, 256)
 
     core_index = lax.broadcasted_iota(jnp.int32, (2, 8, 128), 0)
     ctx_index = lax.broadcasted_iota(jnp.int32, (2, 8, 128), 1)
@@ -290,10 +240,10 @@
     gated = mixer(packed, taps, skip, decay, weight)
     gated = lax.all_to_all(
         gated.reshape(64, 32, 256), ("zl", "x", "zh", "y"), split_axis=0, concat_axis=0, tiled=True
-    ).reshape(8, 256, 256)
-
-    where = jnp.stack([x, y, zh * 2 + zl, co]).astype(jnp.int32)
-    own, other = project(where, bucket_of_slot, gated, here, pieces)
+    ).reshape(2048, 256)
+
+    core = jnp.reshape(co, (1,)).astype(jnp.int32)
+    own, other = project(core, bucket_of_slot, gated, here, tiles)
     other = flip(other, "co", 1, 2)
     return (own + other.astype(F32)).astype(BF16)[None]
 

time: 241 us -> 160 us (0.66)
  starting transfers between devices: 80 us -> 22.4 us
  local copies, waits for them, and re-layouts: 38.4 us -> 4.76 us
  between operations: 0.47 us -> 13.7 us
  other arithmetic: 8.07 us -> 5.03 us
    ppermute x39 -> x3, waiting for transfers between devices: 53.7 us -> 3.1 us  [shift(): return lax.ppermute(value, axis, [(i, (i + step) % 4) for i in range(4)])]
    ppermute x39 -> x3, starting transfers between devices: 53.6 us -> 3.76 us  [shift(): return lax.ppermute(value, axis, [(i, (i + step) % 4) for i in range(4)])]
    all_gather x0 -> x1, waiting for transfers between devices: none -> 44.4 us  [body(): tiles = lax.all_gather(tiles, ('zh', 'zl', 'y', 'x'), axis=0, tiled=True)]
    all_to_all x1, waiting for transfers between devices: 0.01 us -> 22.1 us  [body(): lax.all_to_all(gated.reshape(64, 32, 256), ('zl', 'x', 'zh', 'y'), split_...]
    all_to_all x1, waiting for transfers between devices: 33.6 us -> 16.8 us  [body(): lax.all_to_all(packed, ('zh', 'y'), split_axis=0, concat_axis=0, tiled=True)]
    slice x18 -> x0, local copies, waits for them, and re-layouts: 14.1 us -> none  [the longest x9 7.63 us: ring(): first = shift(below[:half], axis, 1)]
    unnamed x45 -> x18, local copies, waits for them, and re-layouts: 13.7 us -> 0.66 us
    ppermute x6, starting transfers between devices: 15.9 us -> 6.24 us  [flip(): return lax.ppermute(value, axes, [(i, i ^ bits) for i in range(size)])]
  transfers between devices with their start and end apart: 47 -> 12, of which waited for: 8 -> 9; matrix products, arithmetic and copies ran while one was open for 18% -> 4% of each run, Pallas kernels for 4% -> 6%
where the time goes in v2:
time: 160 us; the launch traced here: 159 us
  waiting for transfers between devices  91.7 us (57%)
  starting transfers between devices  22.4 us (14%)
  Pallas kernels  21 us (13%)
  between operations  13.7 us (9%)
  other arithmetic  5.03 us (3%)
  local copies, waits for them, and re-layouts  4.76 us (3%)
    all_gather x1, waiting for transfers between devices, body(): tiles = lax.all_gather(tiles, ('zh', 'zl', 'y', 'x'), axis=0, tiled=True)  44.4 us
    all_to_all x1, waiting for transfers between devices, body(): lax.all_to_all(gated.reshape(64, 32, 256), ('zl', 'x', 'zh', 'y'), split_...  22.1 us
    all_to_all x1, waiting for transfers between devices, body(): lax.all_to_all(packed, ('zh', 'y'), split_axis=0, concat_axis=0, tiled=True)  16.8 us
    pallas_call x1, Pallas kernels, project(): pl.pallas_call(project_kernel, grid=(8,), out_shape=(jax.ShapeDtypeStruct...  11.9 us
    pallas_call x1, Pallas kernels, mixer(): pl.pallas_call(mixer_kernel, out_shape=jax.ShapeDtypeStruct((8, 8, 32, 25...  9.13 us
    all_to_all x1, starting transfers between devices, body(): lax.all_to_all(packed, ('zh', 'y'), split_axis=0, concat_axis=0, tiled=True)  7.74 us
    ppermute x6, starting transfers between devices, flip(): return lax.ppermute(value, axes, [(i, i ^ bits) for i in range(size)])  6.24 us
    ppermute x6, waiting for transfers between devices, flip(): return lax.ppermute(value, axes, [(i, i ^ bits) for i in range(size)])  5.33 us
  transfers between devices with their start and end apart: 12, of which 9 were waited for; matrix products, arithmetic and copies ran while one was open for 4% of the time, Pallas kernels for 6%

profile of v2, /device:TPU:1, one launch (start us, length us, event | category | flops | bytes accessed | tf_op | source)
XLA Modules:
  0.0 159.4 jit_solution(12790951897466234977)
XLA Ops:
  6.5 0.0 copy-start
  6.5 0.0 all-gather.2.cloned.1.call-start
  6.5 0.8 constant_dynamic-slice_fusion.2
  7.4 1.0 constant_dynamic-slice_fusion.3
  8.4 1.5 collective-permute-start.7
  9.9 1.0 collective-permute-done.7
  10.9 0.7 pad_maximum_fusion.1
  11.6 0.0 all-gather.2.cloned.1.call-update
  11.6 0.0 copy-start.1
  11.6 0.0 copy-start.6
  11.7 0.0 copy-start.2
  11.7 0.0 copy-done.3
  11.7 0.1 constant_dynamic-slice_fusion.9
  11.8 0.2 copy.40
  12.0 0.1 pad.10.clone
  12.1 0.2 copy-done.1
  12.3 0.1 compare_and_fusion
  12.4 0.0 copy-done.6
  12.4 0.6 gather_fusion
  13.0 0.0 copy-done.2
  13.0 0.0 copy-start.7
  13.0 0.1 fusion.3
  13.1 0.1 broadcast_select_fusion
  13.2 0.4 bitcast_convert_fusion
  13.6 0.2 maximum_maximum_fusion
  13.9 0.4 collective-permute-start
  14.3 0.0 copy-done.7
  14.3 0.1 and_select_fusion
  14.4 2.6 %collective-permute-start.2 = (s32[2,8,128]{2,0,1:T(2,128)S(1)}, s32[2,8,128]{2,0,1:T(2,128)S(1)}, u32[]{:S(2)}, u32[]{:S(2)}) collective-permute-start(s32[2,8,128]{2,0,1:T(2,128)S(1)} %and_select_fusion), channel_id=1, source_target_pairs={{0,3},{1,0},{2,1},{3,2},{4,7},{5,4},{6,5},{7,6},{8,11},{9,8},{10,9... | collective-permute-start | bytes 24584 | tf_op jit(solution)/shard_map/ppermute | solution.py:19
  17.0 0.5 collective-permute-start.3
  17.6 0.6 collective-permute-start.1
  18.2 0.0 collective-permute-done.2
  18.2 2.9 %collective-permute-done.3 = s32[2,8,128]{2,0,1:T(2,128)S(1)} collective-permute-done((s32[2,8,128]{2,0,1:T(2,128)S(1)}, s32[2,8,128]{2,0,1:T(2,128)S(1)}, u32[]{:S(2)}, u32[]{:S(2)}) %collective-permute-start.3) | collective-permute-done | bytes 8224 | tf_op jit(solution)/shard_map/ppermute | solution.py:19
  21.0 0.2 collective-permute-done.1
  21.3 0.1 add_add_fusion.1
  21.4 3.5 %collective-permute-start.6 = (s32[2,8,128]{2,0,1:T(2,128)S(1)}, s32[2,8,128]{2,0,1:T(2,128)S(1)}, u32[]{:S(2)}, u32[]{:S(2)}) collective-permute-start(s32[2,8,128]{2,0,1:T(2,128)S(1)} %add_add_fusion.1), channel_id=1, source_target_pairs={{0,12},{4,8},{8,4},{12,0},{1,13},{5,9},{9,5},{13,1},{2,14},{6,10},... | collective-permute-start | bytes 24584 | tf_op jit(solution)/shard_map/ppermute | solution.py:23
  24.8 0.0 collective-permute-start.5
  24.8 0.2 collective-permute-start.4
  25.0 0.2 copy.39
  25.3 0.9 collective-permute-done.6
  26.2 0.0 collective-permute-done.5
  26.2 1.2 collective-permute-done.4
  27.4 0.0 collective-permute-done
  27.4 1.3 convert_element_type.27
  28.8 0.1 concatenate.23
  28.8 0.4 fusion
  29.3 1.0 pad_maximum_fusion
  30.3 7.7 %all-to-all-start = ((bf16[8,112,512]{2,1,0:T(8,128)(2,1)}), bf16[8,112,512]{2,1,0:T(8,128)(2,1)S(1)}, u32[]{:S(2)}, u32[]{:S(2)}) async-start(bf16[8,112,512]{2,1,0:T(8,128)(2,1)} %pad_maximum_fusion), calls=%async_computation | async-start | bytes 1835008 | tf_op jit(solution)/shard_map/all_to_all | solution.py:232
  38.0 0.8 dynamic_slice.41
  38.8 0.1 broadcast_in_dim.59
  38.9 0.1 constant_dynamic-slice_fusion.7
  38.9 0.2 reshape.122.taps
  39.1 0.2 reshape.123.skip
  39.3 0.1 constant_dynamic-slice_fusion.5
  39.4 16.8 %all-to-all-done.recv = bf16[8,112,512]{2,1,0:T(8,128)(2,1)S(1)} async-done(((bf16[8,112,512]{2,1,0:T(8,128)(2,1)}), bf16[8,112,512]{2,1,0:T(8,128)(2,1)S(1)}, u32[]{:S(2)}, u32[]{:S(2)}) %all-to-all-start) | async-done | bytes 917536 | tf_op jit(solution)/shard_map/all_to_all | solution.py:232
  56.1 9.1 %mixer.1 = bf16[8,8,32,256]{3,2,1,0:T(8,128)(2,1)} custom-call(bf16[8,112,512]{2,1,0:T(8,128)(2,1)S(1)} %all-to-all-done.recv, f32[3,96,1]{2,1,0:T(8,128)S(1)} %reshape.122.taps, f32[2,256,1]{2,1,0:T(8,128)S(1)} %reshape.123.skip, f32[16,2]{1,0:T(8,128)S(1)} %get-tuple-element.24.decay, f32[16,2]{1,0:T(8,128)S(1)} %get-tuple-element.23.residue), custom_call_target="tpu_custom_call" | custom-call | flops 1610612736 | bytes 4194304 | tf_op jit(solution)/shard_map/mixer/pallas_call | solution.py:97
  65.3 4.7 %all-to-all-start.1 = ((bf16[64,32,256]{2,1,0:T(8,128)(2,1)}), bf16[64,32,256]{2,1,0:T(8,128)(2,1)S(1)}, u32[]{:S(2)}, u32[]{:S(2)}) async-start(bf16[64,32,256]{2,1,0:T(8,128)(2,1)} %bitcast.13), calls=%async_computation.1 | async-start | bytes 2097152 | tf_op jit(solution)/shard_map/all_to_all | solution.py:241
  70.0 0.1 copy.38.ids
  70.1 22.1 %all-to-all-done.1 = bf16[64,32,256]{2,1,0:T(8,128)(2,1)S(1)} async-done(((bf16[64,32,256]{2,1,0:T(8,128)(2,1)}), bf16[64,32,256]{2,1,0:T(8,128)(2,1)S(1)}, u32[]{:S(2)}, u32[]{:S(2)}) %all-to-all-start.1) | async-done | bytes 1048608 | tf_op jit(solution)/shard_map/all_to_all | solution.py:241
  92.2 44.4 %all-gather.2.cloned.1.call-done = bf16[256,144,256]{2,1,0:T(8,128)(2,1)} async-done(((bf16[4,144,256]{2,1,0:T(8,128)(2,1)}), bf16[256,144,256]{2,1,0:T(8,128)(2,1)}) %all-gather.2.cloned.1.call-update) | async-done | bytes 18874384 | tf_op jit(solution)/shard_map/all_gather | solution.py:195
  136.6 11.9 %project.1 = (f32[128,4096]{1,0:T(8,128)S(1)}, bf16[128,4096]{1,0:T(8,128)(2,1)S(1)}) custom-call(s32[1]{0:T(128)} %bitcast.core, s32[32]{0:T(128)S(1)} %copy-done.1, bf16[2048,256]{1,0:T(8,128)(2,1)S(1)} %bitcast.44, s32[256,1]{1,0:T(8,128)S(1)} %copy.38.ids, bf16[2,2,4,4,4,144,256]{6,5,4,3,2,1,0:T(8,128)(2,1)} %bitcast.45), custom_call_target="tpu_custom_call" | custom-call | flops 4294967296 | bytes 25165824 | tf_op jit(solution)/shard_map/project/pallas_call | solution.py:148
  148.5 0.6 collective-permute-start.8
  149.1 2.3 %collective-permute-done.8 = bf16[128,4096]{1,0:T(8,128)(2,1)S(1)} collective-permute-done((bf16[128,4096]{1,0:T(8,128)(2,1)S(1)}, bf16[128,4096]{1,0:T(8,128)(2,1)S(1)}, u32[]{:S(2)}, u32[]{:S(2)}) %collective-permute-start.8) | collective-permute-done | bytes 1048608 | tf_op jit(solution)/shard_map/ppermute | solution.py:23
  151.4 1.2 fusion.1
  (26 shorter events, 0.2 us)
Async XLA Ops:
  6.5 32.3 %copy-start = (f32[3,3,512]{2,1,0:T(4,128)S(1)}, f32[3,3,512]{2,1,0:T(4,128)}, u32[]{:S(2)}) copy-start(f32[3,3,512]{2,1,0:T(4,128)} %param.15) | copy-start | bytes 55300
  6.5 5.1 %copy-start.3 = (bf16[2,128,3,512]{3,1,2,0:T(8,128)(2,1)S(1)}, bf16[2,128,3,512]{3,1,2,0:T(8,128)(2,1)}, u32[]{:S(2)}) copy-start(bf16[2,128,3,512]{3,1,2,0:T(8,128)(2,1)} %param.14) | copy-start | bytes 2359300
  6.5 130.0 %all-gather.2.cloned.1.call-start = ((), (), s32[]{:S(2)}) async-start(), calls=%async_computation.2 | async-start | bytes 19169280 | tf_op jit(solution)/shard_map/all_gather | solution.py:195
  8.4 2.5 %collective-permute-start.7 = (bf16[2,144,256]{2,1,0:T(8,128)(2,1)S(1)}, bf16[2,144,256]{2,1,0:T(8,128)(2,1)S(1)}, u32[]{:S(2)}, u32[]{:S(2)}) collective-permute-start(bf16[2,144,256]{2,1,0:T(8,128)(2,1)S(1)} %pad_maximum_fusion.2), channel_id=1, source_target_pairs={{0,8},{8,0},{1,9},{9,1},{2,10},{10,2},{3,11},{11,3},{4,12},{12,4},... | collective-permute-start | bytes 442376 | tf_op jit(solution)/shard_map/ppermute | solution.py:23
  11.6 0.7 copy-start.1
  11.6 0.7 copy-start.6
  11.7 1.3 copy-start.2
  13.0 1.4 copy-start.7
  13.9 13.5 %collective-permute-start = (bf16[784,512]{1,0:T(8,128)(2,1)S(1)}, bf16[784,512]{1,0:T(8,128)(2,1)}, u32[]{:S(2)}, u32[]{:S(2)}) collective-permute-start(bf16[784,512]{1,0:T(8,128)(2,1)S(1)} %maximum_maximum_fusion), channel_id=1, source_target_pairs={{0,8},{8,0},{1,9},{9,1},{2,10},{10,2},{3,11},{11,3},{4,12},{12,4},... | collective-permute-start | bytes 2408456 | tf_op jit(solution)/shard_map/ppermute | solution.py:23
  14.4 3.8 %collective-permute-start.2 = (s32[2,8,128]{2,0,1:T(2,128)S(1)}, s32[2,8,128]{2,0,1:T(2,128)S(1)}, u32[]{:S(2)}, u32[]{:S(2)}) collective-permute-start(s32[2,8,128]{2,0,1:T(2,128)S(1)} %and_select_fusion), channel_id=1, source_target_pairs={{0,3},{1,0},{2,1},{3,2},{4,7},{5,4},{6,5},{7,6},{8,11},{9,8},{10,9... | collective-permute-start | bytes 24584 | tf_op jit(solution)/shard_map/ppermute | solution.py:19
  17.0 4.0 %collective-permute-start.3 = (s32[2,8,128]{2,0,1:T(2,128)S(1)}, s32[2,8,128]{2,0,1:T(2,128)S(1)}, u32[]{:S(2)}, u32[]{:S(2)}) collective-permute-start(s32[2,8,128]{2,0,1:T(2,128)S(1)} %and_select_fusion), channel_id=1, source_target_pairs={{0,2},{1,3},{2,0},{3,1},{4,6},{5,7},{6,4},{7,5},{8,10},{9,11},{10,... | collective-permute-start | bytes 24584 | tf_op jit(solution)/shard_map/ppermute | solution.py:19
  17.6 3.7 %collective-permute-start.1 = (s32[2,8,128]{2,0,1:T(2,128)S(1)}, s32[2,8,128]{2,0,1:T(2,128)S(1)}, u32[]{:S(2)}, u32[]{:S(2)}) collective-permute-start(s32[2,8,128]{2,0,1:T(2,128)S(1)} %and_select_fusion), channel_id=1, source_target_pairs={{0,1},{1,2},{2,3},{3,0},{4,5},{5,6},{6,7},{7,4},{8,9},{9,10},{10,1... | collective-permute-start | bytes 24584 | tf_op jit(solution)/shard_map/ppermute | solution.py:19
  21.4 4.8 %collective-permute-start.6 = (s32[2,8,128]{2,0,1:T(2,128)S(1)}, s32[2,8,128]{2,0,1:T(2,128)S(1)}, u32[]{:S(2)}, u32[]{:S(2)}) collective-permute-start(s32[2,8,128]{2,0,1:T(2,128)S(1)} %add_add_fusion.1), channel_id=1, source_target_pairs={{0,12},{4,8},{8,4},{12,0},{1,13},{5,9},{9,5},{13,1},{2,14},{6,10},... | collective-permute-start | bytes 24584 | tf_op jit(solution)/shard_map/ppermute | solution.py:23
  24.8 1.3 collective-permute-start.5
  24.8 2.5 %collective-permute-start.4 = (s32[2,8,128]{2,0,1:T(2,128)S(1)}, s32[2,8,128]{2,0,1:T(2,128)S(1)}, u32[]{:S(2)}, u32[]{:S(2)}) collective-permute-start(s32[2,8,128]{2,0,1:T(2,128)S(1)} %add_add_fusion.1), channel_id=1, source_target_pairs={{0,4},{4,0},{8,12},{12,8},{1,5},{5,1},{9,13},{13,9},{2,6},{6,2},{1... | collective-permute-start | bytes 24584 | tf_op jit(solution)/shard_map/ppermute | solution.py:23
  30.3 9.0 %copy-start.4 = (f32[16,32]{1,0:T(8,128)S(1)}, f32[16,32]{1,0:T(8,128)}, u32[]{:S(2)}) copy-start(f32[16,32]{1,0:T(8,128)} %param.17) | copy-start | bytes 6148
  30.3 9.0 %copy-start.5 = (f32[16,32]{1,0:T(8,128)S(1)}, f32[16,32]{1,0:T(8,128)}, u32[]{:S(2)}) copy-start(f32[16,32]{1,0:T(8,128)} %param.16) | copy-start | bytes 6148
  30.3 25.9 %all-to-all-start = ((bf16[8,112,512]{2,1,0:T(8,128)(2,1)}), bf16[8,112,512]{2,1,0:T(8,128)(2,1)S(1)}, u32[]{:S(2)}, u32[]{:S(2)}) async-start(bf16[8,112,512]{2,1,0:T(8,128)(2,1)} %pad_maximum_fusion), calls=%async_computation | async-start | bytes 1835008 | tf_op jit(solution)/shard_map/all_to_all | solution.py:232
  65.3 26.9 %all-to-all-start.1 = ((bf16[64,32,256]{2,1,0:T(8,128)(2,1)}), bf16[64,32,256]{2,1,0:T(8,128)(2,1)S(1)}, u32[]{:S(2)}, u32[]{:S(2)}) async-start(bf16[64,32,256]{2,1,0:T(8,128)(2,1)} %bitcast.13), calls=%async_computation.1 | async-start | bytes 2097152 | tf_op jit(solution)/shard_map/all_to_all | solution.py:241
  148.5 2.9 %collective-permute-start.8 = (bf16[128,4096]{1,0:T(8,128)(2,1)S(1)}, bf16[128,4096]{1,0:T(8,128)(2,1)S(1)}, u32[]{:S(2)}, u32[]{:S(2)}) collective-permute-start(bf16[128,4096]{1,0:T(8,128)(2,1)S(1)} %get-tuple-element.8), channel_id=1, source_target_pairs={{0,8},{8,0},{1,9},{9,1},{2,10},{10,2},{3,11},{11,3},{4,12},{12,4},... | collective-permute-start | bytes 3145736 | tf_op jit(solution)/shard_map/ppermute | solution.py:23
Sparse Core Ops, SparseCore 0:
  11.8 124.7 all-gather.1

commit v3 on v2

v3 whole, which is shorter than its diff:
```python
import functools

import jax
import jax.numpy as jnp
from jax import lax
from jax.experimental import pallas as pl
from jax.experimental.pallas import tpu as pltpu
from jax.sharding import Mesh
from jax.sharding import PartitionSpec as P

F32 = jnp.float32
BF16 = jnp.bfloat16
D = 4096
SEQ = 1024
EPS = 1e-06
OFFSETS = (0, 3, 1, 2)
DP = ("zh", "y", "co")
CTX = ("zl", "x")


def shift(value, axis, step):
    return lax.ppermute(value, axis, [(i, (i + step) % 4) for i in range(4)])


def flip(value, axes, bits, size):
    return lax.ppermute(value, axes, [(i, i ^ bits) for i in range(size)])


def rings(values, axes, after=()):
    near = []
    for value, axis in zip(values, axes):
        near += [shift(value, axis, 1), shift(value, axis, -1)]
    near = lax.optimization_barrier((*near, *after))[:4]
    far = []
    for i, axis in enumerate(axes):
        half = values[i].shape[0] // 2
        far += [shift(near[2 * i][:half], axis, 1), shift(near[2 * i + 1][half:], axis, -1)]
    far = lax.optimization_barrier(tuple(far))
    return [(values[i], *near[2 * i : 2 * i + 2], *far[2 * i : 2 * i + 2]) for i in range(2)]


def filter_kernel(decay, residue, toep):
    for g in range(2):
        time = lax.broadcasted_iota(jnp.int32, (16, SEQ), 1).astype(F32)
        terms = jnp.exp(-decay[:, g : g + 1] * time) * residue[:, g : g + 1]
        filt = jnp.sum(terms, axis=0, keepdims=True).astype(BF16).astype(F32)
        filt = jnp.concatenate([filt, jnp.zeros((1, 128), F32)], axis=1)
        lagged = pltpu.roll(
            jnp.broadcast_to(filt, (128, SEQ + 128)), 0, 1, stride=1, stride_axis=0
        ).astype(BF16)
        for k in range(4):
            toep[g, k, 0:128, :] = lagged[:, 256 * k : 256 * k + 256]
            if k == 0:
                toep[g, k, 128:256, 0:128] = jnp.zeros((128, 128), BF16)
                toep[g, k, 128:256, 128:256] = lagged[:, 0:128]
            else:
                toep[g, k, 128:256, :] = lagged[:, 256 * k - 128 : 256 * k + 128]


def filters(decay, residue):
    vmem = pl.BlockSpec(memory_space=pltpu.VMEM)
    return pl.pallas_call(
        filter_kernel,
        out_shape=jax.ShapeDtypeStruct((2, 4, 256, 256), BF16),
        in_specs=[vmem] * 2,
        out_specs=vmem,
        name="filters",
    )(decay, residue)


def mixer_kernel(recv, taps, skip, toep, out, prod, query):
    table = recv[0, 0:96, :].astype(F32)
    extra = recv[0, 96:112, :].astype(F32)
    square = extra[8:9] + extra[9:10]
    for i in range(1, 8):
        table = table + recv[i, 0:96, :].astype(F32)
        extra = recv[i, 96:112, :].astype(F32)
        square = square + extra[8:9] + extra[9:10]
    table = (table * lax.rsqrt(square / D + EPS)).astype(BF16)

    vocab = lax.broadcasted_iota(jnp.int32, (512, 512), 0).astype(F32)
    lane = lax.broadcasted_iota(jnp.int32, (96, SEQ), 1)

    def one_pair(i, carry):
        extra = recv[i, 96:112, :].astype(F32)
        for j in range(2):
            parts = []
            for a in range(2):
                r = 2 * j + a
                ids = extra[r : r + 1] * 256.0 + extra[4 + r : 5 + r]
                hot = jnp.where(vocab == ids, 1.0, 0.0).astype(BF16)
                parts.append(jnp.dot(table, hot, preferred_element_type=F32))
            z0 = jnp.concatenate(parts, axis=1)
            z1 = jnp.where(lane >= 1, pltpu.roll(z0, 1, 1), 0.0)
            z2 = jnp.where(lane >= 2, pltpu.roll(z0, 2, 1), 0.0)
            f = taps[0] * z0 + taps[1] * z1 + taps[2] * z2
            u = (f[32:64] * f[64:96]).astype(BF16)
            rows = pl.ds(pl.multiple_of((2 * i + j) * 16, 16), 16)
            for g in range(2):
                for b in range(4):
                    cols = slice(256 * b, 256 * b + 256)
                    prod[g, b, rows, :] = u[16 * g : 16 * g + 16, cols]
                    query[g, b, rows, :] = f[16 * g : 16 * g + 16, cols]
        return carry

    lax.fori_loop(0, 8, one_pair, 0)

    for g in range(2):
        for b in range(4):
            mixed = skip[g] * prod[g, b].astype(F32)
            for a in range(b + 1):
                mixed = mixed + jnp.dot(prod[g, a], toep[g, b - a], preferred_element_type=F32)
            gated = (query[g, b] * mixed).astype(BF16)
            for n in range(16):
                for h in range(2):
                    c = 2 * b + h
                    lanes = 256 * (n % 2) + 128 * (c // 4)
                    out[c % 4, n // 2, 16 * g : 16 * g + 16, lanes : lanes + 128] = gated[
                        16 * n : 16 * n + 16, 128 * h : 128 * h + 128
                    ]


def mixer(recv, taps, skip, toep):
    vmem = pl.BlockSpec(memory_space=pltpu.VMEM)
    return pl.pallas_call(
        mixer_kernel,
        out_shape=jax.ShapeDtypeStruct((4, 8, 32, 512), BF16),
        in_specs=[vmem] * 4,
        out_specs=vmem,
        scratch_shapes=[
            pltpu.VMEM((2, 4, 256, 256), BF16),
            pltpu.VMEM((2, 4, 256, 256), F32),
        ],
        compiler_params=pltpu.CompilerParams(vmem_limit_bytes=32 << 20),
        cost_estimate=pl.CostEstimate(
            flops=2 * 16 * 96 * 512 * 1024, bytes_accessed=4 << 20, transcendentals=0
        ),
        name="mixer",
    )(recv, taps, skip, toep)


def project_kernel(far_axis, where, gated, ids, *refs):
    pieces = refs[:5]
    mine, theirs, right, hot = refs[5:]
    x, y, zl, co = where[0], where[1], where[3], where[4]

    for r in range(4):
        x_of = lax.rem(x + OFFSETS[r], 4)
        right[256 * r : 256 * r + 256, :] = gated[x_of]
        word = lax.broadcasted_iota(jnp.int32, (32, 512), 0) + ((zl * 4 + x_of) * 2 + co) * 32
        hot[32 * r : 32 * r + 32, :] = jnp.where(word == ids[...], 1.0, 0.0).astype(BF16)

    def block(xr, yr, s):
        near, far = (xr, yr) if far_axis == "y" else (yr, xr)
        at = 4 * near + s
        if far < 3:
            return pieces[far].at[at]
        return pieces[3].at[at] if at < 8 else pieces[4].at[at - 8]

    for yr in range(4):
        y_of = lax.rem(y + OFFSETS[yr], 4)
        for s in range(4):
            tiles = [block(xr, yr, s) for xr in range(4)]
            rows = jnp.concatenate([t[0:128, :] for t in tiles], axis=1)
            words = jnp.concatenate(
                [t[128:144, 128 * h : 128 * h + 128] for t in tiles for h in range(2)], axis=0
            )
            total = jnp.dot(rows, right[...], preferred_element_type=F32)
            total = total + lax.dot_general(
                words, hot[...], (((0,), (0,)), ((), ())), preferred_element_type=F32
            )
            cols = slice(128 * s, 128 * s + 128)
            mine[y_of, cols, :] = jnp.where(co == 0, total[:, 0:256], total[:, 256:512])
            theirs[y_of, cols, :] = jnp.where(
                co == 0, total[:, 256:512], total[:, 0:256]
            ).astype(BF16)


def project(far_axis, where, gated, ids, pieces):
    vmem = pl.BlockSpec(memory_space=pltpu.VMEM)
    smem = pl.BlockSpec(memory_space=pltpu.SMEM)
    return pl.pallas_call(
        functools.partial(project_kernel, far_axis),
        out_shape=(
            jax.ShapeDtypeStruct((4, 512, 256), F32),
            jax.ShapeDtypeStruct((4, 512, 256), BF16),
        ),
        in_specs=[smem] + [vmem] * 7,
        out_specs=(vmem, vmem),
        scratch_shapes=[pltpu.VMEM((1024, 512), BF16), pltpu.VMEM((128, 512), BF16)],
        compiler_params=pltpu.CompilerParams(vmem_limit_bytes=32 << 20),
        cost_estimate=pl.CostEstimate(
            flops=2 * 512 * 2048 * 1024, bytes_accessed=10 << 20, transcendentals=0
        ),
        name="project_" + far_axis,
    )(where, gated, ids, *pieces)


def merge_kernel(where, mine, theirs, keep, give):
    zl = where[3]
    for y in range(4):
        total = mine[y] + theirs[y].astype(F32)
        low, high = total[:, 0:128], total[:, 128:256]
        keep[y] = jnp.where(zl == 0, low, high)
        give[y] = jnp.where(zl == 0, high, low).astype(BF16)


def merge(where, mine, theirs):
    vmem = pl.BlockSpec(memory_space=pltpu.VMEM)
    smem = pl.BlockSpec(memory_space=pltpu.SMEM)
    return pl.pallas_call(
        merge_kernel,
        out_shape=(
            jax.ShapeDtypeStruct((4, 512, 128), F32),
            jax.ShapeDtypeStruct((4, 512, 128), BF16),
        ),
        in_specs=[smem, vmem, vmem],
        out_specs=(vmem, vmem),
        compiler_params=pltpu.CompilerParams(vmem_limit_bytes=16 << 20),
        name="merge",
    )(where, mine, theirs)


def finish_kernel(where, bucket, keep0, keep1, got0, got1, out):
    zh = where[2]
    for p, (keep, got) in enumerate(((keep0, got0), (keep1, got1))):
        for y in range(4):
            for s in range(4):
                rows = slice(128 * s, 128 * s + 128)
                total = keep[y, rows, :] + got[y, rows, :].astype(F32)
                slot = 16 * lax.rem(zh + p, 2) + 4 * y + s
                cols = pl.ds(pl.multiple_of(bucket[slot] * 128, 128), 128)
                out[:, cols] = total.T.astype(BF16)


def finish(where, bucket, keep, got):
    vmem = pl.BlockSpec(memory_space=pltpu.VMEM)
    smem = pl.BlockSpec(memory_space=pltpu.SMEM)
    return pl.pallas_call(
        finish_kernel,
        out_shape=jax.ShapeDtypeStruct((128, D), BF16),
        in_specs=[smem, smem] + [vmem] * 4,
        out_specs=vmem,
        compiler_params=pltpu.CompilerParams(vmem_limit_bytes=24 << 20),
        name="finish",
    )(where, bucket, *keep, *got)


def body(
    token_ids,
    bucket_of_slot,
    embed_tiles,
    norm_gain,
    in_tiles,
    short_taps,
    decay_rate,
    residue,
    skip_gain,
    out_tiles,
):
    zh, y, co, zl, x = (lax.axis_index(a) for a in ("zh", "y", "co", "zl", "x"))
    zy = zh * 4 + y
    c = zl * 4 + x
    d = zy * 2 + co

    core_index = lax.broadcasted_iota(jnp.int32, (2, 8, 128), 0)
    ctx_index = lax.broadcasted_iota(jnp.int32, (2, 8, 128), 1)
    ids = jnp.where((core_index == co) & (ctx_index == c), token_ids[None], 0)
    ids = ids + shift(ids, "x", 1) + shift(ids, "x", -1) + shift(ids, "x", 2)
    ids, in_tiles = lax.optimization_barrier((ids, in_tiles))
    ids = ids + sum(flip(ids, ("co", "zl"), b, 4) for b in (1, 2, 3))
    here = lax.dynamic_index_in_dim(ids.reshape(2, 2, 4, 128), x, 2, keepdims=False)
    here = here.reshape(1, 512)
    ids = ids.reshape(4, 512)
    ids_rows = jnp.concatenate([ids // 256, ids % 256]).astype(BF16)

    def tile_for(core):
        rows = lax.dynamic_slice_in_dim(out_tiles, core * 256, 256, axis=2)
        words = lax.dynamic_slice_in_dim(embed_tiles, (c * 2 + core) * 32, 32, axis=1)
        words = words.reshape(2, 2, 16, 128).transpose(0, 2, 1, 3).reshape(2, 16, 256)
        return jnp.concatenate([rows, words], axis=1)

    ours, sent = tile_for(co), flip(tile_for(1 - co), "co", 1, 2)
    tiles = jnp.concatenate([jnp.where(co == 0, ours, sent), jnp.where(co == 0, sent, ours)])
    across = flip(tiles, "zh", 1, 2)

    buckets = lax.dynamic_slice_in_dim(bucket_of_slot, 2 * d, 2)
    gain = jnp.take(norm_gain.reshape(32, 128), buckets, axis=0)
    embed_f32 = embed_tiles.astype(F32)
    scaled = (embed_f32 * gain[:, None, :]).astype(BF16)
    square = jnp.sum(embed_f32 * embed_f32, axis=(0, 2))
    high = lax.reduce_precision(square, 8, 7)
    square_rows = jnp.stack([high, square - high]).astype(BF16)

    def partial_for(core):
        weights = lax.dynamic_slice_in_dim(in_tiles, core * 256, 256, axis=3).reshape(2, 128, 768)
        return lax.dot_general(
            weights, scaled, (((0, 1), (0, 2)), ((), ())), preferred_element_type=F32
        )

    given = jnp.concatenate(
        [partial_for(1 - co).astype(BF16), square_rows, jnp.zeros((14, 512), BF16)]
    )
    taken = flip(given, "co", 1, 2).astype(F32)
    table = (partial_for(co) + taken[:768]).astype(BF16).reshape(3, 8, 32, 512)
    square = square + taken[768] + taken[769]
    high = lax.reduce_precision(square, 8, 7)
    square_rows = jnp.stack([high, square - high]).astype(BF16)
    extra = jnp.concatenate([ids_rows, square_rows, jnp.zeros((6, 512), BF16)])
    packed = jnp.concatenate(
        [table[0], table[1], table[2], jnp.broadcast_to(extra[None], (8, 16, 512))], axis=1
    )
    parts = rings((tiles, across), ("x", "y"), (packed,))
    parts = [jnp.concatenate(blocks) for blocks in parts]
    pieces = rings(parts, ("y", "x"))

    packed = lax.all_to_all(packed, ("zh", "y"), split_axis=0, concat_axis=0, tiled=True)

    first = co * 256 + zy * 32
    taps = lax.dynamic_slice_in_dim(short_taps, first, 32, axis=2).reshape(3, 96, 1)
    skip = lax.dynamic_slice_in_dim(skip_gain, first, 32).reshape(2, 1, 16)
    skip = jnp.broadcast_to(skip, (2, 16, 16)).reshape(2, 256, 1)
    decay = lax.dynamic_slice_in_dim(decay_rate, co * 16 + zy * 2, 2, axis=1)
    weight = lax.dynamic_slice_in_dim(residue, co * 16 + zy * 2, 2, axis=1)
    gated = mixer(packed, taps, skip, filters(decay, weight))
    gated = lax.all_to_all(
        gated.reshape(32, 32, 512), ("x", "zh", "y"), split_axis=0, concat_axis=0, tiled=True
    ).reshape(4, 256, 512)

    where = jnp.stack([x, y, zh, zl, co]).astype(jnp.int32)
    keep, got = [], []
    for p, far in enumerate(("y", "x")):
        mine, theirs = project(far, where, gated, here, pieces[p])
        kept, given = merge(where, mine, flip(theirs, "co", 1, 2))
        keep.append(kept)
        got.append(flip(given, "zl", 1, 2))
    return finish(where, bucket_of_slot, keep, got)[None]


def solution(mesh):
    mesh = Mesh(mesh.devices.reshape(2, 4, 2, 2, 4), ("zh", "y", "co", "zl", "x"))
    in_specs = (
        P(DP, CTX),
        P(),
        P(DP, None, None),
        P(),
        P(DP, None, None, CTX),
        P(None, None, CTX),
        P(None, CTX),
        P(None, CTX),
        P(CTX),
        P(DP, None, CTX),
    )
    out_specs = P(DP, CTX, None)
    return jax.shard_map(body, mesh=mesh, in_specs=in_specs, out_specs=out_specs, check_vma=False)
```

time: 160 us -> 156 us (0.975)
  waiting for transfers between devices: 91.7 us -> 47.9 us
  starting transfers between devices: 22.4 us -> 48.3 us
  local copies, waits for them, and re-layouts: 4.76 us -> 29 us
  between operations: 13.7 us -> 0.37 us
  Pallas kernels: 21 us -> 23.8 us
    all_gather x1 -> x0, waiting for transfers between devices: 44.4 us -> none  [body(): tiles = lax.all_gather(tiles, ('zh', 'zl', 'y', 'x'), axis=0, tiled=True)]
    ppermute x6 -> x10, waiting for transfers between devices: 5.33 us -> 28.1 us  [flip(): return lax.ppermute(value, axes, [(i, i ^ bits) for i in range(size)])]
    all_to_all x1, waiting for transfers between devices: 22.1 us -> 0.01 us  [body(): lax.all_to_all(gated.reshape(32, 32, 512), ('x', 'zh', 'y'), split_axis=0...]
    all_to_all x1, waiting for transfers between devices: 16.8 us -> 0.01 us  [body(): lax.all_to_all(packed, ('zh', 'y'), split_axis=0, concat_axis=0, tiled=True)]
    ppermute x3 -> x19, waiting for transfers between devices: 3.1 us -> 19.8 us  [shift(): return lax.ppermute(value, axis, [(i, (i + step) % 4) for i in range(4)])]
    ppermute x3 -> x19, starting transfers between devices: 3.76 us -> 20.3 us  [shift(): return lax.ppermute(value, axis, [(i, (i + step) % 4) for i in range(4)])]
    unnamed x18 -> x32, local copies, waits for them, and re-layouts: 0.66 us -> 12 us
    slice x0 -> x9, local copies, waits for them, and re-layouts: none -> 9.36 us  [the longest x4 4.67 us: rings(): near[2 * i + 1][half:]]
  transfers between devices with their start and end apart: 12 -> 31, of which waited for: 9 -> 12; matrix products, arithmetic and copies ran while one was open for 4% -> 19% of each run, Pallas kernels for 6% -> 11%
where the time goes in v3:
time: 156 us; the launch traced here: 155 us
  starting transfers between devices  48.3 us (31%)
  waiting for transfers between devices  47.9 us (31%)
  local copies, waits for them, and re-layouts  29 us (19%)
  Pallas kernels  23.8 us (15%)
  other arithmetic  4.69 us (3%)
    ppermute x10, waiting for transfers between devices, flip(): return lax.ppermute(value, axes, [(i, i ^ bits) for i in range(size)])  28.1 us
    ppermute x19, starting transfers between devices, shift(): return lax.ppermute(value, axis, [(i, (i + step) % 4) for i in range(4)])  20.3 us
    ppermute x19, waiting for transfers between devices, shift(): return lax.ppermute(value, axis, [(i, (i + step) % 4) for i in range(4)])  19.8 us
    ppermute x10, starting transfers between devices, flip(): return lax.ppermute(value, axes, [(i, i ^ bits) for i in range(size)])  14.5 us
    unnamed x32, local copies, waits for them, and re-layouts  12 us
    pallas_call x2, Pallas kernels, project(): pl.pallas_call(functools.partial(project_kernel, far_axis), out_shape=(ja...  9.4 us
    pallas_call x1, Pallas kernels, mixer(): pl.pallas_call(mixer_kernel, out_shape=jax.ShapeDtypeStruct((4, 8, 32, 51...  8.75 us
    all_to_all x1, starting transfers between devices, body(): lax.all_to_all(gated.reshape(32, 32, 512), ('x', 'zh', 'y'), split_axis=0...  7.18 us
  transfers between devices with their start and end apart: 31, of which 12 were waited for; matrix products, arithmetic and copies ran while one was open for 19% of the time, Pallas kernels for 11%

profile of v3, /device:TPU:1, one launch (start us, length us, event | category | flops | bytes accessed | tf_op | source)
XLA Modules:
  0.0 154.9 jit_solution(7597685028823979665)
XLA Ops:
  0.1 0.8 and_select_fusion
  0.9 3.3 %collective-permute-start.1 = (s32[2,8,128]{2,1,0:T(8,128)S(1)}, s32[2,8,128]{2,1,0:T(8,128)S(1)}, u32[]{:S(2)}, u32[]{:S(2)}) collective-permute-start(s32[2,8,128]{2,1,0:T(8,128)S(1)} %and_select_fusion), channel_id=1, source_target_pairs={{0,3},{1,0},{2,1},{3,2},{4,7},{5,4},{6,5},{7,6},{8,11},{9,8},{10,9... | collective-permute-start | bytes 24584 | tf_op jit(solution)/shard_map/ppermute | solution.py:22
  4.7 0.6 collective-permute-start
  5.3 0.7 constant_dynamic-slice_fusion.2
  6.1 1.0 constant_dynamic-slice_fusion.3
  7.1 1.6 %collective-permute-start.7 = (bf16[2,144,256]{2,1,0:T(8,128)(2,1)S(1)}, bf16[2,144,256]{2,1,0:T(8,128)(2,1)S(1)}, u32[]{:S(2)}, u32[]{:S(2)}) collective-permute-start(bf16[2,144,256]{2,1,0:T(8,128)(2,1)S(1)} %pad_maximum_fusion.3), channel_id=1, source_target_pairs={{0,8},{8,0},{1,9},{9,1},{2,10},{10,2},{3,11},{11,3},{4,12},{12,4},... | collective-permute-start | bytes 442376 | tf_op jit(solution)/shard_map/ppermute | solution.py:26
  9.8 2.7 %collective-permute-start.6 = (s32[2,8,128]{2,1,0:T(8,128)S(1)}, s32[2,8,128]{2,1,0:T(8,128)S(1)}, u32[]{:S(2)}, u32[]{:S(2)}) collective-permute-start(s32[2,8,128]{2,1,0:T(8,128)S(1)} %add_add_fusion.1), channel_id=1, source_target_pairs={{0,12},{4,8},{8,4},{12,0},{1,13},{5,9},{9,5},{13,1},{2,14},{6,10},... | collective-permute-start | bytes 24584 | tf_op jit(solution)/shard_map/ppermute | solution.py:26
  14.4 0.7 pad_maximum_fusion.1
  15.2 3.6 %collective-permute-start.10 = (bf16[4,144,256]{2,1,0:T(8,128)(2,1)}, bf16[4,144,256]{2,1,0:T(8,128)(2,1)}, u32[]{:S(2)}, u32[]{:S(2)}) collective-permute-start(bf16[4,144,256]{2,1,0:T(8,128)(2,1)} %pad_maximum_fusion.1), channel_id=1, source_target_pairs={{0,64},{64,0},{1,65},{65,1},{2,66},{66,2},{3,67},{67,3},{4,68},{68... | collective-permute-start | bytes 884744 | tf_op jit(solution)/shard_map/ppermute | solution.py:26
  18.8 1.1 collective-permute-start.9
  20.4 6.1 %collective-permute-done.10 = bf16[4,144,256]{2,1,0:T(8,128)(2,1)} collective-permute-done((bf16[4,144,256]{2,1,0:T(8,128)(2,1)}, bf16[4,144,256]{2,1,0:T(8,128)(2,1)}, u32[]{:S(2)}, u32[]{:S(2)}) %collective-permute-start.10) | collective-permute-done | bytes 294944 | tf_op jit(solution)/shard_map/ppermute | solution.py:26
  26.4 2.7 %collective-permute-start.12 = (bf16[4,144,256]{2,1,0:T(8,128)(2,1)}, bf16[4,144,256]{2,1,0:T(8,128)(2,1)}, u32[]{:S(2)}, u32[]{:S(2)}) collective-permute-start(bf16[4,144,256]{2,1,0:T(8,128)(2,1)} %collective-permute-done.10), channel_id=1, source_target_pairs={{0,48},{16,0},{32,16},{48,32},{1,49},{17,1},{33,17},{49,33},{2,50}... | collective-permute-start | bytes 884744 | tf_op jit(solution)/shard_map/ppermute | solution.py:22
  29.2 1.8 %constant_dynamic-update-slice_fusion.10 = bf16[16,144,256]{2,1,0:T(8,128)(2,1)} fusion(bf16[4,144,256]{2,1,0:T(8,128)(2,1)} %collective-permute-done.10), kind=kLoop, calls=%fused_computation.25 | loop fusion | bytes 589824
  30.9 1.3 convert_element_type.21
  32.9 1.0 pad_maximum_fusion
  33.9 6.4 %all-to-all-start = ((bf16[8,112,512]{2,1,0:T(8,128)(2,1)}), bf16[8,112,512]{2,1,0:T(8,128)(2,1)S(1)}, u32[]{:S(2)}, u32[]{:S(2)}) async-start(bf16[8,112,512]{2,1,0:T(8,128)(2,1)} %pad_maximum_fusion), calls=%async_computation | async-start | bytes 1835008 | tf_op jit(solution)/shard_map/all_to_all | solution.py:317
  40.3 0.9 slice.51
  41.2 1.0 constant_dynamic-update-slice_fusion.3
  42.2 0.9 slice.52
  43.1 0.9 slice.53
  44.1 0.9 slice.54
  45.0 2.7 %collective-permute-start.16 = (bf16[2,144,256]{2,1,0:T(8,128)(2,1)S(1)}, bf16[2,144,256]{2,1,0:T(8,128)(2,1)S(1)}, u32[]{:S(2)}, u32[]{:S(2)}) collective-permute-start(bf16[2,144,256]{2,1,0:T(8,128)(2,1)S(1)} %slice.54), channel_id=1, source_target_pairs={{0,48},{16,0},{32,16},{48,32},{1,49},{17,1},{33,17},{49,33},{2,50}... | collective-permute-start | bytes 442376 | tf_op jit(solution)/shard_map/ppermute | solution.py:22
  47.7 0.9 collective-permute-start.14
  49.2 1.7 %constant_dynamic-update-slice_fusion.9 = bf16[16,144,256]{2,1,0:T(8,128)(2,1)} fusion(bf16[16,144,256]{2,1,0:T(8,128)(2,1)} %constant_dynamic-update-slice_fusion.10, bf16[4,144,256]{2,1,0:T(8,128)(2,1)} %collective-permute-done.11), kind=kLoop, calls=%fused_computation.24 | loop fusion | bytes 589824
  50.9 1.8 %constant_dynamic-update-slice_fusion.2 = (bf16[16,144,256]{2,1,0:T(8,128)(2,1)S(1)}, bf16[16,144,256]{2,1,0:T(8,128)(2,1)}) fusion(bf16[16,144,256]{2,1,0:T(8,128)(2,1)S(1)} %constant_dynamic-update-slice_fusion.3, bf16[4,144,256]{2,1,0:T(8,128)(2,1)} %collective-permute-done.9, bf16[16,144,256]{2,1,0:T(8,128)(2,1)} %constant_dynamic-update-slice_fusion.9, ...), kind=kLoop, calls=%fused_computation.17 | loop fusion | bytes 1179648
  52.7 1.3 collective-permute-done.16
  54.0 2.9 %collective-permute-done.15 = bf16[2,144,256]{2,1,0:T(8,128)(2,1)S(1)} collective-permute-done((bf16[2,144,256]{2,1,0:T(8,128)(2,1)S(1)}, bf16[2,144,256]{2,1,0:T(8,128)(2,1)S(1)}, u32[]{:S(2)}, u32[]{:S(2)}) %collective-permute-start.15) | collective-permute-done | bytes 147488 | tf_op jit(solution)/shard_map/ppermute | solution.py:22
  56.9 0.7 constant_dynamic-update-slice_fusion.7
  57.6 0.7 constant_dynamic-update-slice_fusion.6.refs_0_
  58.2 0.9 collective-permute-start.20
  59.7 0.7 constant_dynamic-update-slice_fusion.1
  60.4 0.7 constant_dynamic-update-slice_fusion.refs_0_
  61.2 1.3 collective-permute-start.17
  62.5 0.8 dynamic_slice.41
  63.4 0.8 reshape.113.taps
  64.3 0.9 reshape.114.skip
  65.1 0.7 constant_dynamic-slice_fusion.5
  65.8 2.1 %filters.1.toep = bf16[2,4,256,256]{3,2,1,0:T(8,128)(2,1)} custom-call(f32[16,2]{1,0:T(8,128)} %get-tuple-element.79.decay, f32[16,2]{1,0:T(8,128)} %get-tuple-element.78.residue), custom_call_target="tpu_custom_call" | custom-call | tf_op jit(solution)/shard_map/filters/pallas_call | solution.py:62
  67.9 1.2 copy-done.1
  69.1 0.9 copy-done.2
  70.1 0.9 copy-done.3
  71.0 8.7 %mixer.1 = bf16[4,8,32,512]{3,2,1,0:T(8,128)(2,1)} custom-call(bf16[8,112,512]{2,1,0:T(8,128)(2,1)S(1)} %all-to-all-done.recv, f32[3,96,1]{2,1,0:T(8,128)S(1)} %copy-done.3, f32[2,256,1]{2,1,0:T(8,128)S(1)} %copy-done.2, bf16[2,4,256,256]{3,2,1,0:T(8,128)(2,1)S(1)} %copy-done.1), custom_call_target="tpu_custom_call" | custom-call | flops 1610612736 | bytes 4194304 | tf_op jit(solution)/shard_map/mixer/pallas_call | solution.py:125
  79.7 7.2 %all-to-all-start.1 = ((bf16[32,32,512]{2,1,0:T(8,128)(2,1)}), bf16[32,32,512]{2,1,0:T(8,128)(2,1)S(1)}, u32[]{:S(2)}, u32[]{:S(2)}) async-start(bf16[32,32,512]{2,1,0:T(8,128)(2,1)} %bitcast.15), calls=%async_computation.1 | async-start | bytes 2097152 | tf_op jit(solution)/shard_map/all_to_all | solution.py:326
  87.4 1.9 %slice.55 = bf16[8,144,256]{2,1,0:T(8,128)(2,1)} slice(bf16[16,144,256]{2,1,0:T(8,128)(2,1)} %collective-permute-done.17.refs_1_), slice={[0:8], [0:144], [0:256]} | slice | bytes 1179648 | tf_op jit(solution)/shard_map/slice | solution.py:37
  89.3 2.0 %slice.56 = bf16[8,144,256]{2,1,0:T(8,128)(2,1)} slice(bf16[16,144,256]{2,1,0:T(8,128)(2,1)} %collective-permute-done.18.refs_2_), slice={[8:16], [0:144], [0:256]} | slice | bytes 1179648 | tf_op jit(solution)/shard_map/slice | solution.py:37
  91.3 0.9 slice.57
  92.2 0.9 slice.58
  93.1 2.1 %collective-permute-start.24 = (bf16[8,144,256]{2,1,0:T(8,128)(2,1)}, bf16[8,144,256]{2,1,0:T(8,128)(2,1)}, u32[]{:S(2)}, u32[]{:S(2)}) collective-permute-start(bf16[8,144,256]{2,1,0:T(8,128)(2,1)} %slice.58), channel_id=1, source_target_pairs={{0,3},{1,0},{2,1},{3,2},{4,7},{5,4},{6,5},{7,6},{8,11},{9,8},{10,9... | collective-permute-start | bytes 1769480 | tf_op jit(solution)/shard_map/ppermute | solution.py:22
  95.1 2.3 %collective-permute-start.22 = (bf16[8,144,256]{2,1,0:T(8,128)(2,1)}, bf16[8,144,256]{2,1,0:T(8,128)(2,1)}, u32[]{:S(2)}, u32[]{:S(2)}) collective-permute-start(bf16[8,144,256]{2,1,0:T(8,128)(2,1)} %slice.56), channel_id=1, source_target_pairs={{0,48},{16,0},{32,16},{48,32},{1,49},{17,1},{33,17},{49,33},{2,50}... | collective-permute-start | bytes 1769480 | tf_op jit(solution)/shard_map/ppermute | solution.py:22
  97.6 11.2 %collective-permute-done.24.refs_4_ = bf16[8,144,256]{2,1,0:T(8,128)(2,1)} collective-permute-done((bf16[8,144,256]{2,1,0:T(8,128)(2,1)}, bf16[8,144,256]{2,1,0:T(8,128)(2,1)}, u32[]{:S(2)}, u32[]{:S(2)}) %collective-permute-start.24) | collective-permute-done | bytes 589856 | tf_op jit(solution)/shard_map/ppermute | solution.py:22
  108.8 2.4 %collective-permute-done.23.refs_3_ = bf16[8,144,256]{2,1,0:T(8,128)(2,1)} collective-permute-done((bf16[8,144,256]{2,1,0:T(8,128)(2,1)}, bf16[8,144,256]{2,1,0:T(8,128)(2,1)}, u32[]{:S(2)}, u32[]{:S(2)}) %collective-permute-start.23) | collective-permute-done | bytes 589856 | tf_op jit(solution)/shard_map/ppermute | solution.py:22
  111.3 1.3 collective-permute-done.21.refs_3_
  112.6 1.3 copy-done.5
  113.9 4.9 %project_y.1 = (f32[4,512,256]{2,1,0:T(8,128)S(1)}, bf16[4,512,256]{2,1,0:T(8,128)(2,1)S(1)}) custom-call(s32[5]{0:T(128)S(1)} %stack.31.where, bf16[4,256,512]{2,1,0:T(8,128)(2,1)S(1)} %bitcast.38, s32[1,512]{1,0:T(1,128)S(1)} %bitcast.40, bf16[16,144,256]{2,1,0:T(8,128)(2,1)S(1)} %copy-done.5, bf16[16,144,256]{2,1,0:T(8,128)(2,1)} %collective-permute-done.17.refs_1_, ...), custom_call_target="tpu_custom_call" | custom-call | flops 2147483648 | bytes 10485760 | tf_op jit(solution)/shard_map/project_y/pallas_call | solution.py:182
  118.8 4.3 %collective-permute-start.25 = (bf16[4,512,256]{2,1,0:T(8,128)(2,1)S(1)}, bf16[4,512,256]{2,1,0:T(8,128)(2,1)S(1)}, u32[]{:S(2)}, u32[]{:S(2)}) collective-permute-start(bf16[4,512,256]{2,1,0:T(8,128)(2,1)S(1)} %get-tuple-element.48), channel_id=1, source_target_pairs={{0,8},{8,0},{1,9},{9,1},{2,10},{10,2},{3,11},{11,3},{4,12},{12,4},... | collective-permute-start | bytes 3145736 | tf_op jit(solution)/shard_map/ppermute | solution.py:26
  123.1 4.5 %project_x.1 = (f32[4,512,256]{2,1,0:T(8,128)S(1)}, bf16[4,512,256]{2,1,0:T(8,128)(2,1)S(1)}) custom-call(s32[5]{0:T(128)S(1)} %stack.31.where, bf16[4,256,512]{2,1,0:T(8,128)(2,1)S(1)} %bitcast.39, s32[1,512]{1,0:T(1,128)S(1)} %bitcast.41, bf16[16,144,256]{2,1,0:T(8,128)(2,1)} %constant_dynamic-update-slice_fusion.6.refs_0_, ...), custom_call_target="tpu_custom_call" | custom-call | flops 2147483648 | bytes 10485760 | tf_op jit(solution)/shard_map/project_x/pallas_call | solution.py:182
  127.7 0.8 merge.2
  128.5 0.8 collective-permute-start.27
  129.3 1.1 collective-permute-done.26.theirs
  130.4 0.8 merge.3
  131.2 0.8 collective-permute-start.28
  131.9 9.7 %collective-permute-done.27.got0 = bf16[4,512,128]{2,1,0:T(8,128)(2,1)S(1)} collective-permute-done((bf16[4,512,128]{2,1,0:T(8,128)(2,1)S(1)}, bf16[4,512,128]{2,1,0:T(8,128)(2,1)S(1)}, u32[]{:S(2)}, u32[]{:S(2)}) %collective-permute-start.27) | collective-permute-done | bytes 524320 | tf_op jit(solution)/shard_map/ppermute | solution.py:26
  141.6 11.2 %collective-permute-done.28.got1 = bf16[4,512,128]{2,1,0:T(8,128)(2,1)S(1)} collective-permute-done((bf16[4,512,128]{2,1,0:T(8,128)(2,1)S(1)}, bf16[4,512,128]{2,1,0:T(8,128)(2,1)S(1)}, u32[]{:S(2)}, u32[]{:S(2)}) %collective-permute-start.28) | collective-permute-done | bytes 524320 | tf_op jit(solution)/shard_map/ppermute | solution.py:26
  152.9 2.0 %finish.1 = bf16[128,4096]{1,0:T(8,128)(2,1)} custom-call(s32[5]{0:T(128)S(1)} %stack.31.where, s32[32]{0:T(128)S(1)} %copy-done.6, f32[4,512,128]{2,1,0:T(8,128)S(1)} %get-tuple-element.49.keep0, f32[4,512,128]{2,1,0:T(8,128)S(1)} %get-tuple-element.54.keep1, bf16[4,512,128]{2,1,0:T(8,128)(2,1)S(1)} %collective-permute-done.27.got0, ...), custom_call_target="tpu_custom_call" | custom-call | tf_op jit(solution)/shard_map/finish/pallas_call | solution.py:239
  (93 shorter events, 7.0 us)
Async XLA Ops:
  0.0 63.4 %copy-start = (f32[3,3,512]{2,1,0:T(4,128)S(1)}, f32[3,3,512]{2,1,0:T(4,128)}, u32[]{:S(2)}) copy-start(f32[3,3,512]{2,1,0:T(4,128)} %param.15) | copy-start | bytes 55300
  0.0 9.7 %copy-start.12 = (s32[1,128]{1,0:T(1,128)S(1)}, s32[1,128]{1,0:T(1,128)}, u32[]{:S(2)}) copy-start(s32[1,128]{1,0:T(1,128)} %param.10) | copy-start | bytes 1540
  0.0 8.7 %copy-start.7 = (bf16[2,512,128]{2,1,0:T(8,128)(2,1)S(1)}, bf16[2,512,128]{2,1,0:T(8,128)(2,1)}, u32[]{:S(2)}) copy-start(bf16[2,512,128]{2,1,0:T(8,128)(2,1)} %param.12) | copy-start | bytes 786436
  0.0 8.8 %copy-start.6 = (s32[32]{0:T(128)S(1)}, s32[32]{0:T(128)}, u32[]{:S(2)}) copy-start(s32[32]{0:T(128)} %bucket.1) | copy-start | bytes 388
  0.0 8.9 %copy-start.11 = (f32[4096]{0:T(1024)S(1)}, f32[4096]{0:T(1024)}, u32[]{:S(2)}) copy-start(f32[4096]{0:T(1024)} %param.13) | copy-start | bytes 49156
  0.0 12.6 %copy-start.8 = (bf16[2,128,3,512]{3,1,2,0:T(8,128)(2,1)S(1)}, bf16[2,128,3,512]{3,1,2,0:T(8,128)(2,1)}, u32[]{:S(2)}) copy-start(bf16[2,128,3,512]{3,1,2,0:T(8,128)(2,1)} %param.14) | copy-start | bytes 2359300
  0.9 8.8 %collective-permute-start.1 = (s32[2,8,128]{2,1,0:T(8,128)S(1)}, s32[2,8,128]{2,1,0:T(8,128)S(1)}, u32[]{:S(2)}, u32[]{:S(2)}) collective-permute-start(s32[2,8,128]{2,1,0:T(8,128)S(1)} %and_select_fusion), channel_id=1, source_target_pairs={{0,3},{1,0},{2,1},{3,2},{4,7},{5,4},{6,5},{7,6},{8,11},{9,8},{10,9... | collective-permute-start | bytes 24584 | tf_op jit(solution)/shard_map/ppermute | solution.py:22
  4.2 5.5 %collective-permute-start.2 = (s32[2,8,128]{2,1,0:T(8,128)S(1)}, s32[2,8,128]{2,1,0:T(8,128)S(1)}, u32[]{:S(2)}, u32[]{:S(2)}) collective-permute-start(s32[2,8,128]{2,1,0:T(8,128)S(1)} %and_select_fusion), channel_id=1, source_target_pairs={{0,2},{1,3},{2,0},{3,1},{4,6},{5,7},{6,4},{7,5},{8,10},{9,11},{10,... | collective-permute-start | bytes 24584 | tf_op jit(solution)/shard_map/ppermute | solution.py:22
  4.7 5.0 %collective-permute-start = (s32[2,8,128]{2,1,0:T(8,128)S(1)}, s32[2,8,128]{2,1,0:T(8,128)S(1)}, u32[]{:S(2)}, u32[]{:S(2)}) collective-permute-start(s32[2,8,128]{2,1,0:T(8,128)S(1)} %and_select_fusion), channel_id=1, source_target_pairs={{0,1},{1,2},{2,3},{3,0},{4,5},{5,6},{6,7},{7,4},{8,9},{9,10},{10,1... | collective-permute-start | bytes 24584 | tf_op jit(solution)/shard_map/ppermute | solution.py:22
  7.1 7.3 %collective-permute-start.7 = (bf16[2,144,256]{2,1,0:T(8,128)(2,1)S(1)}, bf16[2,144,256]{2,1,0:T(8,128)(2,1)S(1)}, u32[]{:S(2)}, u32[]{:S(2)}) collective-permute-start(bf16[2,144,256]{2,1,0:T(8,128)(2,1)S(1)} %pad_maximum_fusion.3), channel_id=1, source_target_pairs={{0,8},{8,0},{1,9},{9,1},{2,10},{10,2},{3,11},{11,3},{4,12},{12,4},... | collective-permute-start | bytes 442376 | tf_op jit(solution)/shard_map/ppermute | solution.py:26
  9.8 9.0 %collective-permute-start.6 = (s32[2,8,128]{2,1,0:T(8,128)S(1)}, s32[2,8,128]{2,1,0:T(8,128)S(1)}, u32[]{:S(2)}, u32[]{:S(2)}) collective-permute-start(s32[2,8,128]{2,1,0:T(8,128)S(1)} %add_add_fusion.1), channel_id=1, source_target_pairs={{0,12},{4,8},{8,4},{12,0},{1,13},{5,9},{9,5},{13,1},{2,14},{6,10},... | collective-permute-start | bytes 24584 | tf_op jit(solution)/shard_map/ppermute | solution.py:26
  12.4 6.3 %collective-permute-start.5 = (s32[2,8,128]{2,1,0:T(8,128)S(1)}, s32[2,8,128]{2,1,0:T(8,128)S(1)}, u32[]{:S(2)}, u32[]{:S(2)}) collective-permute-start(s32[2,8,128]{2,1,0:T(8,128)S(1)} %add_add_fusion.1), channel_id=1, source_target_pairs={{0,8},{4,12},{8,0},{12,4},{1,9},{5,13},{9,1},{13,5},{2,10},{6,14},... | collective-permute-start | bytes 24584 | tf_op jit(solution)/shard_map/ppermute | solution.py:26
  12.4 6.3 %collective-permute-start.4 = (s32[2,8,128]{2,1,0:T(8,128)S(1)}, s32[2,8,128]{2,1,0:T(8,128)S(1)}, u32[]{:S(2)}, u32[]{:S(2)}) collective-permute-start(s32[2,8,128]{2,1,0:T(8,128)S(1)} %add_add_fusion.1), channel_id=1, source_target_pairs={{0,4},{4,0},{8,12},{12,8},{1,5},{5,1},{9,13},{13,9},{2,6},{6,2},{1... | collective-permute-start | bytes 24584 | tf_op jit(solution)/shard_map/ppermute | solution.py:26
  13.8 17.1 %collective-permute-start.3 = (bf16[784,512]{1,0:T(8,128)(2,1)S(1)}, bf16[784,512]{1,0:T(8,128)(2,1)}, u32[]{:S(2)}, u32[]{:S(2)}) collective-permute-start(bf16[784,512]{1,0:T(8,128)(2,1)S(1)} %maximum_maximum_fusion), channel_id=1, source_target_pairs={{0,8},{8,0},{1,9},{9,1},{2,10},{10,2},{3,11},{11,3},{4,12},{12,4},... | collective-permute-start | bytes 2408456 | tf_op jit(solution)/shard_map/ppermute | solution.py:26
  15.2 11.3 %collective-permute-start.10 = (bf16[4,144,256]{2,1,0:T(8,128)(2,1)}, bf16[4,144,256]{2,1,0:T(8,128)(2,1)}, u32[]{:S(2)}, u32[]{:S(2)}) collective-permute-start(bf16[4,144,256]{2,1,0:T(8,128)(2,1)} %pad_maximum_fusion.1), channel_id=1, source_target_pairs={{0,64},{64,0},{1,65},{65,1},{2,66},{66,2},{3,67},{67,3},{4,68},{68... | collective-permute-start | bytes 884744 | tf_op jit(solution)/shard_map/ppermute | solution.py:26
  18.8 21.4 %collective-permute-start.9 = (bf16[4,144,256]{2,1,0:T(8,128)(2,1)}, bf16[4,144,256]{2,1,0:T(8,128)(2,1)}, u32[]{:S(2)}, u32[]{:S(2)}) collective-permute-start(bf16[4,144,256]{2,1,0:T(8,128)(2,1)} %pad_maximum_fusion.1), channel_id=1, source_target_pairs={{0,3},{1,0},{2,1},{3,2},{4,7},{5,4},{6,5},{7,6},{8,11},{9,8},{10,9... | collective-permute-start | bytes 884744 | tf_op jit(solution)/shard_map/ppermute | solution.py:22
  19.9 20.3 %collective-permute-start.8 = (bf16[4,144,256]{2,1,0:T(8,128)(2,1)}, bf16[4,144,256]{2,1,0:T(8,128)(2,1)}, u32[]{:S(2)}, u32[]{:S(2)}) collective-permute-start(bf16[4,144,256]{2,1,0:T(8,128)(2,1)} %pad_maximum_fusion.1), channel_id=1, source_target_pairs={{0,1},{1,2},{2,3},{3,0},{4,5},{5,6},{6,7},{7,4},{8,9},{9,10},{10,1... | collective-permute-start | bytes 884744 | tf_op jit(solution)/shard_map/ppermute | solution.py:22
  26.4 13.9 %collective-permute-start.12 = (bf16[4,144,256]{2,1,0:T(8,128)(2,1)}, bf16[4,144,256]{2,1,0:T(8,128)(2,1)}, u32[]{:S(2)}, u32[]{:S(2)}) collective-permute-start(bf16[4,144,256]{2,1,0:T(8,128)(2,1)} %collective-permute-done.10), channel_id=1, source_target_pairs={{0,48},{16,0},{32,16},{48,32},{1,49},{17,1},{33,17},{49,33},{2,50}... | collective-permute-start | bytes 884744 | tf_op jit(solution)/shard_map/ppermute | solution.py:22
  29.2 11.1 %collective-permute-start.11 = (bf16[4,144,256]{2,1,0:T(8,128)(2,1)}, bf16[4,144,256]{2,1,0:T(8,128)(2,1)}, u32[]{:S(2)}, u32[]{:S(2)}) collective-permute-start(bf16[4,144,256]{2,1,0:T(8,128)(2,1)} %collective-permute-done.10), channel_id=1, source_target_pairs={{0,16},{16,32},{32,48},{48,0},{1,17},{17,33},{33,49},{49,1},{2,18}... | collective-permute-start | bytes 884744 | tf_op jit(solution)/shard_map/ppermute | solution.py:22
  33.9 34.0 %all-to-all-start = ((bf16[8,112,512]{2,1,0:T(8,128)(2,1)}), bf16[8,112,512]{2,1,0:T(8,128)(2,1)S(1)}, u32[]{:S(2)}, u32[]{:S(2)}) async-start(bf16[8,112,512]{2,1,0:T(8,128)(2,1)} %pad_maximum_fusion), calls=%async_computation | async-start | bytes 1835008 | tf_op jit(solution)/shard_map/all_to_all | solution.py:317
  45.0 9.0 %collective-permute-start.16 = (bf16[2,144,256]{2,1,0:T(8,128)(2,1)S(1)}, bf16[2,144,256]{2,1,0:T(8,128)(2,1)S(1)}, u32[]{:S(2)}, u32[]{:S(2)}) collective-permute-start(bf16[2,144,256]{2,1,0:T(8,128)(2,1)S(1)} %slice.54), channel_id=1, source_target_pairs={{0,48},{16,0},{32,16},{48,32},{1,49},{17,1},{33,17},{49,33},{2,50}... | collective-permute-start | bytes 442376 | tf_op jit(solution)/shard_map/ppermute | solution.py:22
  47.7 9.2 %collective-permute-start.15 = (bf16[2,144,256]{2,1,0:T(8,128)(2,1)S(1)}, bf16[2,144,256]{2,1,0:T(8,128)(2,1)S(1)}, u32[]{:S(2)}, u32[]{:S(2)}) collective-permute-start(bf16[2,144,256]{2,1,0:T(8,128)(2,1)S(1)} %slice.53), channel_id=1, source_target_pairs={{0,16},{16,32},{32,48},{48,0},{1,17},{17,33},{33,49},{49,1},{2,18}... | collective-permute-start | bytes 442376 | tf_op jit(solution)/shard_map/ppermute | solution.py:22
  47.7 9.2 %collective-permute-start.14 = (bf16[2,144,256]{2,1,0:T(8,128)(2,1)S(1)}, bf16[2,144,256]{2,1,0:T(8,128)(2,1)S(1)}, u32[]{:S(2)}, u32[]{:S(2)}) collective-permute-start(bf16[2,144,256]{2,1,0:T(8,128)(2,1)S(1)} %slice.52), channel_id=1, source_target_pairs={{0,3},{1,0},{2,1},{3,2},{4,7},{5,4},{6,5},{7,6},{8,11},{9,8},{10,9... | collective-permute-start | bytes 442376 | tf_op jit(solution)/shard_map/ppermute | solution.py:22
  48.6 8.3 %collective-permute-start.13 = (bf16[2,144,256]{2,1,0:T(8,128)(2,1)S(1)}, bf16[2,144,256]{2,1,0:T(8,128)(2,1)S(1)}, u32[]{:S(2)}, u32[]{:S(2)}) collective-permute-start(bf16[2,144,256]{2,1,0:T(8,128)(2,1)S(1)} %slice.51), channel_id=1, source_target_pairs={{0,1},{1,2},{2,3},{3,0},{4,5},{5,6},{6,7},{7,4},{8,9},{9,10},{10,1... | collective-permute-start | bytes 442376 | tf_op jit(solution)/shard_map/ppermute | solution.py:22
  50.9 14.3 %copy-start.9 = (f32[16,32]{1,0:T(8,128)S(1)}, f32[16,32]{1,0:T(8,128)}, u32[]{:S(2)}) copy-start(f32[16,32]{1,0:T(8,128)} %param.17) | copy-start | bytes 6148
  50.9 14.3 %copy-start.10 = (f32[16,32]{1,0:T(8,128)S(1)}, f32[16,32]{1,0:T(8,128)}, u32[]{:S(2)}) copy-start(f32[16,32]{1,0:T(8,128)} %param.16) | copy-start | bytes 6148
  52.7 4.9 %copy-start.4 = (bf16[16,144,256]{2,1,0:T(8,128)(2,1)}, bf16[16,144,256]{2,1,0:T(8,128)(2,1)S(1)}, u32[]{:S(2)}) copy-start(bf16[16,144,256]{2,1,0:T(8,128)(2,1)S(1)} %get-tuple-element.80) | copy-start | bytes 3538948
  58.2 28.7 %collective-permute-start.20 = (bf16[16,144,256]{2,1,0:T(8,128)(2,1)}, bf16[16,144,256]{2,1,0:T(8,128)(2,1)S(1)}, u32[]{:S(2)}, u32[]{:S(2)}) collective-permute-start(bf16[16,144,256]{2,1,0:T(8,128)(2,1)} %constant_dynamic-update-slice_fusion.6.refs_0_), channel_id=1, source_target_pairs={{0,3},{1,0},{2,1},{3,2},{4,7},{5,4},{6,5},{7,6},{8,11},{9,8},{10,9... | collective-permute-start | bytes 3538952 | tf_op jit(solution)/shard_map/ppermute | solution.py:22
  59.1 27.9 %collective-permute-start.19 = (bf16[16,144,256]{2,1,0:T(8,128)(2,1)}, bf16[16,144,256]{2,1,0:T(8,128)(2,1)S(1)}, u32[]{:S(2)}, u32[]{:S(2)}) collective-permute-start(bf16[16,144,256]{2,1,0:T(8,128)(2,1)} %constant_dynamic-update-slice_fusion.6.refs_0_), channel_id=1, source_target_pairs={{0,1},{1,2},{2,3},{3,0},{4,5},{5,6},{6,7},{7,4},{8,9},{9,10},{10,1... | collective-permute-start | bytes 3538952 | tf_op jit(solution)/shard_map/ppermute | solution.py:22
  61.1 26.4 %collective-permute-start.18 = (bf16[16,144,256]{2,1,0:T(8,128)(2,1)}, bf16[16,144,256]{2,1,0:T(8,128)(2,1)}, u32[]{:S(2)}, u32[]{:S(2)}) collective-permute-start(bf16[16,144,256]{2,1,0:T(8,128)(2,1)} %constant_dynamic-update-slice_fusion.refs_0_), channel_id=1, source_target_pairs={{0,48},{16,0},{32,16},{48,32},{1,49},{17,1},{33,17},{49,33},{2,50}... | collective-permute-start | bytes 3538952 | tf_op jit(solution)/shard_map/ppermute | solution.py:22
  61.2 26.2 %collective-permute-start.17 = (bf16[16,144,256]{2,1,0:T(8,128)(2,1)}, bf16[16,144,256]{2,1,0:T(8,128)(2,1)}, u32[]{:S(2)}, u32[]{:S(2)}) collective-permute-start(bf16[16,144,256]{2,1,0:T(8,128)(2,1)} %constant_dynamic-update-slice_fusion.refs_0_), channel_id=1, source_target_pairs={{0,16},{16,32},{32,48},{48,0},{1,17},{17,33},{33,49},{49,1},{2,18}... | collective-permute-start | bytes 3538952 | tf_op jit(solution)/shard_map/ppermute | solution.py:22
  67.9 1.2 copy-start.1
  69.1 0.9 copy-start.2
  70.1 0.9 copy-start.3
  79.7 32.9 %all-to-all-start.1 = ((bf16[32,32,512]{2,1,0:T(8,128)(2,1)}), bf16[32,32,512]{2,1,0:T(8,128)(2,1)S(1)}, u32[]{:S(2)}, u32[]{:S(2)}) async-start(bf16[32,32,512]{2,1,0:T(8,128)(2,1)} %bitcast.15), calls=%async_computation.1 | async-start | bytes 2097152 | tf_op jit(solution)/shard_map/all_to_all | solution.py:326
  93.1 15.7 %collective-permute-start.24 = (bf16[8,144,256]{2,1,0:T(8,128)(2,1)}, bf16[8,144,256]{2,1,0:T(8,128)(2,1)}, u32[]{:S(2)}, u32[]{:S(2)}) collective-permute-start(bf16[8,144,256]{2,1,0:T(8,128)(2,1)} %slice.58), channel_id=1, source_target_pairs={{0,3},{1,0},{2,1},{3,2},{4,7},{5,4},{6,5},{7,6},{8,11},{9,8},{10,9... | collective-permute-start | bytes 1769480 | tf_op jit(solution)/shard_map/ppermute | solution.py:22
  95.1 16.0 %collective-permute-start.23 = (bf16[8,144,256]{2,1,0:T(8,128)(2,1)}, bf16[8,144,256]{2,1,0:T(8,128)(2,1)}, u32[]{:S(2)}, u32[]{:S(2)}) collective-permute-start(bf16[8,144,256]{2,1,0:T(8,128)(2,1)} %slice.57), channel_id=1, source_target_pairs={{0,1},{1,2},{2,3},{3,0},{4,5},{5,6},{6,7},{7,4},{8,9},{9,10},{10,1... | collective-permute-start | bytes 1769480 | tf_op jit(solution)/shard_map/ppermute | solution.py:22
  95.1 16.2 %collective-permute-start.22 = (bf16[8,144,256]{2,1,0:T(8,128)(2,1)}, bf16[8,144,256]{2,1,0:T(8,128)(2,1)}, u32[]{:S(2)}, u32[]{:S(2)}) collective-permute-start(bf16[8,144,256]{2,1,0:T(8,128)(2,1)} %slice.56), channel_id=1, source_target_pairs={{0,48},{16,0},{32,16},{48,32},{1,49},{17,1},{33,17},{49,33},{2,50}... | collective-permute-start | bytes 1769480 | tf_op jit(solution)/shard_map/ppermute | solution.py:22
  97.5 15.1 %collective-permute-start.21 = (bf16[8,144,256]{2,1,0:T(8,128)(2,1)}, bf16[8,144,256]{2,1,0:T(8,128)(2,1)}, u32[]{:S(2)}, u32[]{:S(2)}) collective-permute-start(bf16[8,144,256]{2,1,0:T(8,128)(2,1)} %slice.55), channel_id=1, source_target_pairs={{0,16},{16,32},{32,48},{48,0},{1,17},{17,33},{33,49},{49,1},{2,18}... | collective-permute-start | bytes 1769480 | tf_op jit(solution)/shard_map/ppermute | solution.py:22
  112.6 1.3 copy-start.5
  118.8 9.0 %collective-permute-start.25 = (bf16[4,512,256]{2,1,0:T(8,128)(2,1)S(1)}, bf16[4,512,256]{2,1,0:T(8,128)(2,1)S(1)}, u32[]{:S(2)}, u32[]{:S(2)}) collective-permute-start(bf16[4,512,256]{2,1,0:T(8,128)(2,1)S(1)} %get-tuple-element.48), channel_id=1, source_target_pairs={{0,8},{8,0},{1,9},{9,1},{2,10},{10,2},{3,11},{11,3},{4,12},{12,4},... | collective-permute-start | bytes 3145736 | tf_op jit(solution)/shard_map/ppermute | solution.py:26
  127.6 2.7 %collective-permute-start.26 = (bf16[4,512,256]{2,1,0:T(8,128)(2,1)S(1)}, bf16[4,512,256]{2,1,0:T(8,128)(2,1)S(1)}, u32[]{:S(2)}, u32[]{:S(2)}) collective-permute-start(bf16[4,512,256]{2,1,0:T(8,128)(2,1)S(1)} %get-tuple-element.53), channel_id=1, source_target_pairs={{0,8},{8,0},{1,9},{9,1},{2,10},{10,2},{3,11},{11,3},{4,12},{12,4},... | collective-permute-start | bytes 3145736 | tf_op jit(solution)/shard_map/ppermute | solution.py:26
  128.5 13.1 %collective-permute-start.27 = (bf16[4,512,128]{2,1,0:T(8,128)(2,1)S(1)}, bf16[4,512,128]{2,1,0:T(8,128)(2,1)S(1)}, u32[]{:S(2)}, u32[]{:S(2)}) collective-permute-start(bf16[4,512,128]{2,1,0:T(8,128)(2,1)S(1)} %get-tuple-element.55), channel_id=1, source_target_pairs={{0,4},{4,0},{1,5},{5,1},{2,6},{6,2},{3,7},{7,3},{8,12},{12,8},{9,1... | collective-permute-start | bytes 1572872 | tf_op jit(solution)/shard_map/ppermute | solution.py:26
  131.2 21.7 %collective-permute-start.28 = (bf16[4,512,128]{2,1,0:T(8,128)(2,1)S(1)}, bf16[4,512,128]{2,1,0:T(8,128)(2,1)S(1)}, u32[]{:S(2)}, u32[]{:S(2)}) collective-permute-start(bf16[4,512,128]{2,1,0:T(8,128)(2,1)S(1)} %get-tuple-element.56), channel_id=1, source_target_pairs={{0,4},{4,0},{1,5},{5,1},{2,6},{6,2},{3,7},{7,3},{8,12},{12,8},{9,1... | collective-permute-start | bytes 1572872 | tf_op jit(solution)/shard_map/ppermute | solution.py:26

commit v4 on v3

--- a/solution.py
+++ b/solution.py
@@ -139,10 +139,20 @@
     )(recv, taps, skip, toep)
 
 
-def project_kernel(far_axis, where, gated, ids, *refs):
-    pieces = refs[:5]
-    mine, theirs, right, hot = refs[5:]
-    x, y, zl, co = where[0], where[1], where[3], where[4]
+def front_block(refs, i, xr, s):
+    return refs[i].at[4 * xr + s]
+
+
+def back_block(refs, i, xr, s):
+    if i == 0:
+        return refs[xr // 2].at[4 * (xr % 2) + s]
+    at = 4 * (i - 1) + s
+    return refs[2 + xr].at[at] if xr < 3 else refs[5 + at // 8].at[at % 8]
+
+
+def project_kernel(count, block, where, gated, ids, *refs):
+    mine, theirs, right, hot = refs[-4:]
+    x, zl, co = where[0], where[3], where[4]
 
     for r in range(4):
         x_of = lax.rem(x + OFFSETS[r], 4)
@@ -150,17 +160,9 @@
         word = lax.broadcasted_iota(jnp.int32, (32, 512), 0) + ((zl * 4 + x_of) * 2 + co) * 32
         hot[32 * r : 32 * r + 32, :] = jnp.where(word == ids[...], 1.0, 0.0).astype(BF16)
 
-    def block(xr, yr, s):
-        near, far = (xr, yr) if far_axis == "y" else (yr, xr)
-        at = 4 * near + s
-        if far < 3:
-            return pieces[far].at[at]
-        return pieces[3].at[at] if at < 8 else pieces[4].at[at - 8]
-
-    for yr in range(4):
-        y_of = lax.rem(y + OFFSETS[yr], 4)
+    for i in range(count):
         for s in range(4):
-            tiles = [block(xr, yr, s) for xr in range(4)]
+            tiles = [block(refs, i, xr, s) for xr in range(4)]
             rows = jnp.concatenate([t[0:128, :] for t in tiles], axis=1)
             words = jnp.concatenate(
                 [t[128:144, 128 * h : 128 * h + 128] for t in tiles for h in range(2)], axis=0
@@ -170,39 +172,39 @@
                 words, hot[...], (((0,), (0,)), ((), ())), preferred_element_type=F32
             )
             cols = slice(128 * s, 128 * s + 128)
-            mine[y_of, cols, :] = jnp.where(co == 0, total[:, 0:256], total[:, 256:512])
-            theirs[y_of, cols, :] = jnp.where(
-                co == 0, total[:, 256:512], total[:, 0:256]
-            ).astype(BF16)
-
-
-def project(far_axis, where, gated, ids, pieces):
+            mine[i, cols, :] = jnp.where(co == 0, total[:, 0:256], total[:, 256:512])
+            theirs[i, cols, :] = jnp.where(co == 0, total[:, 256:512], total[:, 0:256]).astype(
+                BF16
+            )
+
+
+def project(name, count, block, where, gated, ids, pieces):
     vmem = pl.BlockSpec(memory_space=pltpu.VMEM)
     smem = pl.BlockSpec(memory_space=pltpu.SMEM)
     return pl.pallas_call(
-        functools.partial(project_kernel, far_axis),
+        functools.partial(project_kernel, count, block),
         out_shape=(
-            jax.ShapeDtypeStruct((4, 512, 256), F32),
-            jax.ShapeDtypeStruct((4, 512, 256), BF16),
+            jax.ShapeDtypeStruct((count, 512, 256), F32),
+            jax.ShapeDtypeStruct((count, 512, 256), BF16),
         ),
-        in_specs=[smem] + [vmem] * 7,
+        in_specs=[smem] + [vmem] * (2 + len(pieces)),
         out_specs=(vmem, vmem),
         scratch_shapes=[pltpu.VMEM((1024, 512), BF16), pltpu.VMEM((128, 512), BF16)],
         compiler_params=pltpu.CompilerParams(vmem_limit_bytes=32 << 20),
         cost_estimate=pl.CostEstimate(
-            flops=2 * 512 * 2048 * 1024, bytes_accessed=10 << 20, transcendentals=0
+            flops=2 * 512 * 512 * count * 1024, bytes_accessed=3 * count << 20, transcendentals=0
         ),
-        name="project_" + far_axis,
+        name=name,
     )(where, gated, ids, *pieces)
 
 
 def merge_kernel(where, mine, theirs, keep, give):
     zl = where[3]
-    for y in range(4):
-        total = mine[y] + theirs[y].astype(F32)
+    for i in range(mine.shape[0]):
+        total = mine[i] + theirs[i].astype(F32)
         low, high = total[:, 0:128], total[:, 128:256]
-        keep[y] = jnp.where(zl == 0, low, high)
-        give[y] = jnp.where(zl == 0, high, low).astype(BF16)
+        keep[i] = jnp.where(zl == 0, low, high)
+        give[i] = jnp.where(zl == 0, high, low).astype(BF16)
 
 
 def merge(where, mine, theirs):
@@ -211,8 +213,8 @@
     return pl.pallas_call(
         merge_kernel,
         out_shape=(
-            jax.ShapeDtypeStruct((4, 512, 128), F32),
-            jax.ShapeDtypeStruct((4, 512, 128), BF16),
+            jax.ShapeDtypeStruct((mine.shape[0], 512, 128), F32),
+            jax.ShapeDtypeStruct((mine.shape[0], 512, 128), BF16),
         ),
         in_specs=[smem, vmem, vmem],
         out_specs=(vmem, vmem),
@@ -222,13 +224,14 @@
 
 
 def finish_kernel(where, bucket, keep0, keep1, got0, got1, out):
-    zh = where[2]
-    for p, (keep, got) in enumerate(((keep0, got0), (keep1, got1))):
-        for y in range(4):
+    y, zh = where[1], where[2]
+    for p in range(2):
+        for r in range(4):
+            keep, got, i = (keep0, got0, r) if p == 0 and r < 3 else (keep1, got1, p * (r + 1))
             for s in range(4):
                 rows = slice(128 * s, 128 * s + 128)
-                total = keep[y, rows, :] + got[y, rows, :].astype(F32)
-                slot = 16 * lax.rem(zh + p, 2) + 4 * y + s
+                total = keep[i, rows, :] + got[i, rows, :].astype(F32)
+                slot = 16 * lax.rem(zh + p, 2) + 4 * lax.rem(y + OFFSETS[r], 4) + s
                 cols = pl.ds(pl.multiple_of(bucket[slot] * 128, 128), 128)
                 out[:, cols] = total.T.astype(BF16)
 
@@ -280,9 +283,13 @@
         words = words.reshape(2, 2, 16, 128).transpose(0, 2, 1, 3).reshape(2, 16, 256)
         return jnp.concatenate([rows, words], axis=1)
 
-    ours, sent = tile_for(co), flip(tile_for(1 - co), "co", 1, 2)
-    tiles = jnp.concatenate([jnp.where(co == 0, ours, sent), jnp.where(co == 0, sent, ours)])
-    across = flip(tiles, "zh", 1, 2)
+    ours, lent = tile_for(co), tile_for(1 - co)
+
+    def by_core(own, sibling):
+        return jnp.concatenate([jnp.where(co == 0, own, sibling), jnp.where(co == 0, sibling, own)])
+
+    tiles = by_core(ours, flip(lent, "co", 1, 2))
+    across = by_core(flip(ours, "zh", 1, 2), flip(lent, ("zh", "co"), 3, 4))
 
     buckets = lax.dynamic_slice_in_dim(bucket_of_slot, 2 * d, 2)
     gain = jnp.take(norm_gain.reshape(32, 128), buckets, axis=0)
@@ -328,9 +335,13 @@
     ).reshape(4, 256, 512)
 
     where = jnp.stack([x, y, zh, zl, co]).astype(jnp.int32)
+    own_half, other_half = pieces
     keep, got = [], []
-    for p, far in enumerate(("y", "x")):
-        mine, theirs = project(far, where, gated, here, pieces[p])
+    for args in (
+        ("front", 3, front_block, where, gated, here, own_half[:3]),
+        ("back", 5, back_block, where, gated, here, own_half[3:] + other_half),
+    ):
+        mine, theirs = project(*args)
         kept, given = merge(where, mine, flip(theirs, "co", 1, 2))
         keep.append(kept)
         got.append(flip(given, "zl", 1, 2))

time: 156 us -> 153 us (0.981)
  waiting for transfers between devices: 47.9 us -> 44.8 us
  other arithmetic: 4.69 us -> 7.52 us
  local copies, waits for them, and re-layouts: 29 us -> 27.3 us
    ppermute x19, starting transfers between devices: 20.3 us -> 26.7 us  [shift(): return lax.ppermute(value, axis, [(i, (i + step) % 4) for i in range(4)])]
    ppermute x10 -> x11, starting transfers between devices: 14.5 us -> 11.2 us  [flip(): return lax.ppermute(value, axes, [(i, i ^ bits) for i in range(size)])]
    ppermute x10 -> x11, waiting for transfers between devices: 28.1 us -> 25 us  [flip(): return lax.ppermute(value, axes, [(i, i ^ bits) for i in range(size)])]
    all_to_all x1, starting transfers between devices: 6.4 us -> 4.11 us  [body(): lax.all_to_all(packed, ('zh', 'y'), split_axis=0, concat_axis=0, tiled=True)]
    all_to_all x1, starting transfers between devices: 7.18 us -> 5.04 us  [body(): lax.all_to_all(gated.reshape(32, 32, 512), ('x', 'zh', 'y'), split_axis=0...]
    unnamed x32 -> x31, local copies, waits for them, and re-layouts: 12 us -> 10.2 us
  transfers between devices with their start and end apart: 31 -> 32, of which waited for: 12 -> 7; matrix products, arithmetic and copies ran while one was open for 19% -> 20% of each run, Pallas kernels for 11% -> 10%
where the time goes in v4:
time: 153 us; the launch traced here: 152 us
  starting transfers between devices  47 us (31%)
  waiting for transfers between devices  44.8 us (29%)
  local copies, waits for them, and re-layouts  27.3 us (18%)
  Pallas kernels  23.8 us (16%)
  other arithmetic  7.52 us (5%)
    ppermute x19, starting transfers between devices, shift(): return lax.ppermute(value, axis, [(i, (i + step) % 4) for i in range(4)])  26.7 us
    ppermute x11, waiting for transfers between devices, flip(): return lax.ppermute(value, axes, [(i, i ^ bits) for i in range(size)])  25 us
    ppermute x19, waiting for transfers between devices, shift(): return lax.ppermute(value, axis, [(i, (i + step) % 4) for i in range(4)])  19.8 us
    ppermute x11, starting transfers between devices, flip(): return lax.ppermute(value, axes, [(i, i ^ bits) for i in range(size)])  11.2 us
    unnamed x31, local copies, waits for them, and re-layouts  10.2 us
    pallas_call x2, Pallas kernels, project(): pl.pallas_call(functools.partial(project_kernel, count, block), out_shape...  9.42 us
    pallas_call x1, Pallas kernels, mixer(): pl.pallas_call(mixer_kernel, out_shape=jax.ShapeDtypeStruct((4, 8, 32, 51...  8.74 us
    all_to_all x1, starting transfers between devices, body(): lax.all_to_all(gated.reshape(32, 32, 512), ('x', 'zh', 'y'), split_axis=0...  5.04 us
  transfers between devices with their start and end apart: 32, of which 7 were waited for; matrix products, arithmetic and copies ran while one was open for 20% of the time, Pallas kernels for 10%

profile of v4, /device:TPU:1, one launch (start us, length us, event | category | flops | bytes accessed | tf_op | source)
XLA Modules:
  0.0 151.6 jit_solution(1780716993335781060)
XLA Ops:
  0.1 0.8 and_select_fusion
  0.9 3.6 %collective-permute-start.2 = (s32[2,8,128]{2,1,0:T(8,128)S(1)}, s32[2,8,128]{2,1,0:T(8,128)S(1)}, u32[]{:S(2)}, u32[]{:S(2)}) collective-permute-start(s32[2,8,128]{2,1,0:T(8,128)S(1)} %and_select_fusion), channel_id=1, source_target_pairs={{0,2},{1,3},{2,0},{3,1},{4,6},{5,7},{6,4},{7,5},{8,10},{9,11},{10,... | collective-permute-start | bytes 24584 | tf_op jit(solution)/shard_map/ppermute | solution.py:22
  4.5 0.9 collective-permute-start.1
  5.9 0.7 constant_dynamic-slice_fusion.2
  6.7 1.0 constant_dynamic-slice_fusion.3
  8.3 1.5 collective-permute-start.7
  9.8 3.5 %collective-permute-start.11 = (bf16[2,144,256]{2,1,0:T(8,128)(2,1)}, bf16[2,144,256]{2,1,0:T(8,128)(2,1)S(1)}, u32[]{:S(2)}, u32[]{:S(2)}) collective-permute-start(bf16[2,144,256]{2,1,0:T(8,128)(2,1)} %pad_maximum_fusion.4), channel_id=1, source_target_pairs={{0,72},{8,64},{64,8},{72,0},{1,73},{9,65},{65,9},{73,1},{2,74},{10... | collective-permute-start | bytes 442376 | tf_op jit(solution)/shard_map/ppermute | solution.py:26
  14.4 1.2 collective-permute-start.6
  15.6 0.7 collective-permute-start.4
  17.8 0.9 collective-permute-done.6
  18.7 0.7 constant_dynamic-update-slice_fusion.5
  19.5 1.2 collective-permute-start.10
  20.6 0.7 constant_dynamic-update-slice_fusion.4
  21.3 0.7 pad_maximum_fusion.1
  22.4 2.4 %collective-permute-start.9 = (bf16[4,144,256]{2,1,0:T(8,128)(2,1)}, bf16[4,144,256]{2,1,0:T(8,128)(2,1)}, u32[]{:S(2)}, u32[]{:S(2)}) collective-permute-start(bf16[4,144,256]{2,1,0:T(8,128)(2,1)} %pad_maximum_fusion.1), channel_id=1, source_target_pairs={{0,3},{1,0},{2,1},{3,2},{4,7},{5,4},{6,5},{7,6},{8,11},{9,8},{10,9... | collective-permute-start | bytes 884744 | tf_op jit(solution)/shard_map/ppermute | solution.py:22
  24.8 0.8 collective-permute-done.10
  25.7 0.8 pad_maximum_fusion.2
  26.4 1.3 collective-permute-start.12
  27.7 1.4 collective-permute-start.13
  29.2 1.3 convert_element_type.21
  31.1 1.0 pad_maximum_fusion
  32.1 4.1 %all-to-all-start = ((bf16[8,112,512]{2,1,0:T(8,128)(2,1)}), bf16[8,112,512]{2,1,0:T(8,128)(2,1)S(1)}, u32[]{:S(2)}, u32[]{:S(2)}) async-start(bf16[8,112,512]{2,1,0:T(8,128)(2,1)} %pad_maximum_fusion), calls=%async_computation | async-start | bytes 1835008 | tf_op jit(solution)/shard_map/all_to_all | solution.py:324
  36.2 0.9 slice.51
  37.2 1.7 %constant_dynamic-update-slice_fusion.3 = bf16[16,144,256]{2,1,0:T(8,128)(2,1)} fusion(bf16[16,144,256]{2,1,0:T(8,128)(2,1)} %get-tuple-element.61, bf16[4,144,256]{2,1,0:T(8,128)(2,1)} %collective-permute-done.8), kind=kLoop, calls=%fused_computation.21 | loop fusion | bytes 589824
  39.2 0.9 slice.52
  40.1 2.4 %collective-permute-start.15 = (bf16[2,144,256]{2,1,0:T(8,128)(2,1)S(1)}, bf16[2,144,256]{2,1,0:T(8,128)(2,1)S(1)}, u32[]{:S(2)}, u32[]{:S(2)}) collective-permute-start(bf16[2,144,256]{2,1,0:T(8,128)(2,1)S(1)} %slice.52), channel_id=1, source_target_pairs={{0,3},{1,0},{2,1},{3,2},{4,7},{5,4},{6,5},{7,6},{8,11},{9,8},{10,9... | collective-permute-start | bytes 442376 | tf_op jit(solution)/shard_map/ppermute | solution.py:22
  42.5 0.9 slice.53
  43.5 1.5 %collective-permute-start.16 = (bf16[2,144,256]{2,1,0:T(8,128)(2,1)S(1)}, bf16[2,144,256]{2,1,0:T(8,128)(2,1)S(1)}, u32[]{:S(2)}, u32[]{:S(2)}) collective-permute-start(bf16[2,144,256]{2,1,0:T(8,128)(2,1)S(1)} %slice.53), channel_id=1, source_target_pairs={{0,16},{16,32},{32,48},{48,0},{1,17},{17,33},{33,49},{49,1},{2,18}... | collective-permute-start | bytes 442376 | tf_op jit(solution)/shard_map/ppermute | solution.py:22
  45.0 0.9 slice.54
  45.9 1.3 collective-permute-start.17
  47.2 1.0 constant_dynamic-update-slice_fusion.9
  48.2 1.8 %constant_dynamic-update-slice_fusion.2 = (bf16[16,144,256]{2,1,0:T(8,128)(2,1)}, bf16[16,144,256]{2,1,0:T(8,128)(2,1)S(1)}) fusion(bf16[16,144,256]{2,1,0:T(8,128)(2,1)} %constant_dynamic-update-slice_fusion.3, bf16[4,144,256]{2,1,0:T(8,128)(2,1)} %collective-permute-done.9, bf16[16,144,256]{2,1,0:T(8,128)(2,1)S(1)} %constant_dynamic-update-slice_fusion.9, ...), kind=kLoop, calls=%fused_computation.20 | loop fusion | bytes 1179648
  50.0 2.7 %collective-permute-done.16 = bf16[2,144,256]{2,1,0:T(8,128)(2,1)S(1)} collective-permute-done((bf16[2,144,256]{2,1,0:T(8,128)(2,1)S(1)}, bf16[2,144,256]{2,1,0:T(8,128)(2,1)S(1)}, u32[]{:S(2)}, u32[]{:S(2)}) %collective-permute-start.16) | collective-permute-done | bytes 147488 | tf_op jit(solution)/shard_map/ppermute | solution.py:22
  52.8 0.7 constant_dynamic-update-slice_fusion.1
  53.4 0.7 constant_dynamic-update-slice_fusion.refs_0_
  54.1 2.7 %collective-permute-start.19 = (bf16[16,144,256]{2,1,0:T(8,128)(2,1)}, bf16[16,144,256]{2,1,0:T(8,128)(2,1)S(1)}, u32[]{:S(2)}, u32[]{:S(2)}) collective-permute-start(bf16[16,144,256]{2,1,0:T(8,128)(2,1)} %constant_dynamic-update-slice_fusion.refs_0_), channel_id=1, source_target_pairs={{0,48},{16,0},{32,16},{48,32},{1,49},{17,1},{33,17},{49,33},{2,50}... | collective-permute-start | bytes 3538952 | tf_op jit(solution)/shard_map/ppermute | solution.py:22
  58.5 2.3 %collective-permute-start.21 = (bf16[16,144,256]{2,1,0:T(8,128)(2,1)}, bf16[16,144,256]{2,1,0:T(8,128)(2,1)}, u32[]{:S(2)}, u32[]{:S(2)}) collective-permute-start(bf16[16,144,256]{2,1,0:T(8,128)(2,1)} %constant_dynamic-update-slice_fusion.6.refs_2_), channel_id=1, source_target_pairs={{0,3},{1,0},{2,1},{3,2},{4,7},{5,4},{6,5},{7,6},{8,11},{9,8},{10,9... | collective-permute-start | bytes 3538952 | tf_op jit(solution)/shard_map/ppermute | solution.py:22
  60.9 0.8 reshape.113.taps
  61.7 0.8 dynamic_slice.41
  62.5 0.9 reshape.114.skip
  64.1 2.1 %filters.1.toep = bf16[2,4,256,256]{3,2,1,0:T(8,128)(2,1)} custom-call(f32[16,2]{1,0:T(8,128)} %get-tuple-element.84.decay, f32[16,2]{1,0:T(8,128)} %get-tuple-element.83.residue), custom_call_target="tpu_custom_call" | custom-call | tf_op jit(solution)/shard_map/filters/pallas_call | solution.py:62
  66.2 1.2 copy-done.1
  67.4 0.9 copy-done.2
  68.3 0.9 copy-done.3
  69.3 8.7 %mixer.1 = bf16[4,8,32,512]{3,2,1,0:T(8,128)(2,1)} custom-call(bf16[8,112,512]{2,1,0:T(8,128)(2,1)S(1)} %all-to-all-done.recv, f32[3,96,1]{2,1,0:T(8,128)S(1)} %copy-done.3, f32[2,256,1]{2,1,0:T(8,128)S(1)} %copy-done.2, bf16[2,4,256,256]{3,2,1,0:T(8,128)(2,1)S(1)} %copy-done.1), custom_call_target="tpu_custom_call" | custom-call | flops 1610612736 | bytes 4194304 | tf_op jit(solution)/shard_map/mixer/pallas_call | solution.py:125
  78.0 5.0 %all-to-all-start.1 = ((bf16[32,32,512]{2,1,0:T(8,128)(2,1)}), bf16[32,32,512]{2,1,0:T(8,128)(2,1)S(1)}, u32[]{:S(2)}, u32[]{:S(2)}) async-start(bf16[32,32,512]{2,1,0:T(8,128)(2,1)} %bitcast.15), calls=%async_computation.1 | async-start | bytes 2097152 | tf_op jit(solution)/shard_map/all_to_all | solution.py:333
  83.1 1.8 %collective-permute-done.20.refs_3_ = bf16[16,144,256]{2,1,0:T(8,128)(2,1)} collective-permute-done((bf16[16,144,256]{2,1,0:T(8,128)(2,1)}, bf16[16,144,256]{2,1,0:T(8,128)(2,1)}, u32[]{:S(2)}, u32[]{:S(2)}) %collective-permute-start.20) | collective-permute-done | bytes 1179680 | tf_op jit(solution)/shard_map/ppermute | solution.py:22
  84.9 0.9 slice.55
  85.8 0.9 slice.56
  86.7 2.7 %collective-permute-start.24 = (bf16[8,144,256]{2,1,0:T(8,128)(2,1)}, bf16[8,144,256]{2,1,0:T(8,128)(2,1)}, u32[]{:S(2)}, u32[]{:S(2)}) collective-permute-start(bf16[8,144,256]{2,1,0:T(8,128)(2,1)} %slice.56), channel_id=1, source_target_pairs={{0,48},{16,0},{32,16},{48,32},{1,49},{17,1},{33,17},{49,33},{2,50}... | collective-permute-start | bytes 1769480 | tf_op jit(solution)/shard_map/ppermute | solution.py:22
  89.4 1.9 %slice.57 = bf16[8,144,256]{2,1,0:T(8,128)(2,1)} slice(bf16[16,144,256]{2,1,0:T(8,128)(2,1)} %collective-permute-done.20.refs_3_), slice={[0:8], [0:144], [0:256]} | slice | bytes 1179648 | tf_op jit(solution)/shard_map/slice | solution.py:37
  91.3 1.2 collective-permute-start.25
  92.5 1.9 %slice.58 = bf16[8,144,256]{2,1,0:T(8,128)(2,1)} slice(bf16[16,144,256]{2,1,0:T(8,128)(2,1)} %collective-permute-done.21.refs_4_), slice={[8:16], [0:144], [0:256]} | slice | bytes 1179648 | tf_op jit(solution)/shard_map/slice | solution.py:37
  94.4 1.5 collective-permute-start.26
  96.0 15.2 %collective-permute-done.23.refs_0_ = bf16[8,144,256]{2,1,0:T(8,128)(2,1)} collective-permute-done((bf16[8,144,256]{2,1,0:T(8,128)(2,1)}, bf16[8,144,256]{2,1,0:T(8,128)(2,1)}, u32[]{:S(2)}, u32[]{:S(2)}) %collective-permute-start.23) | collective-permute-done | bytes 589856 | tf_op jit(solution)/shard_map/ppermute | solution.py:22
  111.2 1.3 copy-done.5
  112.5 5.9 %back.1 = (f32[5,512,256]{2,1,0:T(8,128)S(1)}, bf16[5,512,256]{2,1,0:T(8,128)(2,1)S(1)}) custom-call(s32[5]{0:T(128)S(1)} %stack.31.where, bf16[4,256,512]{2,1,0:T(8,128)(2,1)S(1)} %bitcast.38, s32[1,512]{1,0:T(1,128)S(1)} %bitcast.40, bf16[8,144,256]{2,1,0:T(8,128)(2,1)} %collective-permute-done.23.refs_0_, ...), custom_call_target="tpu_custom_call" | custom-call | flops 2684354560 | bytes 15728640 | tf_op jit(solution)/shard_map/back/pallas_call | solution.py:184
  118.4 2.4 %collective-permute-start.27 = (bf16[5,512,256]{2,1,0:T(8,128)(2,1)S(1)}, bf16[5,512,256]{2,1,0:T(8,128)(2,1)S(1)}, u32[]{:S(2)}, u32[]{:S(2)}) collective-permute-start(bf16[5,512,256]{2,1,0:T(8,128)(2,1)S(1)} %get-tuple-element.53), channel_id=1, source_target_pairs={{0,8},{8,0},{1,9},{9,1},{2,10},{10,2},{3,11},{11,3},{4,12},{12,4},... | collective-permute-start | bytes 3932168 | tf_op jit(solution)/shard_map/ppermute | solution.py:26
  120.8 3.5 %front.1 = (f32[3,512,256]{2,1,0:T(8,128)S(1)}, bf16[3,512,256]{2,1,0:T(8,128)(2,1)S(1)}) custom-call(s32[5]{0:T(128)S(1)} %stack.31.where, bf16[4,256,512]{2,1,0:T(8,128)(2,1)S(1)} %bitcast.39, s32[1,512]{1,0:T(1,128)S(1)} %bitcast.41, bf16[16,144,256]{2,1,0:T(8,128)(2,1)} %constant_dynamic-update-slice_fusion.refs_0_, ...), custom_call_target="tpu_custom_call" | custom-call | flops 1610612736 | bytes 9437184 | tf_op jit(solution)/shard_map/front/pallas_call | solution.py:184
  124.4 0.9 merge.3
  125.4 1.3 collective-permute-done.22.theirs
  126.7 0.7 merge.2
  127.7 22.0 %collective-permute-done.28.got0 = bf16[3,512,128]{2,1,0:T(8,128)(2,1)S(1)} collective-permute-done((bf16[3,512,128]{2,1,0:T(8,128)(2,1)S(1)}, bf16[3,512,128]{2,1,0:T(8,128)(2,1)S(1)}, u32[]{:S(2)}, u32[]{:S(2)}) %collective-permute-start.28) | collective-permute-done | bytes 393248 | tf_op jit(solution)/shard_map/ppermute | solution.py:26
  149.6 2.0 %finish.1 = bf16[128,4096]{1,0:T(8,128)(2,1)} custom-call(s32[5]{0:T(128)S(1)} %stack.31.where, s32[32]{0:T(128)S(1)} %copy-done.6, f32[3,512,128]{2,1,0:T(8,128)S(1)} %get-tuple-element.45.keep0, f32[5,512,128]{2,1,0:T(8,128)S(1)} %get-tuple-element.54.keep1, bf16[3,512,128]{2,1,0:T(8,128)(2,1)S(1)} %collective-permute-done.28.got0, ...), custom_call_target="tpu_custom_call" | custom-call | tf_op jit(solution)/shard_map/finish/pallas_call | solution.py:242
  (97 shorter events, 8.2 us)
Async XLA Ops:
  0.0 60.8 %copy-start = (f32[3,3,512]{2,1,0:T(4,128)S(1)}, f32[3,3,512]{2,1,0:T(4,128)}, u32[]{:S(2)}) copy-start(f32[3,3,512]{2,1,0:T(4,128)} %param.15) | copy-start | bytes 55300
  0.0 14.4 %copy-start.12 = (s32[1,128]{1,0:T(1,128)S(1)}, s32[1,128]{1,0:T(1,128)}, u32[]{:S(2)}) copy-start(s32[1,128]{1,0:T(1,128)} %param.10) | copy-start | bytes 1540
  0.0 13.3 %copy-start.7 = (bf16[2,512,128]{2,1,0:T(8,128)(2,1)S(1)}, bf16[2,512,128]{2,1,0:T(8,128)(2,1)}, u32[]{:S(2)}) copy-start(bf16[2,512,128]{2,1,0:T(8,128)(2,1)} %param.12) | copy-start | bytes 786436
  0.0 13.5 %copy-start.6 = (s32[32]{0:T(128)S(1)}, s32[32]{0:T(128)}, u32[]{:S(2)}) copy-start(s32[32]{0:T(128)} %bucket.1) | copy-start | bytes 388
  0.0 13.6 %copy-start.11 = (f32[4096]{0:T(1024)S(1)}, f32[4096]{0:T(1024)}, u32[]{:S(2)}) copy-start(f32[4096]{0:T(1024)} %param.13) | copy-start | bytes 49156
  0.0 16.6 %copy-start.8 = (bf16[2,128,3,512]{3,1,2,0:T(8,128)(2,1)S(1)}, bf16[2,128,3,512]{3,1,2,0:T(8,128)(2,1)}, u32[]{:S(2)}) copy-start(bf16[2,128,3,512]{3,1,2,0:T(8,128)(2,1)} %param.14) | copy-start | bytes 2359300
  0.9 13.5 %collective-permute-start.2 = (s32[2,8,128]{2,1,0:T(8,128)S(1)}, s32[2,8,128]{2,1,0:T(8,128)S(1)}, u32[]{:S(2)}, u32[]{:S(2)}) collective-permute-start(s32[2,8,128]{2,1,0:T(8,128)S(1)} %and_select_fusion), channel_id=1, source_target_pairs={{0,2},{1,3},{2,0},{3,1},{4,6},{5,7},{6,4},{7,5},{8,10},{9,11},{10,... | collective-permute-start | bytes 24584 | tf_op jit(solution)/shard_map/ppermute | solution.py:22
  4.5 9.9 %collective-permute-start.1 = (s32[2,8,128]{2,1,0:T(8,128)S(1)}, s32[2,8,128]{2,1,0:T(8,128)S(1)}, u32[]{:S(2)}, u32[]{:S(2)}) collective-permute-start(s32[2,8,128]{2,1,0:T(8,128)S(1)} %and_select_fusion), channel_id=1, source_target_pairs={{0,3},{1,0},{2,1},{3,2},{4,7},{5,4},{6,5},{7,6},{8,11},{9,8},{10,9... | collective-permute-start | bytes 24584 | tf_op jit(solution)/shard_map/ppermute | solution.py:22
  5.3 9.0 %collective-permute-start = (s32[2,8,128]{2,1,0:T(8,128)S(1)}, s32[2,8,128]{2,1,0:T(8,128)S(1)}, u32[]{:S(2)}, u32[]{:S(2)}) collective-permute-start(s32[2,8,128]{2,1,0:T(8,128)S(1)} %and_select_fusion), channel_id=1, source_target_pairs={{0,1},{1,2},{2,3},{3,0},{4,5},{5,6},{6,7},{7,4},{8,9},{9,10},{10,1... | collective-permute-start | bytes 24584 | tf_op jit(solution)/shard_map/ppermute | solution.py:22
  8.3 10.4 %collective-permute-start.7 = (bf16[2,144,256]{2,1,0:T(8,128)(2,1)}, bf16[2,144,256]{2,1,0:T(8,128)(2,1)S(1)}, u32[]{:S(2)}, u32[]{:S(2)}) collective-permute-start(bf16[2,144,256]{2,1,0:T(8,128)(2,1)} %pad_maximum_fusion.4), channel_id=1, source_target_pairs={{0,8},{8,0},{1,9},{9,1},{2,10},{10,2},{3,11},{11,3},{4,12},{12,4},... | collective-permute-start | bytes 442376 | tf_op jit(solution)/shard_map/ppermute | solution.py:26
  9.8 14.9 %collective-permute-start.11 = (bf16[2,144,256]{2,1,0:T(8,128)(2,1)}, bf16[2,144,256]{2,1,0:T(8,128)(2,1)S(1)}, u32[]{:S(2)}, u32[]{:S(2)}) collective-permute-start(bf16[2,144,256]{2,1,0:T(8,128)(2,1)} %pad_maximum_fusion.4), channel_id=1, source_target_pairs={{0,72},{8,64},{64,8},{72,0},{1,73},{9,65},{65,9},{73,1},{2,74},{10... | collective-permute-start | bytes 442376 | tf_op jit(solution)/shard_map/ppermute | solution.py:26
  14.4 4.2 %collective-permute-start.6 = (s32[2,8,128]{2,1,0:T(8,128)S(1)}, s32[2,8,128]{2,1,0:T(8,128)S(1)}, u32[]{:S(2)}, u32[]{:S(2)}) collective-permute-start(s32[2,8,128]{2,1,0:T(8,128)S(1)} %add_add_fusion.1), channel_id=1, source_target_pairs={{0,12},{4,8},{8,4},{12,0},{1,13},{5,9},{9,5},{13,1},{2,14},{6,10},... | collective-permute-start | bytes 24584 | tf_op jit(solution)/shard_map/ppermute | solution.py:26
  15.6 3.1 %collective-permute-start.4 = (s32[2,8,128]{2,1,0:T(8,128)S(1)}, s32[2,8,128]{2,1,0:T(8,128)S(1)}, u32[]{:S(2)}, u32[]{:S(2)}) collective-permute-start(s32[2,8,128]{2,1,0:T(8,128)S(1)} %add_add_fusion.1), channel_id=1, source_target_pairs={{0,4},{4,0},{8,12},{12,8},{1,5},{5,1},{9,13},{13,9},{2,6},{6,2},{1... | collective-permute-start | bytes 24584 | tf_op jit(solution)/shard_map/ppermute | solution.py:26
  16.3 2.3 %collective-permute-start.5 = (s32[2,8,128]{2,1,0:T(8,128)S(1)}, s32[2,8,128]{2,1,0:T(8,128)S(1)}, u32[]{:S(2)}, u32[]{:S(2)}) collective-permute-start(s32[2,8,128]{2,1,0:T(8,128)S(1)} %add_add_fusion.1), channel_id=1, source_target_pairs={{0,8},{4,12},{8,0},{12,4},{1,9},{5,13},{9,1},{13,5},{2,10},{6,14},... | collective-permute-start | bytes 24584 | tf_op jit(solution)/shard_map/ppermute | solution.py:26
  18.7 10.5 %collective-permute-start.3 = (bf16[784,512]{1,0:T(8,128)(2,1)S(1)}, bf16[784,512]{1,0:T(8,128)(2,1)}, u32[]{:S(2)}, u32[]{:S(2)}) collective-permute-start(bf16[784,512]{1,0:T(8,128)(2,1)S(1)} %maximum_maximum_fusion), channel_id=1, source_target_pairs={{0,8},{8,0},{1,9},{9,1},{2,10},{10,2},{3,11},{11,3},{4,12},{12,4},... | collective-permute-start | bytes 2408456 | tf_op jit(solution)/shard_map/ppermute | solution.py:26
  19.5 6.1 %collective-permute-start.10 = (bf16[2,144,256]{2,1,0:T(8,128)(2,1)S(1)}, bf16[2,144,256]{2,1,0:T(8,128)(2,1)S(1)}, u32[]{:S(2)}, u32[]{:S(2)}) collective-permute-start(bf16[2,144,256]{2,1,0:T(8,128)(2,1)S(1)} %get-tuple-element.78), channel_id=1, source_target_pairs={{0,64},{64,0},{1,65},{65,1},{2,66},{66,2},{3,67},{67,3},{4,68},{68... | collective-permute-start | bytes 442376 | tf_op jit(solution)/shard_map/ppermute | solution.py:26
  22.1 14.1 %collective-permute-start.8 = (bf16[4,144,256]{2,1,0:T(8,128)(2,1)}, bf16[4,144,256]{2,1,0:T(8,128)(2,1)}, u32[]{:S(2)}, u32[]{:S(2)}) collective-permute-start(bf16[4,144,256]{2,1,0:T(8,128)(2,1)} %pad_maximum_fusion.1), channel_id=1, source_target_pairs={{0,1},{1,2},{2,3},{3,0},{4,5},{5,6},{6,7},{7,4},{8,9},{9,10},{10,1... | collective-permute-start | bytes 884744 | tf_op jit(solution)/shard_map/ppermute | solution.py:22
  22.4 13.8 %collective-permute-start.9 = (bf16[4,144,256]{2,1,0:T(8,128)(2,1)}, bf16[4,144,256]{2,1,0:T(8,128)(2,1)}, u32[]{:S(2)}, u32[]{:S(2)}) collective-permute-start(bf16[4,144,256]{2,1,0:T(8,128)(2,1)} %pad_maximum_fusion.1), channel_id=1, source_target_pairs={{0,3},{1,0},{2,1},{3,2},{4,7},{5,4},{6,5},{7,6},{8,11},{9,8},{10,9... | collective-permute-start | bytes 884744 | tf_op jit(solution)/shard_map/ppermute | solution.py:22
  26.4 9.8 %collective-permute-start.12 = (bf16[4,144,256]{2,1,0:T(8,128)(2,1)}, bf16[4,144,256]{2,1,0:T(8,128)(2,1)}, u32[]{:S(2)}, u32[]{:S(2)}) collective-permute-start(bf16[4,144,256]{2,1,0:T(8,128)(2,1)} %pad_maximum_fusion.2), channel_id=1, source_target_pairs={{0,16},{16,32},{32,48},{48,0},{1,17},{17,33},{33,49},{49,1},{2,18}... | collective-permute-start | bytes 884744 | tf_op jit(solution)/shard_map/ppermute | solution.py:22
  27.7 8.5 %collective-permute-start.13 = (bf16[4,144,256]{2,1,0:T(8,128)(2,1)}, bf16[4,144,256]{2,1,0:T(8,128)(2,1)}, u32[]{:S(2)}, u32[]{:S(2)}) collective-permute-start(bf16[4,144,256]{2,1,0:T(8,128)(2,1)} %pad_maximum_fusion.2), channel_id=1, source_target_pairs={{0,48},{16,0},{32,16},{48,32},{1,49},{17,1},{33,17},{49,33},{2,50}... | collective-permute-start | bytes 884744 | tf_op jit(solution)/shard_map/ppermute | solution.py:22
  32.1 34.1 %all-to-all-start = ((bf16[8,112,512]{2,1,0:T(8,128)(2,1)}), bf16[8,112,512]{2,1,0:T(8,128)(2,1)S(1)}, u32[]{:S(2)}, u32[]{:S(2)}) async-start(bf16[8,112,512]{2,1,0:T(8,128)(2,1)} %pad_maximum_fusion), calls=%async_computation | async-start | bytes 1835008 | tf_op jit(solution)/shard_map/all_to_all | solution.py:324
  38.9 11.1 %collective-permute-start.14 = (bf16[2,144,256]{2,1,0:T(8,128)(2,1)S(1)}, bf16[2,144,256]{2,1,0:T(8,128)(2,1)S(1)}, u32[]{:S(2)}, u32[]{:S(2)}) collective-permute-start(bf16[2,144,256]{2,1,0:T(8,128)(2,1)S(1)} %slice.51), channel_id=1, source_target_pairs={{0,1},{1,2},{2,3},{3,0},{4,5},{5,6},{6,7},{7,4},{8,9},{9,10},{10,1... | collective-permute-start | bytes 442376 | tf_op jit(solution)/shard_map/ppermute | solution.py:22
  40.1 9.9 %collective-permute-start.15 = (bf16[2,144,256]{2,1,0:T(8,128)(2,1)S(1)}, bf16[2,144,256]{2,1,0:T(8,128)(2,1)S(1)}, u32[]{:S(2)}, u32[]{:S(2)}) collective-permute-start(bf16[2,144,256]{2,1,0:T(8,128)(2,1)S(1)} %slice.52), channel_id=1, source_target_pairs={{0,3},{1,0},{2,1},{3,2},{4,7},{5,4},{6,5},{7,6},{8,11},{9,8},{10,9... | collective-permute-start | bytes 442376 | tf_op jit(solution)/shard_map/ppermute | solution.py:22
  43.5 9.3 %collective-permute-start.16 = (bf16[2,144,256]{2,1,0:T(8,128)(2,1)S(1)}, bf16[2,144,256]{2,1,0:T(8,128)(2,1)S(1)}, u32[]{:S(2)}, u32[]{:S(2)}) collective-permute-start(bf16[2,144,256]{2,1,0:T(8,128)(2,1)S(1)} %slice.53), channel_id=1, source_target_pairs={{0,16},{16,32},{32,48},{48,0},{1,17},{17,33},{33,49},{49,1},{2,18}... | collective-permute-start | bytes 442376 | tf_op jit(solution)/shard_map/ppermute | solution.py:22
  45.9 6.8 %collective-permute-start.17 = (bf16[2,144,256]{2,1,0:T(8,128)(2,1)S(1)}, bf16[2,144,256]{2,1,0:T(8,128)(2,1)S(1)}, u32[]{:S(2)}, u32[]{:S(2)}) collective-permute-start(bf16[2,144,256]{2,1,0:T(8,128)(2,1)S(1)} %slice.54), channel_id=1, source_target_pairs={{0,48},{16,0},{32,16},{48,32},{1,49},{17,1},{33,17},{49,33},{2,50}... | collective-permute-start | bytes 442376 | tf_op jit(solution)/shard_map/ppermute | solution.py:22
  48.2 15.2 %copy-start.9 = (f32[16,32]{1,0:T(8,128)S(1)}, f32[16,32]{1,0:T(8,128)}, u32[]{:S(2)}) copy-start(f32[16,32]{1,0:T(8,128)} %param.17) | copy-start | bytes 6148
  48.2 15.2 %copy-start.10 = (f32[16,32]{1,0:T(8,128)S(1)}, f32[16,32]{1,0:T(8,128)}, u32[]{:S(2)}) copy-start(f32[16,32]{1,0:T(8,128)} %param.16) | copy-start | bytes 6148
  50.0 3.4 %copy-start.4 = (bf16[16,144,256]{2,1,0:T(8,128)(2,1)}, bf16[16,144,256]{2,1,0:T(8,128)(2,1)S(1)}, u32[]{:S(2)}) copy-start(bf16[16,144,256]{2,1,0:T(8,128)(2,1)S(1)} %get-tuple-element.86) | copy-start | bytes 3538948
  54.1 28.9 %collective-permute-start.18 = (bf16[16,144,256]{2,1,0:T(8,128)(2,1)}, bf16[16,144,256]{2,1,0:T(8,128)(2,1)S(1)}, u32[]{:S(2)}, u32[]{:S(2)}) collective-permute-start(bf16[16,144,256]{2,1,0:T(8,128)(2,1)} %constant_dynamic-update-slice_fusion.refs_0_), channel_id=1, source_target_pairs={{0,16},{16,32},{32,48},{48,0},{1,17},{17,33},{33,49},{49,1},{2,18}... | collective-permute-start | bytes 3538952 | tf_op jit(solution)/shard_map/ppermute | solution.py:22
  54.1 28.9 %collective-permute-start.19 = (bf16[16,144,256]{2,1,0:T(8,128)(2,1)}, bf16[16,144,256]{2,1,0:T(8,128)(2,1)S(1)}, u32[]{:S(2)}, u32[]{:S(2)}) collective-permute-start(bf16[16,144,256]{2,1,0:T(8,128)(2,1)} %constant_dynamic-update-slice_fusion.refs_0_), channel_id=1, source_target_pairs={{0,48},{16,0},{32,16},{48,32},{1,49},{17,1},{33,17},{49,33},{2,50}... | collective-permute-start | bytes 3538952 | tf_op jit(solution)/shard_map/ppermute | solution.py:22
  58.1 26.7 %collective-permute-start.20 = (bf16[16,144,256]{2,1,0:T(8,128)(2,1)}, bf16[16,144,256]{2,1,0:T(8,128)(2,1)}, u32[]{:S(2)}, u32[]{:S(2)}) collective-permute-start(bf16[16,144,256]{2,1,0:T(8,128)(2,1)} %constant_dynamic-update-slice_fusion.6.refs_2_), channel_id=1, source_target_pairs={{0,1},{1,2},{2,3},{3,0},{4,5},{5,6},{6,7},{7,4},{8,9},{9,10},{10,1... | collective-permute-start | bytes 3538952 | tf_op jit(solution)/shard_map/ppermute | solution.py:22
  58.5 26.3 %collective-permute-start.21 = (bf16[16,144,256]{2,1,0:T(8,128)(2,1)}, bf16[16,144,256]{2,1,0:T(8,128)(2,1)}, u32[]{:S(2)}, u32[]{:S(2)}) collective-permute-start(bf16[16,144,256]{2,1,0:T(8,128)(2,1)} %constant_dynamic-update-slice_fusion.6.refs_2_), channel_id=1, source_target_pairs={{0,3},{1,0},{2,1},{3,2},{4,7},{5,4},{6,5},{7,6},{8,11},{9,8},{10,9... | collective-permute-start | bytes 3538952 | tf_op jit(solution)/shard_map/ppermute | solution.py:22
  66.2 1.2 copy-start.1
  67.4 0.9 copy-start.2
  68.3 0.9 copy-start.3
  78.0 33.2 %all-to-all-start.1 = ((bf16[32,32,512]{2,1,0:T(8,128)(2,1)}), bf16[32,32,512]{2,1,0:T(8,128)(2,1)S(1)}, u32[]{:S(2)}, u32[]{:S(2)}) async-start(bf16[32,32,512]{2,1,0:T(8,128)(2,1)} %bitcast.15), calls=%async_computation.1 | async-start | bytes 2097152 | tf_op jit(solution)/shard_map/all_to_all | solution.py:333
  85.8 25.4 %collective-permute-start.23 = (bf16[8,144,256]{2,1,0:T(8,128)(2,1)}, bf16[8,144,256]{2,1,0:T(8,128)(2,1)}, u32[]{:S(2)}, u32[]{:S(2)}) collective-permute-start(bf16[8,144,256]{2,1,0:T(8,128)(2,1)} %slice.55), channel_id=1, source_target_pairs={{0,16},{16,32},{32,48},{48,0},{1,17},{17,33},{33,49},{49,1},{2,18}... | collective-permute-start | bytes 1769480 | tf_op jit(solution)/shard_map/ppermute | solution.py:22
  86.7 24.5 %collective-permute-start.24 = (bf16[8,144,256]{2,1,0:T(8,128)(2,1)}, bf16[8,144,256]{2,1,0:T(8,128)(2,1)}, u32[]{:S(2)}, u32[]{:S(2)}) collective-permute-start(bf16[8,144,256]{2,1,0:T(8,128)(2,1)} %slice.56), channel_id=1, source_target_pairs={{0,48},{16,0},{32,16},{48,32},{1,49},{17,1},{33,17},{49,33},{2,50}... | collective-permute-start | bytes 1769480 | tf_op jit(solution)/shard_map/ppermute | solution.py:22
  91.3 19.9 %collective-permute-start.25 = (bf16[8,144,256]{2,1,0:T(8,128)(2,1)}, bf16[8,144,256]{2,1,0:T(8,128)(2,1)}, u32[]{:S(2)}, u32[]{:S(2)}) collective-permute-start(bf16[8,144,256]{2,1,0:T(8,128)(2,1)} %slice.57), channel_id=1, source_target_pairs={{0,1},{1,2},{2,3},{3,0},{4,5},{5,6},{6,7},{7,4},{8,9},{9,10},{10,1... | collective-permute-start | bytes 1769480 | tf_op jit(solution)/shard_map/ppermute | solution.py:22
  94.4 16.8 %collective-permute-start.26 = (bf16[8,144,256]{2,1,0:T(8,128)(2,1)}, bf16[8,144,256]{2,1,0:T(8,128)(2,1)}, u32[]{:S(2)}, u32[]{:S(2)}) collective-permute-start(bf16[8,144,256]{2,1,0:T(8,128)(2,1)} %slice.58), channel_id=1, source_target_pairs={{0,3},{1,0},{2,1},{3,2},{4,7},{5,4},{6,5},{7,6},{8,11},{9,8},{10,9... | collective-permute-start | bytes 1769480 | tf_op jit(solution)/shard_map/ppermute | solution.py:22
  111.2 1.3 copy-start.5
  118.4 6.0 %collective-permute-start.27 = (bf16[5,512,256]{2,1,0:T(8,128)(2,1)S(1)}, bf16[5,512,256]{2,1,0:T(8,128)(2,1)S(1)}, u32[]{:S(2)}, u32[]{:S(2)}) collective-permute-start(bf16[5,512,256]{2,1,0:T(8,128)(2,1)S(1)} %get-tuple-element.53), channel_id=1, source_target_pairs={{0,8},{8,0},{1,9},{9,1},{2,10},{10,2},{3,11},{11,3},{4,12},{12,4},... | collective-permute-start | bytes 3932168 | tf_op jit(solution)/shard_map/ppermute | solution.py:26
  124.3 2.4 %collective-permute-start.22 = (bf16[3,512,256]{2,1,0:T(8,128)(2,1)S(1)}, bf16[3,512,256]{2,1,0:T(8,128)(2,1)S(1)}, u32[]{:S(2)}, u32[]{:S(2)}) collective-permute-start(bf16[3,512,256]{2,1,0:T(8,128)(2,1)S(1)} %get-tuple-element.44), channel_id=1, source_target_pairs={{0,8},{8,0},{1,9},{9,1},{2,10},{10,2},{3,11},{11,3},{4,12},{12,4},... | collective-permute-start | bytes 2359304 | tf_op jit(solution)/shard_map/ppermute | solution.py:26
  125.3 24.3 %collective-permute-start.29 = (bf16[5,512,128]{2,1,0:T(8,128)(2,1)S(1)}, bf16[5,512,128]{2,1,0:T(8,128)(2,1)S(1)}, u32[]{:S(2)}, u32[]{:S(2)}) collective-permute-start(bf16[5,512,128]{2,1,0:T(8,128)(2,1)S(1)} %get-tuple-element.56), channel_id=1, source_target_pairs={{0,4},{4,0},{1,5},{5,1},{2,6},{6,2},{3,7},{7,3},{8,12},{12,8},{9,1... | collective-permute-start | bytes 1966088 | tf_op jit(solution)/shard_map/ppermute | solution.py:26
  127.4 22.2 %collective-permute-start.28 = (bf16[3,512,128]{2,1,0:T(8,128)(2,1)S(1)}, bf16[3,512,128]{2,1,0:T(8,128)(2,1)S(1)}, u32[]{:S(2)}, u32[]{:S(2)}) collective-permute-start(bf16[3,512,128]{2,1,0:T(8,128)(2,1)S(1)} %get-tuple-element.55), channel_id=1, source_target_pairs={{0,4},{4,0},{1,5},{5,1},{2,6},{6,2},{3,7},{7,3},{8,12},{12,8},{9,1... | collective-permute-start | bytes 1179656 | tf_op jit(solution)/shard_map/ppermute | solution.py:26

commit v5 on v4

--- a/solution.py
+++ b/solution.py
@@ -103,7 +103,7 @@
                     query[g, b, rows, :] = f[16 * g : 16 * g + 16, cols]
         return carry
 
-    lax.fori_loop(0, 8, one_pair, 0)
+    lax.fori_loop(0, 8, one_pair, 0, unroll=4)
 
     for g in range(2):
         for b in range(4):

time: 153 us -> 153 us (level)
  no operation moved by 1% of the time
where the time goes in v5:
time: 153 us; the launch traced here: 152 us
  starting transfers between devices  47.9 us (31%)
  waiting for transfers between devices  44.3 us (29%)
  local copies, waits for them, and re-layouts  27.3 us (18%)
  Pallas kernels  23.4 us (15%)
  other arithmetic  7.52 us (5%)
    ppermute x19, starting transfers between devices, shift(): return lax.ppermute(value, axis, [(i, (i + step) % 4) for i in range(4)])  26.7 us
    ppermute x11, waiting for transfers between devices, flip(): return lax.ppermute(value, axes, [(i, i ^ bits) for i in range(size)])  25 us
    ppermute x19, waiting for transfers between devices, shift(): return lax.ppermute(value, axis, [(i, (i + step) % 4) for i in range(4)])  19.3 us
    ppermute x11, starting transfers between devices, flip(): return lax.ppermute(value, axes, [(i, i ^ bits) for i in range(size)])  12.1 us
    unnamed x31, local copies, waits for them, and re-layouts  10.2 us
    pallas_call x2, Pallas kernels, project(): pl.pallas_call(functools.partial(project_kernel, count, block), out_shape...  9.43 us
    pallas_call x1, Pallas kernels, mixer(): pl.pallas_call(mixer_kernel, out_shape=jax.ShapeDtypeStruct((4, 8, 32, 51...  8.31 us
    all_to_all x1, starting transfers between devices, body(): lax.all_to_all(gated.reshape(32, 32, 512), ('x', 'zh', 'y'), split_axis=0...  5.04 us
  transfers between devices with their start and end apart: 32, of which 7 were waited for; matrix products, arithmetic and copies ran while one was open for 20% of the time, Pallas kernels for 10%

profile of v5, /device:TPU:1, one launch (start us, length us, event | category | flops | bytes accessed | tf_op | source)
XLA Modules:
  0.0 151.6 jit_solution(16311663448842130911)
XLA Ops:
  0.1 0.8 and_select_fusion
  0.9 3.6 %collective-permute-start.2 = (s32[2,8,128]{2,1,0:T(8,128)S(1)}, s32[2,8,128]{2,1,0:T(8,128)S(1)}, u32[]{:S(2)}, u32[]{:S(2)}) collective-permute-start(s32[2,8,128]{2,1,0:T(8,128)S(1)} %and_select_fusion), channel_id=1, source_target_pairs={{0,2},{1,3},{2,0},{3,1},{4,6},{5,7},{6,4},{7,5},{8,10},{9,11},{10,... | collective-permute-start | bytes 24584 | tf_op jit(solution)/shard_map/ppermute | solution.py:22
  4.5 0.9 collective-permute-start.1
  5.9 0.7 constant_dynamic-slice_fusion.2
  6.7 1.0 constant_dynamic-slice_fusion.3
  8.3 1.5 collective-permute-start.7
  9.8 3.5 %collective-permute-start.11 = (bf16[2,144,256]{2,1,0:T(8,128)(2,1)}, bf16[2,144,256]{2,1,0:T(8,128)(2,1)S(1)}, u32[]{:S(2)}, u32[]{:S(2)}) collective-permute-start(bf16[2,144,256]{2,1,0:T(8,128)(2,1)} %pad_maximum_fusion.4), channel_id=1, source_target_pairs={{0,72},{8,64},{64,8},{72,0},{1,73},{9,65},{65,9},{73,1},{2,74},{10... | collective-permute-start | bytes 442376 | tf_op jit(solution)/shard_map/ppermute | solution.py:26
  14.4 1.2 collective-permute-start.6
  15.6 0.7 collective-permute-start.4
  17.8 0.9 collective-permute-done.6
  18.7 0.7 constant_dynamic-update-slice_fusion.5
  19.5 1.2 collective-permute-start.10
  20.6 0.7 constant_dynamic-update-slice_fusion.4
  21.3 0.7 pad_maximum_fusion.1
  22.4 2.4 %collective-permute-start.9 = (bf16[4,144,256]{2,1,0:T(8,128)(2,1)}, bf16[4,144,256]{2,1,0:T(8,128)(2,1)}, u32[]{:S(2)}, u32[]{:S(2)}) collective-permute-start(bf16[4,144,256]{2,1,0:T(8,128)(2,1)} %pad_maximum_fusion.1), channel_id=1, source_target_pairs={{0,3},{1,0},{2,1},{3,2},{4,7},{5,4},{6,5},{7,6},{8,11},{9,8},{10,9... | collective-permute-start | bytes 884744 | tf_op jit(solution)/shard_map/ppermute | solution.py:22
  24.8 0.8 collective-permute-done.10
  25.7 0.8 pad_maximum_fusion.2
  26.4 1.3 collective-permute-start.12
  27.7 1.4 collective-permute-start.13
  29.2 1.3 convert_element_type.21
  31.1 1.0 pad_maximum_fusion
  32.1 4.1 %all-to-all-start = ((bf16[8,112,512]{2,1,0:T(8,128)(2,1)}), bf16[8,112,512]{2,1,0:T(8,128)(2,1)S(1)}, u32[]{:S(2)}, u32[]{:S(2)}) async-start(bf16[8,112,512]{2,1,0:T(8,128)(2,1)} %pad_maximum_fusion), calls=%async_computation | async-start | bytes 1835008 | tf_op jit(solution)/shard_map/all_to_all | solution.py:324
  36.2 0.9 slice.51
  37.2 1.7 %constant_dynamic-update-slice_fusion.3 = bf16[16,144,256]{2,1,0:T(8,128)(2,1)} fusion(bf16[16,144,256]{2,1,0:T(8,128)(2,1)} %get-tuple-element.61, bf16[4,144,256]{2,1,0:T(8,128)(2,1)} %collective-permute-done.8), kind=kLoop, calls=%fused_computation.21 | loop fusion | bytes 589824
  39.2 0.9 slice.52
  40.1 2.4 %collective-permute-start.15 = (bf16[2,144,256]{2,1,0:T(8,128)(2,1)S(1)}, bf16[2,144,256]{2,1,0:T(8,128)(2,1)S(1)}, u32[]{:S(2)}, u32[]{:S(2)}) collective-permute-start(bf16[2,144,256]{2,1,0:T(8,128)(2,1)S(1)} %slice.52), channel_id=1, source_target_pairs={{0,3},{1,0},{2,1},{3,2},{4,7},{5,4},{6,5},{7,6},{8,11},{9,8},{10,9... | collective-permute-start | bytes 442376 | tf_op jit(solution)/shard_map/ppermute | solution.py:22
  42.5 0.9 slice.53
  43.5 1.5 %collective-permute-start.16 = (bf16[2,144,256]{2,1,0:T(8,128)(2,1)S(1)}, bf16[2,144,256]{2,1,0:T(8,128)(2,1)S(1)}, u32[]{:S(2)}, u32[]{:S(2)}) collective-permute-start(bf16[2,144,256]{2,1,0:T(8,128)(2,1)S(1)} %slice.53), channel_id=1, source_target_pairs={{0,16},{16,32},{32,48},{48,0},{1,17},{17,33},{33,49},{49,1},{2,18}... | collective-permute-start | bytes 442376 | tf_op jit(solution)/shard_map/ppermute | solution.py:22
  45.0 0.9 slice.54
  45.9 1.3 collective-permute-start.17
  47.2 1.0 constant_dynamic-update-slice_fusion.9
  48.2 1.8 %constant_dynamic-update-slice_fusion.2 = (bf16[16,144,256]{2,1,0:T(8,128)(2,1)}, bf16[16,144,256]{2,1,0:T(8,128)(2,1)S(1)}) fusion(bf16[16,144,256]{2,1,0:T(8,128)(2,1)} %constant_dynamic-update-slice_fusion.3, bf16[4,144,256]{2,1,0:T(8,128)(2,1)} %collective-permute-done.9, bf16[16,144,256]{2,1,0:T(8,128)(2,1)S(1)} %constant_dynamic-update-slice_fusion.9, ...), kind=kLoop, calls=%fused_computation.20 | loop fusion | bytes 1179648
  50.0 2.7 %collective-permute-done.16 = bf16[2,144,256]{2,1,0:T(8,128)(2,1)S(1)} collective-permute-done((bf16[2,144,256]{2,1,0:T(8,128)(2,1)S(1)}, bf16[2,144,256]{2,1,0:T(8,128)(2,1)S(1)}, u32[]{:S(2)}, u32[]{:S(2)}) %collective-permute-start.16) | collective-permute-done | bytes 147488 | tf_op jit(solution)/shard_map/ppermute | solution.py:22
  52.8 0.7 constant_dynamic-update-slice_fusion.1
  53.4 0.7 constant_dynamic-update-slice_fusion.refs_0_
  54.1 2.7 %collective-permute-start.19 = (bf16[16,144,256]{2,1,0:T(8,128)(2,1)}, bf16[16,144,256]{2,1,0:T(8,128)(2,1)S(1)}, u32[]{:S(2)}, u32[]{:S(2)}) collective-permute-start(bf16[16,144,256]{2,1,0:T(8,128)(2,1)} %constant_dynamic-update-slice_fusion.refs_0_), channel_id=1, source_target_pairs={{0,48},{16,0},{32,16},{48,32},{1,49},{17,1},{33,17},{49,33},{2,50}... | collective-permute-start | bytes 3538952 | tf_op jit(solution)/shard_map/ppermute | solution.py:22
  58.5 2.3 %collective-permute-start.21 = (bf16[16,144,256]{2,1,0:T(8,128)(2,1)}, bf16[16,144,256]{2,1,0:T(8,128)(2,1)}, u32[]{:S(2)}, u32[]{:S(2)}) collective-permute-start(bf16[16,144,256]{2,1,0:T(8,128)(2,1)} %constant_dynamic-update-slice_fusion.6.refs_2_), channel_id=1, source_target_pairs={{0,3},{1,0},{2,1},{3,2},{4,7},{5,4},{6,5},{7,6},{8,11},{9,8},{10,9... | collective-permute-start | bytes 3538952 | tf_op jit(solution)/shard_map/ppermute | solution.py:22
  60.9 0.8 reshape.113.taps
  61.7 0.8 dynamic_slice.41
  62.5 0.9 reshape.114.skip
  64.1 2.1 %filters.1.toep = bf16[2,4,256,256]{3,2,1,0:T(8,128)(2,1)} custom-call(f32[16,2]{1,0:T(8,128)} %get-tuple-element.84.decay, f32[16,2]{1,0:T(8,128)} %get-tuple-element.83.residue), custom_call_target="tpu_custom_call" | custom-call | tf_op jit(solution)/shard_map/filters/pallas_call | solution.py:62
  66.2 1.2 copy-done.1
  67.4 0.9 copy-done.2
  68.3 0.9 copy-done.3
  69.3 8.3 %mixer.1 = bf16[4,8,32,512]{3,2,1,0:T(8,128)(2,1)} custom-call(bf16[8,112,512]{2,1,0:T(8,128)(2,1)S(1)} %all-to-all-done.recv, f32[3,96,1]{2,1,0:T(8,128)S(1)} %copy-done.3, f32[2,256,1]{2,1,0:T(8,128)S(1)} %copy-done.2, bf16[2,4,256,256]{3,2,1,0:T(8,128)(2,1)S(1)} %copy-done.1), custom_call_target="tpu_custom_call" | custom-call | flops 1610612736 | bytes 4194304 | tf_op jit(solution)/shard_map/mixer/pallas_call | solution.py:125
  77.6 5.0 %all-to-all-start.1 = ((bf16[32,32,512]{2,1,0:T(8,128)(2,1)}), bf16[32,32,512]{2,1,0:T(8,128)(2,1)S(1)}, u32[]{:S(2)}, u32[]{:S(2)}) async-start(bf16[32,32,512]{2,1,0:T(8,128)(2,1)} %bitcast.15), calls=%async_computation.1 | async-start | bytes 2097152 | tf_op jit(solution)/shard_map/all_to_all | solution.py:333
  82.6 2.2 %collective-permute-done.20.refs_3_ = bf16[16,144,256]{2,1,0:T(8,128)(2,1)} collective-permute-done((bf16[16,144,256]{2,1,0:T(8,128)(2,1)}, bf16[16,144,256]{2,1,0:T(8,128)(2,1)}, u32[]{:S(2)}, u32[]{:S(2)}) %collective-permute-start.20) | collective-permute-done | bytes 1179680 | tf_op jit(solution)/shard_map/ppermute | solution.py:22
  84.9 0.9 slice.55
  85.8 0.9 slice.56
  86.7 2.7 %collective-permute-start.24 = (bf16[8,144,256]{2,1,0:T(8,128)(2,1)}, bf16[8,144,256]{2,1,0:T(8,128)(2,1)}, u32[]{:S(2)}, u32[]{:S(2)}) collective-permute-start(bf16[8,144,256]{2,1,0:T(8,128)(2,1)} %slice.56), channel_id=1, source_target_pairs={{0,48},{16,0},{32,16},{48,32},{1,49},{17,1},{33,17},{49,33},{2,50}... | collective-permute-start | bytes 1769480 | tf_op jit(solution)/shard_map/ppermute | solution.py:22
  89.4 1.9 %slice.57 = bf16[8,144,256]{2,1,0:T(8,128)(2,1)} slice(bf16[16,144,256]{2,1,0:T(8,128)(2,1)} %collective-permute-done.20.refs_3_), slice={[0:8], [0:144], [0:256]} | slice | bytes 1179648 | tf_op jit(solution)/shard_map/slice | solution.py:37
  91.3 1.2 collective-permute-start.25
  92.5 1.9 %slice.58 = bf16[8,144,256]{2,1,0:T(8,128)(2,1)} slice(bf16[16,144,256]{2,1,0:T(8,128)(2,1)} %collective-permute-done.21.refs_4_), slice={[8:16], [0:144], [0:256]} | slice | bytes 1179648 | tf_op jit(solution)/shard_map/slice | solution.py:37
  94.4 1.5 collective-permute-start.26
  96.0 14.3 %collective-permute-done.23.refs_0_ = bf16[8,144,256]{2,1,0:T(8,128)(2,1)} collective-permute-done((bf16[8,144,256]{2,1,0:T(8,128)(2,1)}, bf16[8,144,256]{2,1,0:T(8,128)(2,1)}, u32[]{:S(2)}, u32[]{:S(2)}) %collective-permute-start.23) | collective-permute-done | bytes 589856 | tf_op jit(solution)/shard_map/ppermute | solution.py:22
  110.3 1.3 copy-done.5
  111.6 5.9 %back.1 = (f32[5,512,256]{2,1,0:T(8,128)S(1)}, bf16[5,512,256]{2,1,0:T(8,128)(2,1)S(1)}) custom-call(s32[5]{0:T(128)S(1)} %stack.31.where, bf16[4,256,512]{2,1,0:T(8,128)(2,1)S(1)} %bitcast.38, s32[1,512]{1,0:T(1,128)S(1)} %bitcast.40, bf16[8,144,256]{2,1,0:T(8,128)(2,1)} %collective-permute-done.23.refs_0_, ...), custom_call_target="tpu_custom_call" | custom-call | flops 2684354560 | bytes 15728640 | tf_op jit(solution)/shard_map/back/pallas_call | solution.py:184
  117.5 3.3 %collective-permute-start.27 = (bf16[5,512,256]{2,1,0:T(8,128)(2,1)S(1)}, bf16[5,512,256]{2,1,0:T(8,128)(2,1)S(1)}, u32[]{:S(2)}, u32[]{:S(2)}) collective-permute-start(bf16[5,512,256]{2,1,0:T(8,128)(2,1)S(1)} %get-tuple-element.53), channel_id=1, source_target_pairs={{0,8},{8,0},{1,9},{9,1},{2,10},{10,2},{3,11},{11,3},{4,12},{12,4},... | collective-permute-start | bytes 3932168 | tf_op jit(solution)/shard_map/ppermute | solution.py:26
  120.8 3.5 %front.1 = (f32[3,512,256]{2,1,0:T(8,128)S(1)}, bf16[3,512,256]{2,1,0:T(8,128)(2,1)S(1)}) custom-call(s32[5]{0:T(128)S(1)} %stack.31.where, bf16[4,256,512]{2,1,0:T(8,128)(2,1)S(1)} %bitcast.39, s32[1,512]{1,0:T(1,128)S(1)} %bitcast.41, bf16[16,144,256]{2,1,0:T(8,128)(2,1)} %constant_dynamic-update-slice_fusion.refs_0_, ...), custom_call_target="tpu_custom_call" | custom-call | flops 1610612736 | bytes 9437184 | tf_op jit(solution)/shard_map/front/pallas_call | solution.py:184
  124.5 0.9 merge.3
  125.4 1.3 collective-permute-done.22.theirs
  126.7 0.7 merge.2
  127.7 22.0 %collective-permute-done.28.got0 = bf16[3,512,128]{2,1,0:T(8,128)(2,1)S(1)} collective-permute-done((bf16[3,512,128]{2,1,0:T(8,128)(2,1)S(1)}, bf16[3,512,128]{2,1,0:T(8,128)(2,1)S(1)}, u32[]{:S(2)}, u32[]{:S(2)}) %collective-permute-start.28) | collective-permute-done | bytes 393248 | tf_op jit(solution)/shard_map/ppermute | solution.py:26
  149.6 2.0 %finish.1 = bf16[128,4096]{1,0:T(8,128)(2,1)} custom-call(s32[5]{0:T(128)S(1)} %stack.31.where, s32[32]{0:T(128)S(1)} %copy-done.6, f32[3,512,128]{2,1,0:T(8,128)S(1)} %get-tuple-element.45.keep0, f32[5,512,128]{2,1,0:T(8,128)S(1)} %get-tuple-element.54.keep1, bf16[3,512,128]{2,1,0:T(8,128)(2,1)S(1)} %collective-permute-done.28.got0, ...), custom_call_target="tpu_custom_call" | custom-call | tf_op jit(solution)/shard_map/finish/pallas_call | solution.py:242
  (97 shorter events, 8.2 us)
Async XLA Ops:
  0.0 60.8 %copy-start = (f32[3,3,512]{2,1,0:T(4,128)S(1)}, f32[3,3,512]{2,1,0:T(4,128)}, u32[]{:S(2)}) copy-start(f32[3,3,512]{2,1,0:T(4,128)} %param.15) | copy-start | bytes 55300
  0.0 14.4 %copy-start.12 = (s32[1,128]{1,0:T(1,128)S(1)}, s32[1,128]{1,0:T(1,128)}, u32[]{:S(2)}) copy-start(s32[1,128]{1,0:T(1,128)} %param.10) | copy-start | bytes 1540
  0.0 13.3 %copy-start.7 = (bf16[2,512,128]{2,1,0:T(8,128)(2,1)S(1)}, bf16[2,512,128]{2,1,0:T(8,128)(2,1)}, u32[]{:S(2)}) copy-start(bf16[2,512,128]{2,1,0:T(8,128)(2,1)} %param.12) | copy-start | bytes 786436
  0.0 13.5 %copy-start.6 = (s32[32]{0:T(128)S(1)}, s32[32]{0:T(128)}, u32[]{:S(2)}) copy-start(s32[32]{0:T(128)} %bucket.1) | copy-start | bytes 388
  0.0 13.6 %copy-start.11 = (f32[4096]{0:T(1024)S(1)}, f32[4096]{0:T(1024)}, u32[]{:S(2)}) copy-start(f32[4096]{0:T(1024)} %param.13) | copy-start | bytes 49156
  0.0 16.6 %copy-start.8 = (bf16[2,128,3,512]{3,1,2,0:T(8,128)(2,1)S(1)}, bf16[2,128,3,512]{3,1,2,0:T(8,128)(2,1)}, u32[]{:S(2)}) copy-start(bf16[2,128,3,512]{3,1,2,0:T(8,128)(2,1)} %param.14) | copy-start | bytes 2359300
  0.9 13.5 %collective-permute-start.2 = (s32[2,8,128]{2,1,0:T(8,128)S(1)}, s32[2,8,128]{2,1,0:T(8,128)S(1)}, u32[]{:S(2)}, u32[]{:S(2)}) collective-permute-start(s32[2,8,128]{2,1,0:T(8,128)S(1)} %and_select_fusion), channel_id=1, source_target_pairs={{0,2},{1,3},{2,0},{3,1},{4,6},{5,7},{6,4},{7,5},{8,10},{9,11},{10,... | collective-permute-start | bytes 24584 | tf_op jit(solution)/shard_map/ppermute | solution.py:22
  4.5 9.9 %collective-permute-start.1 = (s32[2,8,128]{2,1,0:T(8,128)S(1)}, s32[2,8,128]{2,1,0:T(8,128)S(1)}, u32[]{:S(2)}, u32[]{:S(2)}) collective-permute-start(s32[2,8,128]{2,1,0:T(8,128)S(1)} %and_select_fusion), channel_id=1, source_target_pairs={{0,3},{1,0},{2,1},{3,2},{4,7},{5,4},{6,5},{7,6},{8,11},{9,8},{10,9... | collective-permute-start | bytes 24584 | tf_op jit(solution)/shard_map/ppermute | solution.py:22
  5.3 9.0 %collective-permute-start = (s32[2,8,128]{2,1,0:T(8,128)S(1)}, s32[2,8,128]{2,1,0:T(8,128)S(1)}, u32[]{:S(2)}, u32[]{:S(2)}) collective-permute-start(s32[2,8,128]{2,1,0:T(8,128)S(1)} %and_select_fusion), channel_id=1, source_target_pairs={{0,1},{1,2},{2,3},{3,0},{4,5},{5,6},{6,7},{7,4},{8,9},{9,10},{10,1... | collective-permute-start | bytes 24584 | tf_op jit(solution)/shard_map/ppermute | solution.py:22
  8.3 10.4 %collective-permute-start.7 = (bf16[2,144,256]{2,1,0:T(8,128)(2,1)}, bf16[2,144,256]{2,1,0:T(8,128)(2,1)S(1)}, u32[]{:S(2)}, u32[]{:S(2)}) collective-permute-start(bf16[2,144,256]{2,1,0:T(8,128)(2,1)} %pad_maximum_fusion.4), channel_id=1, source_target_pairs={{0,8},{8,0},{1,9},{9,1},{2,10},{10,2},{3,11},{11,3},{4,12},{12,4},... | collective-permute-start | bytes 442376 | tf_op jit(solution)/shard_map/ppermute | solution.py:26
  9.8 14.9 %collective-permute-start.11 = (bf16[2,144,256]{2,1,0:T(8,128)(2,1)}, bf16[2,144,256]{2,1,0:T(8,128)(2,1)S(1)}, u32[]{:S(2)}, u32[]{:S(2)}) collective-permute-start(bf16[2,144,256]{2,1,0:T(8,128)(2,1)} %pad_maximum_fusion.4), channel_id=1, source_target_pairs={{0,72},{8,64},{64,8},{72,0},{1,73},{9,65},{65,9},{73,1},{2,74},{10... | collective-permute-start | bytes 442376 | tf_op jit(solution)/shard_map/ppermute | solution.py:26
  14.4 4.2 %collective-permute-start.6 = (s32[2,8,128]{2,1,0:T(8,128)S(1)}, s32[2,8,128]{2,1,0:T(8,128)S(1)}, u32[]{:S(2)}, u32[]{:S(2)}) collective-permute-start(s32[2,8,128]{2,1,0:T(8,128)S(1)} %add_add_fusion.1), channel_id=1, source_target_pairs={{0,12},{4,8},{8,4},{12,0},{1,13},{5,9},{9,5},{13,1},{2,14},{6,10},... | collective-permute-start | bytes 24584 | tf_op jit(solution)/shard_map/ppermute | solution.py:26
  15.6 3.1 %collective-permute-start.4 = (s32[2,8,128]{2,1,0:T(8,128)S(1)}, s32[2,8,128]{2,1,0:T(8,128)S(1)}, u32[]{:S(2)}, u32[]{:S(2)}) collective-permute-start(s32[2,8,128]{2,1,0:T(8,128)S(1)} %add_add_fusion.1), channel_id=1, source_target_pairs={{0,4},{4,0},{8,12},{12,8},{1,5},{5,1},{9,13},{13,9},{2,6},{6,2},{1... | collective-permute-start | bytes 24584 | tf_op jit(solution)/shard_map/ppermute | solution.py:26
  16.3 2.3 %collective-permute-start.5 = (s32[2,8,128]{2,1,0:T(8,128)S(1)}, s32[2,8,128]{2,1,0:T(8,128)S(1)}, u32[]{:S(2)}, u32[]{:S(2)}) collective-permute-start(s32[2,8,128]{2,1,0:T(8,128)S(1)} %add_add_fusion.1), channel_id=1, source_target_pairs={{0,8},{4,12},{8,0},{12,4},{1,9},{5,13},{9,1},{13,5},{2,10},{6,14},... | collective-permute-start | bytes 24584 | tf_op jit(solution)/shard_map/ppermute | solution.py:26
  18.7 10.5 %collective-permute-start.3 = (bf16[784,512]{1,0:T(8,128)(2,1)S(1)}, bf16[784,512]{1,0:T(8,128)(2,1)}, u32[]{:S(2)}, u32[]{:S(2)}) collective-permute-start(bf16[784,512]{1,0:T(8,128)(2,1)S(1)} %maximum_maximum_fusion), channel_id=1, source_target_pairs={{0,8},{8,0},{1,9},{9,1},{2,10},{10,2},{3,11},{11,3},{4,12},{12,4},... | collective-permute-start | bytes 2408456 | tf_op jit(solution)/shard_map/ppermute | solution.py:26
  19.5 6.1 %collective-permute-start.10 = (bf16[2,144,256]{2,1,0:T(8,128)(2,1)S(1)}, bf16[2,144,256]{2,1,0:T(8,128)(2,1)S(1)}, u32[]{:S(2)}, u32[]{:S(2)}) collective-permute-start(bf16[2,144,256]{2,1,0:T(8,128)(2,1)S(1)} %get-tuple-element.78), channel_id=1, source_target_pairs={{0,64},{64,0},{1,65},{65,1},{2,66},{66,2},{3,67},{67,3},{4,68},{68... | collective-permute-start | bytes 442376 | tf_op jit(solution)/shard_map/ppermute | solution.py:26
  22.1 14.1 %collective-permute-start.8 = (bf16[4,144,256]{2,1,0:T(8,128)(2,1)}, bf16[4,144,256]{2,1,0:T(8,128)(2,1)}, u32[]{:S(2)}, u32[]{:S(2)}) collective-permute-start(bf16[4,144,256]{2,1,0:T(8,128)(2,1)} %pad_maximum_fusion.1), channel_id=1, source_target_pairs={{0,1},{1,2},{2,3},{3,0},{4,5},{5,6},{6,7},{7,4},{8,9},{9,10},{10,1... | collective-permute-start | bytes 884744 | tf_op jit(solution)/shard_map/ppermute | solution.py:22
  22.4 13.8 %collective-permute-start.9 = (bf16[4,144,256]{2,1,0:T(8,128)(2,1)}, bf16[4,144,256]{2,1,0:T(8,128)(2,1)}, u32[]{:S(2)}, u32[]{:S(2)}) collective-permute-start(bf16[4,144,256]{2,1,0:T(8,128)(2,1)} %pad_maximum_fusion.1), channel_id=1, source_target_pairs={{0,3},{1,0},{2,1},{3,2},{4,7},{5,4},{6,5},{7,6},{8,11},{9,8},{10,9... | collective-permute-start | bytes 884744 | tf_op jit(solution)/shard_map/ppermute | solution.py:22
  26.4 9.8 %collective-permute-start.12 = (bf16[4,144,256]{2,1,0:T(8,128)(2,1)}, bf16[4,144,256]{2,1,0:T(8,128)(2,1)}, u32[]{:S(2)}, u32[]{:S(2)}) collective-permute-start(bf16[4,144,256]{2,1,0:T(8,128)(2,1)} %pad_maximum_fusion.2), channel_id=1, source_target_pairs={{0,16},{16,32},{32,48},{48,0},{1,17},{17,33},{33,49},{49,1},{2,18}... | collective-permute-start | bytes 884744 | tf_op jit(solution)/shard_map/ppermute | solution.py:22
  27.7 8.5 %collective-permute-start.13 = (bf16[4,144,256]{2,1,0:T(8,128)(2,1)}, bf16[4,144,256]{2,1,0:T(8,128)(2,1)}, u32[]{:S(2)}, u32[]{:S(2)}) collective-permute-start(bf16[4,144,256]{2,1,0:T(8,128)(2,1)} %pad_maximum_fusion.2), channel_id=1, source_target_pairs={{0,48},{16,0},{32,16},{48,32},{1,49},{17,1},{33,17},{49,33},{2,50}... | collective-permute-start | bytes 884744 | tf_op jit(solution)/shard_map/ppermute | solution.py:22
  32.1 34.1 %all-to-all-start = ((bf16[8,112,512]{2,1,0:T(8,128)(2,1)}), bf16[8,112,512]{2,1,0:T(8,128)(2,1)S(1)}, u32[]{:S(2)}, u32[]{:S(2)}) async-start(bf16[8,112,512]{2,1,0:T(8,128)(2,1)} %pad_maximum_fusion), calls=%async_computation | async-start | bytes 1835008 | tf_op jit(solution)/shard_map/all_to_all | solution.py:324
  38.9 11.1 %collective-permute-start.14 = (bf16[2,144,256]{2,1,0:T(8,128)(2,1)S(1)}, bf16[2,144,256]{2,1,0:T(8,128)(2,1)S(1)}, u32[]{:S(2)}, u32[]{:S(2)}) collective-permute-start(bf16[2,144,256]{2,1,0:T(8,128)(2,1)S(1)} %slice.51), channel_id=1, source_target_pairs={{0,1},{1,2},{2,3},{3,0},{4,5},{5,6},{6,7},{7,4},{8,9},{9,10},{10,1... | collective-permute-start | bytes 442376 | tf_op jit(solution)/shard_map/ppermute | solution.py:22
  40.1 9.9 %collective-permute-start.15 = (bf16[2,144,256]{2,1,0:T(8,128)(2,1)S(1)}, bf16[2,144,256]{2,1,0:T(8,128)(2,1)S(1)}, u32[]{:S(2)}, u32[]{:S(2)}) collective-permute-start(bf16[2,144,256]{2,1,0:T(8,128)(2,1)S(1)} %slice.52), channel_id=1, source_target_pairs={{0,3},{1,0},{2,1},{3,2},{4,7},{5,4},{6,5},{7,6},{8,11},{9,8},{10,9... | collective-permute-start | bytes 442376 | tf_op jit(solution)/shard_map/ppermute | solution.py:22
  43.5 9.3 %collective-permute-start.16 = (bf16[2,144,256]{2,1,0:T(8,128)(2,1)S(1)}, bf16[2,144,256]{2,1,0:T(8,128)(2,1)S(1)}, u32[]{:S(2)}, u32[]{:S(2)}) collective-permute-start(bf16[2,144,256]{2,1,0:T(8,128)(2,1)S(1)} %slice.53), channel_id=1, source_target_pairs={{0,16},{16,32},{32,48},{48,0},{1,17},{17,33},{33,49},{49,1},{2,18}... | collective-permute-start | bytes 442376 | tf_op jit(solution)/shard_map/ppermute | solution.py:22
  45.9 6.8 %collective-permute-start.17 = (bf16[2,144,256]{2,1,0:T(8,128)(2,1)S(1)}, bf16[2,144,256]{2,1,0:T(8,128)(2,1)S(1)}, u32[]{:S(2)}, u32[]{:S(2)}) collective-permute-start(bf16[2,144,256]{2,1,0:T(8,128)(2,1)S(1)} %slice.54), channel_id=1, source_target_pairs={{0,48},{16,0},{32,16},{48,32},{1,49},{17,1},{33,17},{49,33},{2,50}... | collective-permute-start | bytes 442376 | tf_op jit(solution)/shard_map/ppermute | solution.py:22
  48.2 15.2 %copy-start.9 = (f32[16,32]{1,0:T(8,128)S(1)}, f32[16,32]{1,0:T(8,128)}, u32[]{:S(2)}) copy-start(f32[16,32]{1,0:T(8,128)} %param.17) | copy-start | bytes 6148
  48.2 15.2 %copy-start.10 = (f32[16,32]{1,0:T(8,128)S(1)}, f32[16,32]{1,0:T(8,128)}, u32[]{:S(2)}) copy-start(f32[16,32]{1,0:T(8,128)} %param.16) | copy-start | bytes 6148
  50.0 3.4 %copy-start.4 = (bf16[16,144,256]{2,1,0:T(8,128)(2,1)}, bf16[16,144,256]{2,1,0:T(8,128)(2,1)S(1)}, u32[]{:S(2)}) copy-start(bf16[16,144,256]{2,1,0:T(8,128)(2,1)S(1)} %get-tuple-element.86) | copy-start | bytes 3538948
  54.1 28.5 %collective-permute-start.18 = (bf16[16,144,256]{2,1,0:T(8,128)(2,1)}, bf16[16,144,256]{2,1,0:T(8,128)(2,1)S(1)}, u32[]{:S(2)}, u32[]{:S(2)}) collective-permute-start(bf16[16,144,256]{2,1,0:T(8,128)(2,1)} %constant_dynamic-update-slice_fusion.refs_0_), channel_id=1, source_target_pairs={{0,16},{16,32},{32,48},{48,0},{1,17},{17,33},{33,49},{49,1},{2,18}... | collective-permute-start | bytes 3538952 | tf_op jit(solution)/shard_map/ppermute | solution.py:22
  54.1 28.5 %collective-permute-start.19 = (bf16[16,144,256]{2,1,0:T(8,128)(2,1)}, bf16[16,144,256]{2,1,0:T(8,128)(2,1)S(1)}, u32[]{:S(2)}, u32[]{:S(2)}) collective-permute-start(bf16[16,144,256]{2,1,0:T(8,128)(2,1)} %constant_dynamic-update-slice_fusion.refs_0_), channel_id=1, source_target_pairs={{0,48},{16,0},{32,16},{48,32},{1,49},{17,1},{33,17},{49,33},{2,50}... | collective-permute-start | bytes 3538952 | tf_op jit(solution)/shard_map/ppermute | solution.py:22
  58.1 26.7 %collective-permute-start.20 = (bf16[16,144,256]{2,1,0:T(8,128)(2,1)}, bf16[16,144,256]{2,1,0:T(8,128)(2,1)}, u32[]{:S(2)}, u32[]{:S(2)}) collective-permute-start(bf16[16,144,256]{2,1,0:T(8,128)(2,1)} %constant_dynamic-update-slice_fusion.6.refs_2_), channel_id=1, source_target_pairs={{0,1},{1,2},{2,3},{3,0},{4,5},{5,6},{6,7},{7,4},{8,9},{9,10},{10,1... | collective-permute-start | bytes 3538952 | tf_op jit(solution)/shard_map/ppermute | solution.py:22
  58.5 26.3 %collective-permute-start.21 = (bf16[16,144,256]{2,1,0:T(8,128)(2,1)}, bf16[16,144,256]{2,1,0:T(8,128)(2,1)}, u32[]{:S(2)}, u32[]{:S(2)}) collective-permute-start(bf16[16,144,256]{2,1,0:T(8,128)(2,1)} %constant_dynamic-update-slice_fusion.6.refs_2_), channel_id=1, source_target_pairs={{0,3},{1,0},{2,1},{3,2},{4,7},{5,4},{6,5},{7,6},{8,11},{9,8},{10,9... | collective-permute-start | bytes 3538952 | tf_op jit(solution)/shard_map/ppermute | solution.py:22
  66.2 1.2 copy-start.1
  67.4 0.9 copy-start.2
  68.3 0.9 copy-start.3
  77.6 32.8 %all-to-all-start.1 = ((bf16[32,32,512]{2,1,0:T(8,128)(2,1)}), bf16[32,32,512]{2,1,0:T(8,128)(2,1)S(1)}, u32[]{:S(2)}, u32[]{:S(2)}) async-start(bf16[32,32,512]{2,1,0:T(8,128)(2,1)} %bitcast.15), calls=%async_computation.1 | async-start | bytes 2097152 | tf_op jit(solution)/shard_map/all_to_all | solution.py:333
  85.8 24.5 %collective-permute-start.23 = (bf16[8,144,256]{2,1,0:T(8,128)(2,1)}, bf16[8,144,256]{2,1,0:T(8,128)(2,1)}, u32[]{:S(2)}, u32[]{:S(2)}) collective-permute-start(bf16[8,144,256]{2,1,0:T(8,128)(2,1)} %slice.55), channel_id=1, source_target_pairs={{0,16},{16,32},{32,48},{48,0},{1,17},{17,33},{33,49},{49,1},{2,18}... | collective-permute-start | bytes 1769480 | tf_op jit(solution)/shard_map/ppermute | solution.py:22
  86.7 23.6 %collective-permute-start.24 = (bf16[8,144,256]{2,1,0:T(8,128)(2,1)}, bf16[8,144,256]{2,1,0:T(8,128)(2,1)}, u32[]{:S(2)}, u32[]{:S(2)}) collective-permute-start(bf16[8,144,256]{2,1,0:T(8,128)(2,1)} %slice.56), channel_id=1, source_target_pairs={{0,48},{16,0},{32,16},{48,32},{1,49},{17,1},{33,17},{49,33},{2,50}... | collective-permute-start | bytes 1769480 | tf_op jit(solution)/shard_map/ppermute | solution.py:22
  91.3 19.0 %collective-permute-start.25 = (bf16[8,144,256]{2,1,0:T(8,128)(2,1)}, bf16[8,144,256]{2,1,0:T(8,128)(2,1)}, u32[]{:S(2)}, u32[]{:S(2)}) collective-permute-start(bf16[8,144,256]{2,1,0:T(8,128)(2,1)} %slice.57), channel_id=1, source_target_pairs={{0,1},{1,2},{2,3},{3,0},{4,5},{5,6},{6,7},{7,4},{8,9},{9,10},{10,1... | collective-permute-start | bytes 1769480 | tf_op jit(solution)/shard_map/ppermute | solution.py:22
  94.4 15.9 %collective-permute-start.26 = (bf16[8,144,256]{2,1,0:T(8,128)(2,1)}, bf16[8,144,256]{2,1,0:T(8,128)(2,1)}, u32[]{:S(2)}, u32[]{:S(2)}) collective-permute-start(bf16[8,144,256]{2,1,0:T(8,128)(2,1)} %slice.58), channel_id=1, source_target_pairs={{0,3},{1,0},{2,1},{3,2},{4,7},{5,4},{6,5},{7,6},{8,11},{9,8},{10,9... | collective-permute-start | bytes 1769480 | tf_op jit(solution)/shard_map/ppermute | solution.py:22
  110.3 1.3 copy-start.5
  117.5 6.9 %collective-permute-start.27 = (bf16[5,512,256]{2,1,0:T(8,128)(2,1)S(1)}, bf16[5,512,256]{2,1,0:T(8,128)(2,1)S(1)}, u32[]{:S(2)}, u32[]{:S(2)}) collective-permute-start(bf16[5,512,256]{2,1,0:T(8,128)(2,1)S(1)} %get-tuple-element.53), channel_id=1, source_target_pairs={{0,8},{8,0},{1,9},{9,1},{2,10},{10,2},{3,11},{11,3},{4,12},{12,4},... | collective-permute-start | bytes 3932168 | tf_op jit(solution)/shard_map/ppermute | solution.py:26
  124.4 2.4 %collective-permute-start.22 = (bf16[3,512,256]{2,1,0:T(8,128)(2,1)S(1)}, bf16[3,512,256]{2,1,0:T(8,128)(2,1)S(1)}, u32[]{:S(2)}, u32[]{:S(2)}) collective-permute-start(bf16[3,512,256]{2,1,0:T(8,128)(2,1)S(1)} %get-tuple-element.44), channel_id=1, source_target_pairs={{0,8},{8,0},{1,9},{9,1},{2,10},{10,2},{3,11},{11,3},{4,12},{12,4},... | collective-permute-start | bytes 2359304 | tf_op jit(solution)/shard_map/ppermute | solution.py:26
  125.3 24.3 %collective-permute-start.29 = (bf16[5,512,128]{2,1,0:T(8,128)(2,1)S(1)}, bf16[5,512,128]{2,1,0:T(8,128)(2,1)S(1)}, u32[]{:S(2)}, u32[]{:S(2)}) collective-permute-start(bf16[5,512,128]{2,1,0:T(8,128)(2,1)S(1)} %get-tuple-element.56), channel_id=1, source_target_pairs={{0,4},{4,0},{1,5},{5,1},{2,6},{6,2},{3,7},{7,3},{8,12},{12,8},{9,1... | collective-permute-start | bytes 1966088 | tf_op jit(solution)/shard_map/ppermute | solution.py:26
  127.5 22.2 %collective-permute-start.28 = (bf16[3,512,128]{2,1,0:T(8,128)(2,1)S(1)}, bf16[3,512,128]{2,1,0:T(8,128)(2,1)S(1)}, u32[]{:S(2)}, u32[]{:S(2)}) collective-permute-start(bf16[3,512,128]{2,1,0:T(8,128)(2,1)S(1)} %get-tuple-element.55), channel_id=1, source_target_pairs={{0,4},{4,0},{1,5},{5,1},{2,6},{6,2},{3,7},{7,3},{8,12},{12,8},{9,1... | collective-permute-start | bytes 1179656 | tf_op jit(solution)/shard_map/ppermute | solution.py:26
